TPU v7x, 1024 devices: a whole 4x8x16 slice. The times are simulated.
1024 devices in a mesh: dp: 32 (over x_lo, y, core), expert: 32 (over x_hi, z).
Axes of the slice: x: 4 (x_hi: 2, x_lo: 2; x = x_hi * 2 + x_lo), y: 8, z: 16, core: 2. Of those that a mesh axis runs over, the one named last changes fastest.
Arguments:
- tokens: bfloat16 [2048, 4096], P('expert', 'dp'), may hold values from -6 to 6
- grad_out: bfloat16 [2048, 4096], P('expert', 'dp'), may hold values from -6 to 6
- routes: int32 [2048, 8], P('expert'), may hold values from 0 to 31, all different within a row; in each aligned block of 64 rows (0 to 63, 64 to 127, ...) at most 24 rows name the same one
- gate_probs: float32 [2048, 8], P('expert'), may hold values from 0.03 to 0.6
- w_gate: bfloat16 [32, 4096, 768], P('expert', 'dp'), may hold values from -0.09375 to 0.09375
- w_up: bfloat16 [32, 4096, 768], P('expert', 'dp'), may hold values from -0.09375 to 0.09375
- w_down: bfloat16 [32, 768, 4096], P('expert', None, 'dp'), may hold values from -0.21875 to 0.21875
- dest: int32 [32], P('expert'), may hold values from 0 to 31, as said below
- next_master: float32 [32, 384, 2048], P('expert', 'dp'), may hold values from -3 to 3
- next_first: float32 [32, 384, 2048], P('expert', 'dp'), may hold values from -3 to 3
- next_second: float32 [32, 384, 2048], P('expert', 'dp'), may hold values from 0.01 to 1
Outputs:
- mixed: bfloat16 [2048, 4096], P('expert', 'dp')
- token_grad: bfloat16 [2048, 4096], P('expert', 'dp')
- grad_gate: bfloat16 [32, 4096, 768], P('expert', 'dp')
- grad_up: bfloat16 [32, 4096, 768], P('expert', 'dp')
- grad_down: bfloat16 [32, 768, 4096], P('expert', None, 'dp')
- moved_master: float32 [32, 384, 2048], P('expert', 'dp')
- moved_first: float32 [32, 384, 2048], P('expert', 'dp')
- moved_second: float32 [32, 384, 2048], P('expert', 'dp')
Inputs may be any that keep to these rules, and one draw needn't show every extreme that they name: `routes`: among the 64 tokens of one group, no expert is named more than 24 times, a bound that some block reaches. `dest`: each entry is its own index or its index plus 32//2 modulo 32, and an entry and its partner's entry name each other.
All inputs are finite; a program needn't handle non-finite values.
Results may differ from a plain program's by a relative error of at most 0.0064.
Values may be sent and summed in bfloat16 or wider, within the bound.
No kernel may reach another device: no remote copies, remote signals or barrier semaphores. Data moves between devices by JAX's collectives and lax.ppermute only.
A program may use at most 64 MiB of HBM per device.

v0:
```python
import jax
import jax.numpy as jnp
from jax import lax
from jax.sharding import PartitionSpec as P


def partner_2(value, axis, bit):
    mask = 2**bit
    pairs = [(source, source ^ mask) for source in range(lax.axis_size(axis))]
    return lax.ppermute(value, axis, pairs)


def slot_table(route_rows, expert_count, capacity):
    flat_ids = route_rows.reshape(-1)
    onehot = (flat_ids[:, None] == jnp.arange(expert_count, dtype=jnp.int32)[None, :]).astype(
        jnp.int32
    )
    earlier = jnp.cumsum(onehot, axis=0) - onehot
    position = jnp.sum(earlier * onehot, axis=1)
    slot_ids = flat_ids * capacity + position
    return (
        slot_ids[:, None] == jnp.arange(expert_count * capacity, dtype=jnp.int32)[None, :]
    ).astype(jnp.bfloat16)


def relocate(dest, next_master, next_first, next_second):
    top_bit = lax.axis_size("expert").bit_length() - 2
    partner = partner_2((next_master, next_first, next_second), "expert", top_bit)
    moving = dest[0] != lax.axis_index("expert")
    return (
        jnp.where(moving, partner[0], next_master),
        jnp.where(moving, partner[1], next_first),
        jnp.where(moving, partner[2], next_second),
    )


def shards(
    tokens,
    grad_out,
    routes,
    gate_probs,
    w_gate,
    w_up,
    w_down,
    dest,
    next_master,
    next_first,
    next_second,
):
    moved = relocate(dest, next_master, next_first, next_second)
    tok_count, width_block = tokens.shape
    choose_count = routes.shape[1]
    local_experts = w_gate.shape[0]
    groups = lax.axis_size("expert")
    expert_count = local_experts * groups
    capacity = max(2, min(tok_count, 3 * tok_count * choose_count // (2 * expert_count)))
    table = slot_table(routes, expert_count, capacity)
    probs_flat = gate_probs.reshape(-1)
    x_assign = jnp.repeat(tokens, choose_count, axis=0)
    dy_assign = (
        probs_flat[:, None] * jnp.repeat(grad_out, choose_count, axis=0).astype(jnp.float32)
    ).astype(jnp.bfloat16)
    contract = (((0,), (0,)), ((), ()))
    x_slots = lax.dot_general(table, x_assign, contract, preferred_element_type=jnp.float32).astype(
        jnp.bfloat16
    )
    dy_slots = lax.dot_general(
        table, dy_assign, contract, preferred_element_type=jnp.float32
    ).astype(jnp.bfloat16)
    x_slots = x_slots.reshape(expert_count, capacity, width_block)
    dy_slots = dy_slots.reshape(expert_count, capacity, width_block)
    recv_x, recv_dy = (
        lax.all_to_all(x_slots, "expert", split_axis=0, concat_axis=1, tiled=True),
        lax.all_to_all(dy_slots, "expert", split_axis=0, concat_axis=1, tiled=True),
    )
    gate_part = jnp.einsum("emd,edf->mef", recv_x, w_gate, preferred_element_type=jnp.float32)
    up_part = jnp.einsum("emd,edf->mef", recv_x, w_up, preferred_element_type=jnp.float32)
    back_part = jnp.einsum("emd,efd->mef", recv_dy, w_down, preferred_element_type=jnp.float32)
    share = lax.psum_scatter(
        jnp.stack([gate_part, up_part, back_part], axis=2), "dp", scatter_dimension=0, tiled=True
    )
    gate = share[:, :, 0]
    up_val = share[:, :, 1]
    back = share[:, :, 2]
    sigma_val = jax.nn.sigmoid(gate)
    act = gate * sigma_val * up_val
    grad_g = back * up_val * sigma_val * (1.0 + gate * (1.0 - sigma_val))
    grad_u = back * gate * sigma_val
    whole = lax.all_gather(
        jnp.stack([act, grad_g, grad_u], axis=2).astype(jnp.bfloat16), "dp", axis=0, tiled=True
    )
    act = whole[:, :, 0]
    grad_g = whole[:, :, 1]
    grad_u = whole[:, :, 2]
    slot_y = jnp.einsum("mef,efd->emd", act, w_down, preferred_element_type=jnp.float32).astype(
        jnp.bfloat16
    )
    slot_dx = (
        jnp.einsum("mef,edf->emd", grad_g, w_gate, preferred_element_type=jnp.float32)
        + jnp.einsum("mef,edf->emd", grad_u, w_up, preferred_element_type=jnp.float32)
    ).astype(jnp.bfloat16)
    grad_gate = jnp.einsum(
        "emd,mef->edf", recv_x, grad_g, preferred_element_type=jnp.float32
    ).astype(jnp.bfloat16)
    grad_up = jnp.einsum("emd,mef->edf", recv_x, grad_u, preferred_element_type=jnp.float32).astype(
        jnp.bfloat16
    )
    grad_down = jnp.einsum("mef,emd->efd", act, recv_dy, preferred_element_type=jnp.float32).astype(
        jnp.bfloat16
    )
    back_y, back_dx = (
        lax.all_to_all(slot_y, "expert", split_axis=1, concat_axis=0, tiled=True),
        lax.all_to_all(slot_dx, "expert", split_axis=1, concat_axis=0, tiled=True),
    )
    y_flat = back_y.reshape(expert_count * capacity, width_block)
    dx_flat = back_dx.reshape(expert_count * capacity, width_block)
    y_assign = jnp.dot(table, y_flat, preferred_element_type=jnp.float32)
    dx_assign = jnp.dot(table, dx_flat, preferred_element_type=jnp.float32)
    mixed = jnp.sum(
        (probs_flat[:, None] * y_assign).reshape(tok_count, choose_count, width_block), axis=1
    ).astype(jnp.bfloat16)
    token_grad = jnp.sum(dx_assign.reshape(tok_count, choose_count, width_block), axis=1).astype(
        jnp.bfloat16
    )
    return (mixed, token_grad, grad_gate, grad_up, grad_down, moved[0], moved[1], moved[2])


def solution(mesh):
    placed = (
        P("expert", "dp"),
        P("expert", "dp"),
        P("expert", None),
        P("expert", None),
        P("expert", "dp", None),
        P("expert", "dp", None),
        P("expert", None, "dp"),
        P("expert"),
        P("expert", "dp", None),
        P("expert", "dp", None),
        P("expert", "dp", None),
    )
    return jax.shard_map(
        shards,
        mesh=mesh,
        in_specs=placed,
        out_specs=(
            P("expert", "dp"),
            P("expert", "dp"),
            P("expert", "dp", None),
            P("expert", "dp", None),
            P("expert", None, "dp"),
            P("expert", "dp", None),
            P("expert", "dp", None),
            P("expert", "dp", None),
        ),
        check_vma=False,
    )
```

profile of v0, /device:TPU:1, one launch (start us, length us, event | category | flops | bytes accessed | tf_op | source)
XLA Modules:
  0.0 351.8 jit_solution(16833651821252551446)
XLA Ops:
  7.2 0.0 copy-start
  7.2 0.0 copy-start.3
  7.2 0.8 copy.43
  8.0 0.1 eq.61
  8.1 0.1 reshape.237
  8.2 1.2 reduce-window.6
  9.4 0.2 slice_reduce_fusion
  9.7 0.1 fusion.42
  9.8 2.1 fusion.7
  11.9 22.3 %all-to-all-start = ((bf16[32,24,128]{2,1,0:T(8,128)(2,1)}), bf16[32,24,128]{2,1,0:T(8,128)(2,1)S(1)}, u32[]{:S(2)}, u32[]{:S(2)}) async-start(bf16[32,24,128]{2,1,0:T(8,128)(2,1)} %bitcast.2), calls=%async_computation | async-start | bytes 393216 | tf_op jit(solution)/shard_map/all_to_all | solution.py:73
  34.2 0.8 copy.42
  34.9 0.1 mul.82
  35.0 0.7 convert_element_type.72
  35.7 1.4 fusion.8
  37.2 15.6 %all-to-all-done = bf16[32,24,128]{2,1,0:T(8,128)(2,1)S(1)} async-done(((bf16[32,24,128]{2,1,0:T(8,128)(2,1)}), bf16[32,24,128]{2,1,0:T(8,128)(2,1)S(1)}, u32[]{:S(2)}, u32[]{:S(2)}) %all-to-all-start) | async-done | bytes 196640 | tf_op jit(solution)/shard_map/all_to_all | solution.py:73
  52.8 5.0 %all-to-all-start.1 = ((bf16[32,24,128]{2,1,0:T(8,128)(2,1)}), bf16[32,24,128]{2,1,0:T(8,128)(2,1)S(1)}, u32[]{:S(2)}, u32[]{:S(2)}) async-start(bf16[32,24,128]{2,1,0:T(8,128)(2,1)} %bitcast.15), calls=%async_computation.1 | async-start | bytes 393216 | tf_op jit(solution)/shard_map/all_to_all | solution.py:74
  57.8 0.0 reduce-scatter.2.cloned.1.call-start
  57.9 0.4 convolution_bitcast_fusion.1
  58.3 1.9 convolution_bitcast_fusion.2
  60.2 15.5 %all-to-all-done.1 = bf16[32,24,128]{2,1,0:T(8,128)(2,1)S(1)} async-done(((bf16[32,24,128]{2,1,0:T(8,128)(2,1)}), bf16[32,24,128]{2,1,0:T(8,128)(2,1)S(1)}, u32[]{:S(2)}, u32[]{:S(2)}) %all-to-all-start.1) | async-done | bytes 196640 | tf_op jit(solution)/shard_map/all_to_all | solution.py:74
  75.7 0.0 copy-done
  75.7 0.5 convolution_bitcast_fusion
  76.2 1.2 copy-done.1
  77.4 3.4 pad_maximum_fusion
  80.8 0.0 reduce-scatter.2.cloned.1.call-update
  80.8 0.0 all-gather.2.cloned.1.call-start
  80.8 126.0 %reduce-scatter.2.cloned.1.call-done = f32[24,1,3,768]{3,0,2,1:T(8,128)} async-done(((f32[768,1,3,768]{3,0,2,1:T(8,128)}), f32[24,1,3,768]{3,0,2,1:T(8,128)}) %reduce-scatter.2.cloned.1.call-update) | async-done | bytes 221200 | tf_op jit(solution)/shard_map/reduce_scatter | solution.py:79
  206.8 1.0 multiply_convert_fusion.2
  207.9 0.7 pad_maximum_fusion.1
  208.5 0.0 all-gather.2.cloned.1.call-update
  208.6 1.9 collective-permute-start.2
  210.5 4.9 %collective-permute-start.1 = (f32[1,12,2048]{2,0,1:T(1,128)S(1)}, f32[1,12,2048]{2,0,1:T(1,128)S(1)}, u32[]{:S(2)}, u32[]{:S(2)}) collective-permute-start(f32[1,12,2048]{2,0,1:T(1,128)S(1)} %copy-done.5), channel_id=1, source_target_pairs={{0,16},{1,17},{2,18},{3,19},{4,20},{5,21},{6,22},{7,23},{8,24},{9,... | collective-permute-start | bytes 294920 | tf_op jit(solution)/shard_map/ppermute | solution.py:10
  215.4 1.9 collective-permute-start
  217.3 0.1 reduce_sum.31
  217.4 0.1 copy.47
  217.5 0.1 copy.48
  218.2 0.0 collective-permute-done.2
  218.3 0.7 broadcast_select_fusion
  219.0 62.8 %all-gather.2.cloned.1.call-done = bf16[768,1,3,768]{3,0,2,1:T(8,128)(2,1)} async-done(((bf16[24,1,3,768]{3,0,2,1:T(8,128)(2,1)}), bf16[768,1,3,768]{3,0,2,1:T(8,128)(2,1)}) %all-gather.2.cloned.1.call-update) | async-done | bytes 3538960 | tf_op jit(solution)/shard_map/all_gather | solution.py:89
  281.8 1.7 fusion.11
  283.5 0.3 copy.65
  283.8 0.5 broadcast.72
  284.3 1.8 reduce.2
  286.1 0.7 reshape.256
  286.9 15.2 %all-to-all-start.2 = ((bf16[32,2,1536]{2,1,0:T(2,128)(2,1)}), bf16[32,2,1536]{2,1,0:T(2,128)(2,1)S(1)}, u32[]{:S(2)}, u32[]{:S(2)}) async-start(bf16[32,2,1536]{2,1,0:T(2,128)(2,1)} %reshape.256), calls=%async_computation.3 | async-start | bytes 393216 | tf_op jit(solution)/shard_map/all_to_all | solution.py:112
  302.1 0.0 collective-permute-done.1
  302.1 0.7 broadcast_select_fusion.1
  302.8 1.7 fusion.20
  304.6 1.7 fusion.15
  306.3 0.3 copy.64
  306.6 1.8 reduce.3
  308.4 0.7 reshape.258
  309.2 12.3 %all-to-all-done.2 = bf16[32,2,1536]{2,1,0:T(2,128)(2,1)S(1)} async-done(((bf16[32,2,1536]{2,1,0:T(2,128)(2,1)}), bf16[32,2,1536]{2,1,0:T(2,128)(2,1)S(1)}, u32[]{:S(2)}, u32[]{:S(2)}) %all-to-all-start.2) | async-done | bytes 196640 | tf_op jit(solution)/shard_map/all_to_all | solution.py:112
  321.5 4.3 %all-to-all-start.3 = ((bf16[32,2,1536]{2,1,0:T(2,128)(2,1)}), bf16[32,2,1536]{2,1,0:T(2,128)(2,1)S(1)}, u32[]{:S(2)}, u32[]{:S(2)}) async-start(bf16[32,2,1536]{2,1,0:T(2,128)(2,1)} %reshape.258), calls=%async_computation.4 | async-start | bytes 393216 | tf_op jit(solution)/shard_map/all_to_all | solution.py:113
  325.8 0.0 collective-permute-done
  325.8 0.7 broadcast_select_fusion.2
  326.6 2.3 fusion.12
  328.9 2.3 fusion.13
  331.2 2.5 fusion.14
  333.7 0.1 reshape.257
  333.8 1.1 fusion.16
  334.9 8.9 %all-to-all-done.3 = bf16[32,2,1536]{2,1,0:T(2,128)(2,1)S(1)} async-done(((bf16[32,2,1536]{2,1,0:T(2,128)(2,1)}), bf16[32,2,1536]{2,1,0:T(2,128)(2,1)S(1)}, u32[]{:S(2)}, u32[]{:S(2)}) %all-to-all-start.3) | async-done | bytes 196640 | tf_op jit(solution)/shard_map/all_to_all | solution.py:113
  343.7 0.1 reshape.259
  343.9 1.1 fusion.17
  (17 shorter events, 0.1 us)
Async XLA Ops:
  7.2 68.6 %copy-start = (bf16[1,768,128]{2,1,0:T(8,128)(2,1)S(1)}, bf16[1,768,128]{2,1,0:T(8,128)(2,1)}, u32[]{:S(2)}) copy-start(bf16[1,768,128]{2,1,0:T(8,128)(2,1)} %param.17) | copy-start | bytes 589828
  7.2 50.7 %copy-start.3 = (bf16[1,128,768]{2,1,0:T(8,128)(2,1)S(1)}, bf16[1,128,768]{2,1,0:T(8,128)(2,1)}, u32[]{:S(2)}) copy-start(bf16[1,128,768]{2,1,0:T(8,128)(2,1)} %param.16) | copy-start | bytes 589828
  11.9 46.5 %copy-start.2 = (bf16[1,128,768]{2,1,0:T(8,128)(2,1)S(1)}, bf16[1,128,768]{2,1,0:T(8,128)(2,1)}, u32[]{:S(2)}) copy-start(bf16[1,128,768]{2,1,0:T(8,128)(2,1)} %param.15) | copy-start | bytes 589828
  11.9 40.9 %all-to-all-start = ((bf16[32,24,128]{2,1,0:T(8,128)(2,1)}), bf16[32,24,128]{2,1,0:T(8,128)(2,1)S(1)}, u32[]{:S(2)}, u32[]{:S(2)}) async-start(bf16[32,24,128]{2,1,0:T(8,128)(2,1)} %bitcast.2), calls=%async_computation | async-start | bytes 393216 | tf_op jit(solution)/shard_map/all_to_all | solution.py:73
  52.8 22.9 %all-to-all-start.1 = ((bf16[32,24,128]{2,1,0:T(8,128)(2,1)}), bf16[32,24,128]{2,1,0:T(8,128)(2,1)S(1)}, u32[]{:S(2)}, u32[]{:S(2)}) async-start(bf16[32,24,128]{2,1,0:T(8,128)(2,1)} %bitcast.15), calls=%async_computation.1 | async-start | bytes 393216 | tf_op jit(solution)/shard_map/all_to_all | solution.py:74
  57.8 149.0 %reduce-scatter.2.cloned.1.call-start = ((), (), s32[]{:S(2)}) async-start(), calls=%async_computation.5 | async-start | bytes 7299072 | tf_op jit(solution)/shard_map/reduce_scatter | solution.py:79
  75.7 1.7 copy-start.1
  80.8 127.8 %copy-start.4 = (f32[1,12,2048]{2,0,1:T(1,128)S(1)}, f32[1,12,2048]{2,0,1:T(1,128)}, u32[]{:S(2)}) copy-start(f32[1,12,2048]{2,0,1:T(1,128)} %param.21) | copy-start | bytes 294916
  80.8 129.7 %copy-start.5 = (f32[1,12,2048]{2,0,1:T(1,128)S(1)}, f32[1,12,2048]{2,0,1:T(1,128)}, u32[]{:S(2)}) copy-start(f32[1,12,2048]{2,0,1:T(1,128)} %param.20) | copy-start | bytes 294916
  80.8 134.6 %copy-start.6 = (f32[1,12,2048]{2,0,1:T(1,128)S(1)}, f32[1,12,2048]{2,0,1:T(1,128)}, u32[]{:S(2)}) copy-start(f32[1,12,2048]{2,0,1:T(1,128)} %param.19) | copy-start | bytes 294916
  80.8 136.7 %copy-start.7 = (s32[64,8]{0,1:T(8,128)S(1)}, s32[64,8]{0,1:T(8,128)}, u32[]{:S(2)}) copy-start(s32[64,8]{0,1:T(8,128)} %param.13) | copy-start | bytes 6148
  80.8 201.0 %all-gather.2.cloned.1.call-start = ((), (), s32[]{:S(2)}) async-start(), calls=%async_computation.6 | async-start | bytes 3649536 | tf_op jit(solution)/shard_map/all_gather | solution.py:89
  208.6 9.7 %collective-permute-start.2 = (f32[1,12,2048]{2,0,1:T(1,128)S(1)}, f32[1,12,2048]{2,0,1:T(1,128)S(1)}, u32[]{:S(2)}, u32[]{:S(2)}) collective-permute-start(f32[1,12,2048]{2,0,1:T(1,128)S(1)} %copy-done.4), channel_id=1, source_target_pairs={{0,16},{1,17},{2,18},{3,19},{4,20},{5,21},{6,22},{7,23},{8,24},{9,... | collective-permute-start | bytes 294920 | tf_op jit(solution)/shard_map/ppermute | solution.py:10
  210.5 91.6 %collective-permute-start.1 = (f32[1,12,2048]{2,0,1:T(1,128)S(1)}, f32[1,12,2048]{2,0,1:T(1,128)S(1)}, u32[]{:S(2)}, u32[]{:S(2)}) collective-permute-start(f32[1,12,2048]{2,0,1:T(1,128)S(1)} %copy-done.5), channel_id=1, source_target_pairs={{0,16},{1,17},{2,18},{3,19},{4,20},{5,21},{6,22},{7,23},{8,24},{9,... | collective-permute-start | bytes 294920 | tf_op jit(solution)/shard_map/ppermute | solution.py:10
  215.4 110.5 %collective-permute-start = (f32[1,12,2048]{2,0,1:T(1,128)S(1)}, f32[1,12,2048]{2,0,1:T(1,128)S(1)}, u32[]{:S(2)}, u32[]{:S(2)}) collective-permute-start(f32[1,12,2048]{2,0,1:T(1,128)S(1)} %copy-done.6), channel_id=1, source_target_pairs={{0,16},{1,17},{2,18},{3,19},{4,20},{5,21},{6,22},{7,23},{8,24},{9,... | collective-permute-start | bytes 294920 | tf_op jit(solution)/shard_map/ppermute | solution.py:10
  286.9 34.6 %all-to-all-start.2 = ((bf16[32,2,1536]{2,1,0:T(2,128)(2,1)}), bf16[32,2,1536]{2,1,0:T(2,128)(2,1)S(1)}, u32[]{:S(2)}, u32[]{:S(2)}) async-start(bf16[32,2,1536]{2,1,0:T(2,128)(2,1)} %reshape.256), calls=%async_computation.3 | async-start | bytes 393216 | tf_op jit(solution)/shard_map/all_to_all | solution.py:112
  321.5 22.2 %all-to-all-start.3 = ((bf16[32,2,1536]{2,1,0:T(2,128)(2,1)}), bf16[32,2,1536]{2,1,0:T(2,128)(2,1)S(1)}, u32[]{:S(2)}, u32[]{:S(2)}) async-start(bf16[32,2,1536]{2,1,0:T(2,128)(2,1)} %reshape.258), calls=%async_computation.4 | async-start | bytes 393216 | tf_op jit(solution)/shard_map/all_to_all | solution.py:113
Sparse Core Ops, SparseCore 0:
  80.9 125.8 reduce-scatter.1
  210.1 71.6 all-gather.1
where the time goes:
time: 355 us; the launch traced here: 352 us
  waiting for transfers between devices  241 us (68%)
  starting transfers between devices  55.7 us (16%)
  matrix products  20.7 us (6%)
  between operations  15 us (4%)
  other arithmetic  12.9 us (4%)
  local copies, waits for them, and re-layouts  6.44 us (2%)
    reduce_scatter x1, waiting for transfers between devices, shards(): lax.psum_scatter(jnp.stack([gate_part, up_part, back_part], axis=2), 'dp'...  126 us
    all_gather x1, waiting for transfers between devices, shards(): lax.all_gather(jnp.stack([act, grad_g, grad_u], axis=2).astype(jnp.bfloat...  62.8 us
    all_to_all x1, starting transfers between devices, shards(): lax.all_to_all(x_slots, 'expert', split_axis=0, concat_axis=1, tiled=True)  22.3 us
    all_to_all x1, waiting for transfers between devices, shards(): lax.all_to_all(x_slots, 'expert', split_axis=0, concat_axis=1, tiled=True)  15.6 us
    all_to_all x1, waiting for transfers between devices, shards(): lax.all_to_all(dy_slots, 'expert', split_axis=0, concat_axis=1, tiled=True)  15.5 us
    all_to_all x1, starting transfers between devices, shards(): lax.all_to_all(slot_y, 'expert', split_axis=1, concat_axis=0, tiled=True)  15.2 us
    all_to_all x1, waiting for transfers between devices, shards(): lax.all_to_all(slot_y, 'expert', split_axis=1, concat_axis=0, tiled=True)  12.3 us
    all_to_all x1, waiting for transfers between devices, shards(): lax.all_to_all(slot_dx, 'expert', split_axis=1, concat_axis=0, tiled=True)  8.87 us
  transfers between devices with their start and end apart: 9, of which 6 were waited for; matrix products, arithmetic and copies ran while one was open for 8% of the time, Pallas kernels for 0%

commit v1 on v0

v1 whole, which is shorter than its diff:
```python
import functools

import jax
import jax.numpy as jnp
from jax import lax
from jax.experimental import pallas as pl
from jax.experimental.pallas import tpu as pltpu
from jax.sharding import Mesh
from jax.sharding import PartitionSpec as P

EXPERT = ("x_hi", "z")
DP = ("x_lo", "y", "core")
QUAD = ("x_lo", "core")
F32 = jnp.float32
BF16 = jnp.bfloat16
SWAP = [(0, 1), (1, 0)]

TOK = 64
TOP = 8
GROUPS = 32
PART = 6
QUADS = 4
ROWS = GROUPS * PART
WIDE = GROUPS * PART * QUADS
BLK = 128
FF = 768
Y = 8

PARAMS = pltpu.CompilerParams(vmem_limit_bytes=48 * 1024 * 1024)


def call(kernel, out_shape, operands, flops=0, moved=0):
    vmem = pl.BlockSpec(memory_space=pltpu.VMEM)
    smem = pl.BlockSpec(memory_space=pltpu.SMEM)
    return pl.pallas_call(
        kernel,
        out_shape=out_shape,
        in_specs=[smem if o.dtype == jnp.int32 and o.size == 1 else vmem for o in operands],
        out_specs=jax.tree.map(lambda _: vmem, out_shape),
        compiler_params=PARAMS,
        cost_estimate=pl.CostEstimate(flops=flops, bytes_accessed=moved, transcendentals=0),
    )(*operands)


def row_fields(shape, dim):
    r = lax.broadcasted_iota(jnp.int32, shape, dim)
    pair = (r * 2731) >> 16
    rest = r - pair * (QUADS * PART)
    member = (rest * 43) >> 8
    return pair, member, rest - member * PART


def three(value):
    hi = value.astype(BF16)
    left = value - hi.astype(F32)
    mid = left.astype(BF16)
    return hi, mid, (left - mid.astype(F32)).astype(BF16)


def dot(a, b, dims):
    return lax.dot_general(a, b, (dims, ((), ())), preferred_element_type=F32)


def dispatch_kernel(q_ref, routes_ref, probs_ref, near_ref, far_ref, pay_ref, mask_ref, prob_ref):
    q = q_ref[0]
    shape = (TOK, WIDE)
    pair, member, slot = row_fields(shape, 1)
    chosen = jnp.zeros(shape, F32)
    weight = jnp.zeros(shape, F32)
    for k in range(TOP):
        hit = routes_ref[:, k : k + 1] == pair
        chosen = jnp.where(hit, 1.0, chosen)
        weight = jnp.where(hit, probs_ref[:, k : k + 1], weight)
    row = lax.broadcasted_iota(jnp.int32, (TOK, TOK), 0)
    col = lax.broadcasted_iota(jnp.int32, (TOK, TOK), 1)
    before = jnp.where(col < row, 1.0, 0.0).astype(BF16)
    position = dot(before, chosen.astype(BF16), ((1,), (0,)))
    here = (chosen > 0.5) & (position == (q * PART + slot).astype(F32))
    mask = jnp.where(here, 1.0, 0.0)
    prob = jnp.where(here, weight, 0.0)
    mask_ref[...] = mask.astype(BF16)
    prob_ref[...] = prob
    masks = [jnp.where(member == d, mask, 0.0).astype(BF16) for d in range(QUADS)]
    parts = three(prob)
    x = jnp.zeros((WIDE, BLK), F32)
    dy = jnp.zeros((WIDE, BLK), F32)
    zero = jnp.zeros(shape, BF16)
    for d in range(QUADS):
        source = near_ref if d < 2 else far_ref
        lo = (d % 2) * TOK
        x_tok = source[lo : lo + TOK, :BLK]
        dy_tok = source[lo : lo + TOK, BLK:]
        x = x + dot(masks[d], x_tok, ((0,), (0,)))
        for part in parts:
            dy = dy + dot(jnp.where(member == d, part, zero), dy_tok, ((0,), (0,)))
    pay_ref[:, :BLK] = x.astype(BF16)
    pay_ref[:, BLK:] = dy.astype(BF16)


def place(d):
    i = lax.broadcasted_iota(jnp.int32, (ROWS, WIDE), 0)
    r = lax.broadcasted_iota(jnp.int32, (ROWS, WIDE), 1)
    group = (i * 10923) >> 16
    want = group * (QUADS * PART) + d * PART + (i - group * PART)
    return jnp.where(r == want, 1.0, 0.0).astype(BF16)


def partial_kernel(pay_ref, w0, w1, w2, w3, sums_ref, x_ref, dy_ref):
    got = pay_ref[...]
    for d in range(QUADS):
        moved = dot(place(d), got, ((1,), (0,))).astype(BF16)
        x_ref[:, d * BLK : (d + 1) * BLK] = moved[:, :BLK]
        dy_ref[:, d * BLK : (d + 1) * BLK] = moved[:, BLK:]
    for k in range(3):
        rows_ref = dy_ref if k == 2 else x_ref
        total = jnp.zeros((ROWS, FF), F32)
        for d, w in enumerate((w0, w1, w2, w3)):
            total = total + dot(rows_ref[:, d * BLK : (d + 1) * BLK], w[k], ((1,), (0,)))
        sums_ref[:, k * FF : (k + 1) * FF] = total.astype(BF16)


def act_kernel(in_ref, out_ref):
    rows = ROWS // Y
    for lo in range(0, FF, 256):
        vals = []
        for k in range(3):
            block = in_ref[:, k * FF + lo : k * FF + lo + 256].astype(F32)
            total = block[:rows]
            for y in range(1, Y):
                total = total + block[y * rows : (y + 1) * rows]
            vals.append(total)
        gate, up, back = vals
        s = jax.nn.sigmoid(gate)
        out_ref[:, lo : lo + 256] = (gate * s * up).astype(BF16)
        out_ref[:, FF + lo : FF + lo + 256] = (
            back * up * s * (1.0 + gate * (1.0 - s))
        ).astype(BF16)
        out_ref[:, 2 * FF + lo : 2 * FF + lo + 256] = (back * gate * s).astype(BF16)


def back_kernel(h_ref, w0, w1, w2, w3, pay_ref):
    act = h_ref[:, :FF]
    grad_g = h_ref[:, FF : 2 * FF]
    grad_u = h_ref[:, 2 * FF :]
    total = jnp.zeros((WIDE, 2 * BLK), F32)
    for d, w in enumerate((w0, w1, w2, w3)):
        y = dot(act, w[2], ((1,), (1,)))
        dx = dot(grad_g, w[0], ((1,), (1,))) + dot(grad_u, w[1], ((1,), (1,)))
        both = jnp.concatenate([y.astype(BF16), dx.astype(BF16)], axis=1)
        total = total + dot(place(d), both, ((0,), (0,)))
    pay_ref[...] = total.astype(BF16)


def grad_kernel(h_ref, x_ref, dy_ref, keep_ref, send_ref):
    for d in range(QUADS):
        for k in range(3):
            rows_ref = dy_ref if k == 2 else x_ref
            h_at = (FF, 2 * FF, 0)[k]
            part = dot(
                rows_ref[:, d * BLK : (d + 1) * BLK], h_ref[:, h_at : h_at + FF], ((0,), (0,))
            )
            if d % 2:
                send_ref[d // 2, k] = part.astype(BF16)
            else:
                keep_ref[d // 2, k] = part


def combine_kernel(q_ref, pay_ref, mask_ref, prob_ref, out_ref):
    q = q_ref[0]
    shape = (TOK, WIDE)
    _, member, _ = row_fields(shape, 1)
    y = pay_ref[:, :BLK]
    dx = pay_ref[:, BLK:]
    mask = mask_ref[...].astype(F32)
    prob = prob_ref[...]
    for d in range(QUADS):
        at = member == d
        mixed = jnp.zeros((TOK, BLK), F32)
        for part in three(jnp.where(at, prob, 0.0)):
            mixed = mixed + dot(part, y, ((1,), (0,)))
        grad = dot(jnp.where(at, mask, 0.0).astype(BF16), dx, ((1,), (0,)))
        out_ref[q ^ d] = jnp.concatenate([mixed, grad], axis=1).astype(BF16)


def shape_of(*dims, dtype=BF16):
    return jax.ShapeDtypeStruct(dims, dtype)


def shards(
    tokens,
    grad_out,
    routes,
    gate_probs,
    w_gate,
    w_up,
    w_down,
    dest,
    next_master,
    next_first,
    next_second,
):
    quad = (lax.axis_index("x_lo") * 2 + lax.axis_index("core")).astype(jnp.int32).reshape(1)

    with jax.named_scope("tokens_to_quad"):
        mine = jnp.concatenate([tokens, grad_out], axis=1)
        near = jnp.concatenate([mine, lax.ppermute(mine, "core", SWAP)], axis=0)
        far = lax.ppermute(near, "x_lo", SWAP)

    with jax.named_scope("weights_to_quad"):
        w0 = jnp.stack([w_gate[0], w_up[0], w_down[0].T])
        w2 = lax.ppermute(w0, "x_lo", SWAP)
        w1 = lax.ppermute(w0, "core", SWAP)
        w3 = lax.ppermute(w2, "core", SWAP)

    with jax.named_scope("dispatch"):
        pay, mask, prob = call(
            dispatch_kernel,
            (shape_of(WIDE, 2 * BLK), shape_of(TOK, WIDE), shape_of(TOK, WIDE, dtype=F32)),
            (quad, routes, gate_probs, near, far),
            flops=2 * 16 * TOK * WIDE * BLK,
            moved=800000,
        )
        got = lax.all_to_all(pay, EXPERT, split_axis=0, concat_axis=0, tiled=True)

    with jax.named_scope("partial_sums"):
        sums, x_rows, dy_rows = call(
            partial_kernel,
            (shape_of(ROWS, 3 * FF), shape_of(ROWS, 4 * BLK), shape_of(ROWS, 4 * BLK)),
            (got, w0, w1, w2, w3),
            flops=2 * 3 * ROWS * FF * 4 * BLK,
            moved=4000000,
        )
        parts = lax.all_to_all(sums, "y", split_axis=0, concat_axis=0, tiled=True)

    with jax.named_scope("activation"):
        hidden = call(
            act_kernel, shape_of(ROWS // Y, 3 * FF), (parts,), flops=4000000, moved=1000000
        )
        whole = lax.all_gather(hidden, "y", axis=0, tiled=True)

    with jax.named_scope("slot_outputs"):
        back = call(
            back_kernel,
            shape_of(WIDE, 2 * BLK),
            (whole, w0, w1, w2, w3),
            flops=2 * 3 * ROWS * FF * 4 * BLK,
            moved=4000000,
        )
        returned = lax.all_to_all(back, EXPERT, split_axis=0, concat_axis=0, tiled=True)

    with jax.named_scope("weight_grads"):
        keep, send = call(
            grad_kernel,
            (shape_of(2, 3, BLK, FF, dtype=F32), shape_of(2, 3, BLK, FF)),
            (whole, x_rows, dy_rows),
            flops=2 * 3 * ROWS * FF * 4 * BLK,
            moved=6000000,
        )
        pair = keep + lax.ppermute(send, "core", SWAP).astype(F32)
        other = lax.ppermute(pair[1].astype(BF16), "x_lo", SWAP)
        grads = (pair[0] + other.astype(F32)).astype(BF16)

    with jax.named_scope("combine"):
        mixes = call(
            combine_kernel,
            shape_of(QUADS, TOK, 2 * BLK),
            (quad, returned, mask, prob),
            flops=2 * 16 * TOK * WIDE * BLK,
            moved=800000,
        )
        mixes = lax.all_to_all(mixes, QUAD, split_axis=0, concat_axis=0, tiled=True)
        mixes = jnp.sum(mixes.astype(F32), axis=0).astype(BF16)

    with jax.named_scope("relocate"):
        state = jnp.concatenate([next_master, next_first, next_second], axis=0)
        partner = lax.ppermute(state, "x_hi", SWAP)
        place_index = lax.axis_index(EXPERT).astype(jnp.int32)
        moving = dest[0] != place_index
        moved = jnp.where(moving, partner, state)

    return (
        mixes[:, :BLK],
        mixes[:, BLK:],
        grads[0][None],
        grads[1][None],
        grads[2].T[None],
        moved[0:1],
        moved[1:2],
        moved[2:3],
    )


def solution(mesh):
    fine = Mesh(
        mesh.devices.reshape(2, 8, 2, 2, 16), ("x_lo", "y", "core", "x_hi", "z")
    )
    return jax.shard_map(
        shards,
        mesh=fine,
        in_specs=(
            P(EXPERT, DP),
            P(EXPERT, DP),
            P(EXPERT, None),
            P(EXPERT, None),
            P(EXPERT, DP, None),
            P(EXPERT, DP, None),
            P(EXPERT, None, DP),
            P(EXPERT),
            P(EXPERT, DP, None),
            P(EXPERT, DP, None),
            P(EXPERT, DP, None),
        ),
        out_specs=(
            P(EXPERT, DP),
            P(EXPERT, DP),
            P(EXPERT, DP, None),
            P(EXPERT, DP, None),
            P(EXPERT, None, DP),
            P(EXPERT, DP, None),
            P(EXPERT, DP, None),
            P(EXPERT, DP, None),
        ),
        check_vma=False,
    )
```

time: 355 us -> 187 us (0.53)
  waiting for transfers between devices: 241 us -> 36.8 us
  blocking collectives: 0 us -> 47.7 us
  matrix products: 20.7 us -> 0 us
  starting transfers between devices: 55.7 us -> 74.8 us
  between operations: 15 us -> 1.47 us
  Pallas kernels: 0 us -> 9.81 us
  other arithmetic: 12.9 us -> 6.49 us
    reduce_scatter x1 -> x0, waiting for transfers between devices: 126 us -> none  [shards(): lax.psum_scatter(jnp.stack([gate_part, up_part, back_part], axis=2), 'dp'...]
    all_gather x1 -> x0, waiting for transfers between devices: 62.8 us -> none  [shards(): lax.all_gather(jnp.stack([act, grad_g, grad_u], axis=2).astype(jnp.bfloat...]
    all_to_all x4 -> x3, waiting for transfers between devices: 52.3 us -> 9.5 us  [the longest x1 5.5 us: shards(): mixes = lax.all_to_all(mixes, QUAD, split_axis=0, concat_axis=0, tiled=True)]
    ppermute x3 -> x8, starting transfers between devices: 8.73 us -> 48.3 us  [the longest x1 16.1 us: shards(): near = jnp.concatenate([mine, lax.ppermute(mine, 'core', SWAP)], axis=0)]
    all_to_all x0 -> x1, blocking collectives: none -> 27.6 us  [shards(): parts = lax.all_to_all(sums, 'y', split_axis=0, concat_axis=0, tiled=True)]
    ppermute x3 -> x8, waiting for transfers between devices: 0.01 us -> 27.2 us  [the longest x1 12.6 us: shards(): w2 = lax.ppermute(w0, 'x_lo', SWAP)]
    dot_general x13 -> x0, matrix products: 20.7 us -> none  [the longest x1 2.47 us: shards(): jnp.einsum('mef,emd->efd', act, recv_dy, preferred_element_type=jnp.float32)]
    all_to_all x4 -> x3, starting transfers between devices: 46.8 us -> 26.5 us  [the longest x1 13.5 us: shards(): lax.all_to_all(back, EXPERT, split_axis=0, concat_axis=0, tiled=True)]
  transfers between devices with their start and end apart: 9 -> 11, of which waited for: 6 -> 7; matrix products, arithmetic and copies ran while one was open for 8% -> 5% of each run, Pallas kernels for 0% -> 2%
where the time goes in v1:
time: 187 us; the launch traced here: 186 us
  starting transfers between devices  74.8 us (40%)
  blocking collectives  47.7 us (26%)
  waiting for transfers between devices  36.8 us (20%)
  Pallas kernels  9.81 us (5%)
  local copies, waits for them, and re-layouts  8.62 us (5%)
  other arithmetic  6.49 us (3%)
    all_to_all x1, blocking collectives, shards(): parts = lax.all_to_all(sums, 'y', split_axis=0, concat_axis=0, tiled=True)  27.6 us
    all_gather x1, blocking collectives, shards(): whole = lax.all_gather(hidden, 'y', axis=0, tiled=True)  20.1 us
    ppermute x1, starting transfers between devices, shards(): near = jnp.concatenate([mine, lax.ppermute(mine, 'core', SWAP)], axis=0)  16.1 us
    all_to_all x1, starting transfers between devices, shards(): lax.all_to_all(back, EXPERT, split_axis=0, concat_axis=0, tiled=True)  13.5 us
    ppermute x1, starting transfers between devices, shards(): pair = keep + lax.ppermute(send, 'core', SWAP).astype(F32)  13.5 us
    ppermute x1, waiting for transfers between devices, shards(): w2 = lax.ppermute(w0, 'x_lo', SWAP)  12.6 us
    ppermute x1, waiting for transfers between devices, shards(): partner = lax.ppermute(state, 'x_hi', SWAP)  10.7 us
    pallas_call x6, Pallas kernels, call(): pl.pallas_call(kernel, out_shape=out_shape, in_specs=[smem if o.dtype ==...  9.81 us
  transfers between devices with their start and end apart: 11, of which 7 were waited for; matrix products, arithmetic and copies ran while one was open for 5% of the time, Pallas kernels for 2%

profile of v1, /device:TPU:1, one launch (start us, length us, event | category | flops | bytes accessed | tf_op | source)
XLA Modules:
  0.0 185.6 jit_solution(1071884785881957125)
XLA Ops:
  0.6 0.7 constant_dynamic-update-slice_fusion.1
  1.4 0.7 constant_dynamic-update-slice_fusion
  2.1 16.1 %collective-permute-start = (bf16[64,256]{1,0:T(8,128)(2,1)S(1)}, bf16[64,256]{1,0:T(8,128)(2,1)S(1)}, u32[]{:S(2)}, u32[]{:S(2)}) collective-permute-start(bf16[64,256]{1,0:T(8,128)(2,1)S(1)} %constant_dynamic-update-slice_fusion), channel_id=1, source_target_pairs={{0,32},{32,0},{1,33},{33,1},{2,34},{34,2},{3,35},{35,3},{4,36},{36... | collective-permute-start | bytes 98312 | tf_op jit(solution)/shard_map/tokens_to_quad/ppermute | solution.py:206
  18.1 0.8 collective-permute-done
  19.0 1.9 %collective-permute-start.1 = (bf16[128,256]{1,0:T(8,128)(2,1)S(1)}, bf16[128,256]{1,0:T(8,128)(2,1)S(1)}, u32[]{:S(2)}, u32[]{:S(2)}) collective-permute-start(bf16[128,256]{1,0:T(8,128)(2,1)S(1)} %pad_maximum_fusion.2.near_ref), channel_id=1, source_target_pairs={{0,512},{512,0},{1,513},{513,1},{2,514},{514,2},{3,515},{515,3},{4... | collective-permute-start | bytes 196616 | tf_op jit(solution)/shard_map/tokens_to_quad/ppermute | solution.py:207
  20.9 0.8 copy.19.routes_ref
  21.7 0.8 copy.20.probs_ref
  22.4 1.5 collective-permute-done.1.far_ref
  24.0 2.2 %dispatch.1 = (bf16[768,256]{1,0:T(8,128)(2,1)}, bf16[64,768]{1,0:T(8,128)(2,1)S(1)}, f32[64,768]{1,0:T(8,128)S(1)}) custom-call(s32[1]{0:T(128)} %bitcast.q_ref, s32[64,8]{1,0:T(8,128)S(1)} %copy.19.routes_ref, f32[64,8]{1,0:T(8,128)S(1)} %copy.20.probs_ref, bf16[128,256]{1,0:T(8,128)(2,1)S(1)} %pad_maximum_fusion.2.near_ref, ...), custom_call_target="tpu_custom_call" | custom-call | flops 201326592 | bytes 800000 | tf_op jit(solution)/shard_map/dispatch/pallas_call | solution.py:35
  26.2 8.7 %all-to-all-start = ((bf16[32,24,256]{2,1,0:T(8,128)(2,1)}), bf16[32,24,256]{2,1,0:T(8,128)(2,1)S(1)}, u32[]{:S(2)}, u32[]{:S(2)}) async-start(bf16[32,24,256]{2,1,0:T(8,128)(2,1)} %bitcast.1), calls=%async_computation | async-start | bytes 786432 | tf_op jit(solution)/shard_map/dispatch/all_to_all | solution.py:223
  34.9 1.1 copy.21
  35.9 1.1 pad_maximum_fusion.w0
  37.0 2.2 %collective-permute-start.3 = (bf16[3,128,768]{2,1,0:T(8,128)(2,1)S(1)}, bf16[3,128,768]{2,1,0:T(8,128)(2,1)S(1)}, u32[]{:S(2)}, u32[]{:S(2)}) collective-permute-start(bf16[3,128,768]{2,1,0:T(8,128)(2,1)S(1)} %pad_maximum_fusion.w0), channel_id=1, source_target_pairs={{0,512},{512,0},{1,513},{513,1},{2,514},{514,2},{3,515},{515,3},{4... | collective-permute-start | bytes 1769480 | tf_op jit(solution)/shard_map/weights_to_quad/ppermute | solution.py:211
  39.3 4.0 %collective-permute-start.2 = (bf16[3,128,768]{2,1,0:T(8,128)(2,1)S(1)}, bf16[3,128,768]{2,1,0:T(8,128)(2,1)S(1)}, u32[]{:S(2)}, u32[]{:S(2)}) collective-permute-start(bf16[3,128,768]{2,1,0:T(8,128)(2,1)S(1)} %pad_maximum_fusion.w0), channel_id=1, source_target_pairs={{0,32},{32,0},{1,33},{33,1},{2,34},{34,2},{3,35},{35,3},{4,36},{36... | collective-permute-start | bytes 1769480 | tf_op jit(solution)/shard_map/weights_to_quad/ppermute | solution.py:212
  43.2 12.6 %collective-permute-done.3.w2 = bf16[3,128,768]{2,1,0:T(8,128)(2,1)S(1)} collective-permute-done((bf16[3,128,768]{2,1,0:T(8,128)(2,1)S(1)}, bf16[3,128,768]{2,1,0:T(8,128)(2,1)S(1)}, u32[]{:S(2)}, u32[]{:S(2)}) %collective-permute-start.3) | collective-permute-done | bytes 589856 | tf_op jit(solution)/shard_map/weights_to_quad/ppermute | solution.py:211
  55.8 4.0 %collective-permute-start.4 = (bf16[3,128,768]{2,1,0:T(8,128)(2,1)S(1)}, bf16[3,128,768]{2,1,0:T(8,128)(2,1)S(1)}, u32[]{:S(2)}, u32[]{:S(2)}) collective-permute-start(bf16[3,128,768]{2,1,0:T(8,128)(2,1)S(1)} %collective-permute-done.3.w2), channel_id=1, source_target_pairs={{0,32},{32,0},{1,33},{33,1},{2,34},{34,2},{3,35},{35,3},{4,36},{36... | collective-permute-start | bytes 1769480 | tf_op jit(solution)/shard_map/weights_to_quad/ppermute | solution.py:213
  59.8 0.0 collective-permute-done.2.w1
  59.8 1.6 collective-permute-done.4.w3
  61.4 0.0 all-to-all-done
  61.4 1.5 partial_sums.1
  63.0 27.6 %all_to_all.38 = bf16[8,24,2304]{2,1,0:T(8,128)(2,1)S(1)} all-to-all(bf16[8,24,2304]{2,1,0:T(8,128)(2,1)S(1)} %bitcast.31), channel_id=1, replica_groups=mesh['x_lo'=2,'y'=8,'core'=2,'x_hi'=2,'z'=16] {'y'}, dimensions={0} | all-to-all | bytes 1769472 | tf_op jit(solution)/shard_map/partial_sums/all_to_all | solution.py:233
  90.6 0.1 activation.1
  90.8 20.1 %all_gather.3.h_ref = bf16[192,2304]{1,0:T(8,128)(2,1)S(1)} all-gather(bf16[24,2304]{1,0:T(8,128)(2,1)S(1)} %activation.1), channel_id=1, replica_groups=mesh['x_lo'=2,'y'=8,'core'=2,'x_hi'=2,'z'=16] {'y'}, dimensions={0}, use_global_device_ids=true | all-gather | bytes 995328 | tf_op jit(solution)/shard_map/activation/all_gather | solution.py:239
  110.8 1.9 %weight_grads.1 = (f32[2,3,128,768]{3,2,1,0:T(8,128)S(1)}, bf16[2,3,128,768]{3,2,1,0:T(8,128)(2,1)}) custom-call(bf16[192,2304]{1,0:T(8,128)(2,1)S(1)} %all_gather.3.h_ref, bf16[192,512]{1,0:T(8,128)(2,1)S(1)} %get-tuple-element.20.x_ref, bf16[192,512]{1,0:T(8,128)(2,1)S(1)} %get-tuple-element.21.dy_ref), custom_call_target="tpu_custom_call" | custom-call | flops 452984832 | bytes 6000000 | tf_op jit(solution)/shard_map/weight_grads/pallas_call | solution.py:35
  112.7 0.0 copy-start
  112.7 0.0 copy-start.3
  112.7 13.5 %collective-permute-start.5 = (bf16[2,3,128,768]{3,2,1,0:T(8,128)(2,1)}, bf16[2,3,128,768]{3,2,1,0:T(8,128)(2,1)}, u32[]{:S(2)}, u32[]{:S(2)}) collective-permute-start(bf16[2,3,128,768]{3,2,1,0:T(8,128)(2,1)} %get-tuple-element.23), channel_id=1, source_target_pairs={{0,32},{32,0},{1,33},{33,1},{2,34},{34,2},{3,35},{35,3},{4,36},{36... | collective-permute-start | bytes 3538952 | tf_op jit(solution)/shard_map/weight_grads/ppermute | solution.py:259
  126.2 2.8 %slot_outputs.1 = bf16[768,256]{1,0:T(8,128)(2,1)} custom-call(bf16[192,2304]{1,0:T(8,128)(2,1)S(1)} %all_gather.3.h_ref, bf16[3,128,768]{2,1,0:T(8,128)(2,1)S(1)} %pad_maximum_fusion.w0, bf16[3,128,768]{2,1,0:T(8,128)(2,1)S(1)} %collective-permute-done.2.w1, bf16[3,128,768]{2,1,0:T(8,128)(2,1)S(1)} %collective-permute-done.3.w2, ...), custom_call_target="tpu_custom_call" | custom-call | flops 452984832 | bytes 4000000 | tf_op jit(solution)/shard_map/slot_outputs/pallas_call | solution.py:35
  129.0 0.0 copy-done
  129.0 0.0 copy-start.1
  129.0 13.5 %all-to-all-start.2 = ((bf16[32,24,256]{2,1,0:T(8,128)(2,1)}), bf16[32,24,256]{2,1,0:T(8,128)(2,1)S(1)}, u32[]{:S(2)}, u32[]{:S(2)}) async-start(bf16[32,24,256]{2,1,0:T(8,128)(2,1)} %bitcast.8), calls=%async_computation.2 | async-start | bytes 786432 | tf_op jit(solution)/shard_map/slot_outputs/all_to_all | solution.py:249
  142.5 0.0 copy-done.3
  142.5 1.2 pad_maximum_fusion.1
  143.7 4.7 %collective-permute-start.7 = (f32[3,12,2048]{2,0,1:T(4,128)S(1)}, f32[3,12,2048]{2,0,1:T(4,128)}, u32[]{:S(2)}, u32[]{:S(2)}) collective-permute-start(f32[3,12,2048]{2,0,1:T(4,128)S(1)} %pad_maximum_fusion.1), channel_id=1, source_target_pairs={{0,16},{16,0},{1,17},{17,1},{2,18},{18,2},{3,19},{19,3},{4,20},{20... | collective-permute-start | bytes 884744 | tf_op jit(solution)/shard_map/relocate/ppermute | solution.py:276
  149.0 10.7 %collective-permute-done.7 = f32[3,12,2048]{2,0,1:T(4,128)} collective-permute-done((f32[3,12,2048]{2,0,1:T(4,128)S(1)}, f32[3,12,2048]{2,0,1:T(4,128)}, u32[]{:S(2)}, u32[]{:S(2)}) %collective-permute-start.7) | collective-permute-done | bytes 294944 | tf_op jit(solution)/shard_map/relocate/ppermute | solution.py:276
  159.7 1.3 broadcast_select_fusion
  161.0 0.0 collective-permute-done.5
  161.0 0.0 copy-done.1
  161.0 1.5 convert_add_fusion
  162.5 0.0 copy-start.2
  162.5 0.1 fusion.2
  162.6 1.4 copy-done.2
  164.0 2.0 %collective-permute-start.6 = (bf16[3,128,768]{2,1,0:T(8,128)(2,1)S(1)}, bf16[3,128,768]{2,1,0:T(8,128)(2,1)S(1)}, u32[]{:S(2)}, u32[]{:S(2)}) collective-permute-start(bf16[3,128,768]{2,1,0:T(8,128)(2,1)S(1)} %fusion.2), channel_id=1, source_target_pairs={{0,512},{512,0},{1,513},{513,1},{2,514},{514,2},{3,515},{515,3},{4... | collective-permute-start | bytes 1769480 | tf_op jit(solution)/shard_map/weight_grads/ppermute | solution.py:260
  166.0 4.0 %all-to-all-done.2 = bf16[32,24,256]{2,1,0:T(8,128)(2,1)S(1)} async-done(((bf16[32,24,256]{2,1,0:T(8,128)(2,1)}), bf16[32,24,256]{2,1,0:T(8,128)(2,1)S(1)}, u32[]{:S(2)}, u32[]{:S(2)}) %all-to-all-start.2) | async-done | bytes 393248 | tf_op jit(solution)/shard_map/slot_outputs/all_to_all | solution.py:249
  170.0 1.2 combine.1
  171.2 4.3 %all-to-all-start.3 = ((bf16[4,64,256]{2,1,0:T(8,128)(2,1)}), bf16[4,64,256]{2,1,0:T(8,128)(2,1)S(1)}, u32[]{:S(2)}, u32[]{:S(2)}) async-start(bf16[4,64,256]{2,1,0:T(8,128)(2,1)} %combine.1), calls=%async_computation.3 | async-start | bytes 262144 | tf_op jit(solution)/shard_map/combine/all_to_all | solution.py:271
  175.6 0.9 fusion.3
  176.5 5.5 %all-to-all-done.3 = bf16[4,64,256]{2,1,0:T(8,128)(2,1)S(1)} async-done(((bf16[4,64,256]{2,1,0:T(8,128)(2,1)}), bf16[4,64,256]{2,1,0:T(8,128)(2,1)S(1)}, u32[]{:S(2)}, u32[]{:S(2)}) %all-to-all-start.3) | async-done | bytes 131104 | tf_op jit(solution)/shard_map/combine/all_to_all | solution.py:271
  182.0 0.6 fusion.4
  182.6 0.0 collective-permute-done.6
  182.6 1.4 fusion.1
  184.0 0.8 slice_bitcast_fusion.1
  184.8 0.8 copy.22
  (2 shorter events, 0.0 us)
Async XLA Ops:
  2.1 16.9 %collective-permute-start = (bf16[64,256]{1,0:T(8,128)(2,1)S(1)}, bf16[64,256]{1,0:T(8,128)(2,1)S(1)}, u32[]{:S(2)}, u32[]{:S(2)}) collective-permute-start(bf16[64,256]{1,0:T(8,128)(2,1)S(1)} %constant_dynamic-update-slice_fusion), channel_id=1, source_target_pairs={{0,32},{32,0},{1,33},{33,1},{2,34},{34,2},{3,35},{35,3},{4,36},{36... | collective-permute-start | bytes 98312 | tf_op jit(solution)/shard_map/tokens_to_quad/ppermute | solution.py:206
  19.0 5.0 %collective-permute-start.1 = (bf16[128,256]{1,0:T(8,128)(2,1)S(1)}, bf16[128,256]{1,0:T(8,128)(2,1)S(1)}, u32[]{:S(2)}, u32[]{:S(2)}) collective-permute-start(bf16[128,256]{1,0:T(8,128)(2,1)S(1)} %pad_maximum_fusion.2.near_ref), channel_id=1, source_target_pairs={{0,512},{512,0},{1,513},{513,1},{2,514},{514,2},{3,515},{515,3},{4... | collective-permute-start | bytes 196616 | tf_op jit(solution)/shard_map/tokens_to_quad/ppermute | solution.py:207
  26.2 35.3 %all-to-all-start = ((bf16[32,24,256]{2,1,0:T(8,128)(2,1)}), bf16[32,24,256]{2,1,0:T(8,128)(2,1)S(1)}, u32[]{:S(2)}, u32[]{:S(2)}) async-start(bf16[32,24,256]{2,1,0:T(8,128)(2,1)} %bitcast.1), calls=%async_computation | async-start | bytes 786432 | tf_op jit(solution)/shard_map/dispatch/all_to_all | solution.py:223
  37.0 18.8 %collective-permute-start.3 = (bf16[3,128,768]{2,1,0:T(8,128)(2,1)S(1)}, bf16[3,128,768]{2,1,0:T(8,128)(2,1)S(1)}, u32[]{:S(2)}, u32[]{:S(2)}) collective-permute-start(bf16[3,128,768]{2,1,0:T(8,128)(2,1)S(1)} %pad_maximum_fusion.w0), channel_id=1, source_target_pairs={{0,512},{512,0},{1,513},{513,1},{2,514},{514,2},{3,515},{515,3},{4... | collective-permute-start | bytes 1769480 | tf_op jit(solution)/shard_map/weights_to_quad/ppermute | solution.py:211
  39.3 20.6 %collective-permute-start.2 = (bf16[3,128,768]{2,1,0:T(8,128)(2,1)S(1)}, bf16[3,128,768]{2,1,0:T(8,128)(2,1)S(1)}, u32[]{:S(2)}, u32[]{:S(2)}) collective-permute-start(bf16[3,128,768]{2,1,0:T(8,128)(2,1)S(1)} %pad_maximum_fusion.w0), channel_id=1, source_target_pairs={{0,32},{32,0},{1,33},{33,1},{2,34},{34,2},{3,35},{35,3},{4,36},{36... | collective-permute-start | bytes 1769480 | tf_op jit(solution)/shard_map/weights_to_quad/ppermute | solution.py:212
  55.8 5.6 %collective-permute-start.4 = (bf16[3,128,768]{2,1,0:T(8,128)(2,1)S(1)}, bf16[3,128,768]{2,1,0:T(8,128)(2,1)S(1)}, u32[]{:S(2)}, u32[]{:S(2)}) collective-permute-start(bf16[3,128,768]{2,1,0:T(8,128)(2,1)S(1)} %collective-permute-done.3.w2), channel_id=1, source_target_pairs={{0,32},{32,0},{1,33},{33,1},{2,34},{34,2},{3,35},{35,3},{4,36},{36... | collective-permute-start | bytes 1769480 | tf_op jit(solution)/shard_map/weights_to_quad/ppermute | solution.py:213
  112.7 16.3 %copy-start = (f32[2,3,128,768]{3,2,1,0:T(8,128)}, f32[2,3,128,768]{3,2,1,0:T(8,128)S(1)}, u32[]{:S(2)}) copy-start(f32[2,3,128,768]{3,2,1,0:T(8,128)S(1)} %get-tuple-element.22) | copy-start | bytes 7077892
  112.7 29.8 %copy-start.3 = (f32[1,12,2048]{2,0,1:T(1,128)S(1)}, f32[1,12,2048]{2,0,1:T(1,128)}, u32[]{:S(2)}) copy-start(f32[1,12,2048]{2,0,1:T(1,128)} %param.21) | copy-start | bytes 294916
  112.7 48.3 %collective-permute-start.5 = (bf16[2,3,128,768]{3,2,1,0:T(8,128)(2,1)}, bf16[2,3,128,768]{3,2,1,0:T(8,128)(2,1)}, u32[]{:S(2)}, u32[]{:S(2)}) collective-permute-start(bf16[2,3,128,768]{3,2,1,0:T(8,128)(2,1)} %get-tuple-element.23), channel_id=1, source_target_pairs={{0,32},{32,0},{1,33},{33,1},{2,34},{34,2},{3,35},{35,3},{4,36},{36... | collective-permute-start | bytes 3538952 | tf_op jit(solution)/shard_map/weight_grads/ppermute | solution.py:259
  129.0 32.0 %copy-start.1 = (f32[2,3,128,768]{3,2,1,0:T(8,128)S(1)}, f32[2,3,128,768]{3,2,1,0:T(8,128)}, u32[]{:S(2)}) copy-start(f32[2,3,128,768]{3,2,1,0:T(8,128)} %copy-done) | copy-start | bytes 7077892
  129.0 41.0 %all-to-all-start.2 = ((bf16[32,24,256]{2,1,0:T(8,128)(2,1)}), bf16[32,24,256]{2,1,0:T(8,128)(2,1)S(1)}, u32[]{:S(2)}, u32[]{:S(2)}) async-start(bf16[32,24,256]{2,1,0:T(8,128)(2,1)} %bitcast.8), calls=%async_computation.2 | async-start | bytes 786432 | tf_op jit(solution)/shard_map/slot_outputs/all_to_all | solution.py:249
  143.7 16.0 %collective-permute-start.7 = (f32[3,12,2048]{2,0,1:T(4,128)S(1)}, f32[3,12,2048]{2,0,1:T(4,128)}, u32[]{:S(2)}, u32[]{:S(2)}) collective-permute-start(f32[3,12,2048]{2,0,1:T(4,128)S(1)} %pad_maximum_fusion.1), channel_id=1, source_target_pairs={{0,16},{16,0},{1,17},{17,1},{2,18},{18,2},{3,19},{19,3},{4,20},{20... | collective-permute-start | bytes 884744 | tf_op jit(solution)/shard_map/relocate/ppermute | solution.py:276
  162.5 1.4 copy-start.2
  164.0 18.7 %collective-permute-start.6 = (bf16[3,128,768]{2,1,0:T(8,128)(2,1)S(1)}, bf16[3,128,768]{2,1,0:T(8,128)(2,1)S(1)}, u32[]{:S(2)}, u32[]{:S(2)}) collective-permute-start(bf16[3,128,768]{2,1,0:T(8,128)(2,1)S(1)} %fusion.2), channel_id=1, source_target_pairs={{0,512},{512,0},{1,513},{513,1},{2,514},{514,2},{3,515},{515,3},{4... | collective-permute-start | bytes 1769480 | tf_op jit(solution)/shard_map/weight_grads/ppermute | solution.py:260
  171.2 10.8 %all-to-all-start.3 = ((bf16[4,64,256]{2,1,0:T(8,128)(2,1)}), bf16[4,64,256]{2,1,0:T(8,128)(2,1)S(1)}, u32[]{:S(2)}, u32[]{:S(2)}) async-start(bf16[4,64,256]{2,1,0:T(8,128)(2,1)} %combine.1), calls=%async_computation.3 | async-start | bytes 262144 | tf_op jit(solution)/shard_map/combine/all_to_all | solution.py:271

commit v2 on v1

--- a/solution.py
+++ b/solution.py
@@ -61,7 +61,12 @@
     return lax.dot_general(a, b, (dims, ((), ())), preferred_element_type=F32)
 
 
-def dispatch_kernel(q_ref, routes_ref, probs_ref, near_ref, far_ref, pay_ref, mask_ref, prob_ref):
+def join_kernel(a_ref, b_ref, out_ref):
+    out_ref[:, :BLK] = a_ref[...]
+    out_ref[:, BLK:] = b_ref[...]
+
+
+def table_kernel(q_ref, routes_ref, probs_ref, mask_ref, prob_ref):
     q = q_ref[0]
     shape = (TOK, WIDE)
     pair, member, slot = row_fields(shape, 1)
@@ -80,6 +85,13 @@
     prob = jnp.where(here, weight, 0.0)
     mask_ref[...] = mask.astype(BF16)
     prob_ref[...] = prob
+
+
+def dispatch_kernel(mask_ref, prob_ref, near_ref, far_ref, pay_ref):
+    shape = (TOK, WIDE)
+    _, member, _ = row_fields(shape, 1)
+    mask = mask_ref[...].astype(F32)
+    prob = prob_ref[...]
     masks = [jnp.where(member == d, mask, 0.0).astype(BF16) for d in range(QUADS)]
     parts = three(prob)
     x = jnp.zeros((WIDE, BLK), F32)
@@ -202,7 +214,7 @@
     quad = (lax.axis_index("x_lo") * 2 + lax.axis_index("core")).astype(jnp.int32).reshape(1)
 
     with jax.named_scope("tokens_to_quad"):
-        mine = jnp.concatenate([tokens, grad_out], axis=1)
+        mine = call(join_kernel, shape_of(TOK, 2 * BLK), (tokens, grad_out), moved=65536)
         near = jnp.concatenate([mine, lax.ppermute(mine, "core", SWAP)], axis=0)
         far = lax.ppermute(near, "x_lo", SWAP)
 
@@ -213,14 +225,24 @@
         w3 = lax.ppermute(w2, "core", SWAP)
 
     with jax.named_scope("dispatch"):
-        pay, mask, prob = call(
+        mask, prob = call(
+            table_kernel,
+            (shape_of(TOK, WIDE), shape_of(TOK, WIDE, dtype=F32)),
+            (quad, routes, gate_probs),
+            flops=2 * TOK * TOK * WIDE,
+            moved=300000,
+        )
+        pay = call(
             dispatch_kernel,
-            (shape_of(WIDE, 2 * BLK), shape_of(TOK, WIDE), shape_of(TOK, WIDE, dtype=F32)),
-            (quad, routes, gate_probs, near, far),
+            shape_of(WIDE, 2 * BLK),
+            (mask, prob, near, far),
             flops=2 * 16 * TOK * WIDE * BLK,
             moved=800000,
         )
         got = lax.all_to_all(pay, EXPERT, split_axis=0, concat_axis=0, tiled=True)
+
+    with jax.named_scope("relocate"):
+        state = jnp.concatenate([next_master, next_first, next_second], axis=0)
 
     with jax.named_scope("partial_sums"):
         sums, x_rows, dy_rows = call(
@@ -230,7 +252,10 @@
             flops=2 * 3 * ROWS * FF * 4 * BLK,
             moved=4000000,
         )
+        sums, state = lax.optimization_barrier((sums, state))
         parts = lax.all_to_all(sums, "y", split_axis=0, concat_axis=0, tiled=True)
+        partner = lax.ppermute(state, "x_hi", SWAP)
+        parts, partner = lax.optimization_barrier((parts, partner))
 
     with jax.named_scope("activation"):
         hidden = call(
@@ -246,6 +271,7 @@
             flops=2 * 3 * ROWS * FF * 4 * BLK,
             moved=4000000,
         )
+        back, whole = lax.optimization_barrier((back, whole))
         returned = lax.all_to_all(back, EXPERT, split_axis=0, concat_axis=0, tiled=True)
 
     with jax.named_scope("weight_grads"):
@@ -272,8 +298,6 @@
         mixes = jnp.sum(mixes.astype(F32), axis=0).astype(BF16)
 
     with jax.named_scope("relocate"):
-        state = jnp.concatenate([next_master, next_first, next_second], axis=0)
-        partner = lax.ppermute(state, "x_hi", SWAP)
         place_index = lax.axis_index(EXPERT).astype(jnp.int32)
         moving = dest[0] != place_index
         moved = jnp.where(moving, partner, state)

time: 187 us -> 186 us (level)
  blocking collectives: 47.7 us -> 21.1 us
  waiting for transfers between devices: 36.8 us -> 56.1 us
  starting transfers between devices: 74.8 us -> 80.4 us
  local copies, waits for them, and re-layouts: 8.62 us -> 10.9 us
    all_to_all x1 -> x0, blocking collectives: 27.6 us -> none  [shards(): parts = lax.all_to_all(sums, 'y', split_axis=0, concat_axis=0, tiled=True)]
    all_to_all x1, waiting for transfers between devices: 4 us -> 20.8 us  [shards(): lax.all_to_all(back, EXPERT, split_axis=0, concat_axis=0, tiled=True)]
    all_to_all x0 -> x1, waiting for transfers between devices: none -> 10.9 us  [shards(): parts = lax.all_to_all(sums, 'y', split_axis=0, concat_axis=0, tiled=True)]
    all_to_all x0 -> x1, starting transfers between devices: none -> 6.82 us  [shards(): parts = lax.all_to_all(sums, 'y', split_axis=0, concat_axis=0, tiled=True)]
    ppermute x1, waiting for transfers between devices: 10.7 us -> 6.51 us  [shards(): partner = lax.ppermute(state, 'x_hi', SWAP)]
    unnamed x13 -> x34, local copies, waits for them, and re-layouts: 5.51 us -> 8.49 us
    all_to_all x1, waiting for transfers between devices: 5.5 us -> 2.67 us  [shards(): mixes = lax.all_to_all(mixes, QUAD, split_axis=0, concat_axis=0, tiled=True)]
    pallas_call x6 -> x8, Pallas kernels: 9.81 us -> 9.73 us  [call(): pl.pallas_call(kernel, out_shape=out_shape, in_specs=[smem if o.dtype ==...]
  transfers between devices with their start and end apart: 11 -> 12, of which waited for: 7 -> 8; matrix products, arithmetic and copies ran while one was open for 5% -> 4% of each run, Pallas kernels for 2% -> 1%
where the time goes in v2:
time: 186 us; the launch traced here: 185 us
  starting transfers between devices  80.4 us (43%)
  waiting for transfers between devices  56.1 us (30%)
  blocking collectives  21.1 us (11%)
  local copies, waits for them, and re-layouts  10.9 us (6%)
  Pallas kernels  9.73 us (5%)
  other arithmetic  4.9 us (3%)
    all_gather x1, blocking collectives, shards(): whole = lax.all_gather(hidden, 'y', axis=0, tiled=True)  21.1 us
    all_to_all x1, waiting for transfers between devices, shards(): lax.all_to_all(back, EXPERT, split_axis=0, concat_axis=0, tiled=True)  20.8 us
    ppermute x1, starting transfers between devices, shards(): near = jnp.concatenate([mine, lax.ppermute(mine, 'core', SWAP)], axis=0)  16.2 us
    all_to_all x1, starting transfers between devices, shards(): lax.all_to_all(back, EXPERT, split_axis=0, concat_axis=0, tiled=True)  13.6 us
    ppermute x1, waiting for transfers between devices, shards(): w2 = lax.ppermute(w0, 'x_lo', SWAP)  12.7 us
    ppermute x1, starting transfers between devices, shards(): pair = keep + lax.ppermute(send, 'core', SWAP).astype(F32)  11.7 us
    all_to_all x1, waiting for transfers between devices, shards(): parts = lax.all_to_all(sums, 'y', split_axis=0, concat_axis=0, tiled=True)  10.9 us
    pallas_call x8, Pallas kernels, call(): pl.pallas_call(kernel, out_shape=out_shape, in_specs=[smem if o.dtype ==...  9.73 us
  transfers between devices with their start and end apart: 12, of which 8 were waited for; matrix products, arithmetic and copies ran while one was open for 4% of the time, Pallas kernels for 1%

profile of v2, /device:TPU:1, one launch (start us, length us, event | category | flops | bytes accessed | tf_op | source)
XLA Modules:
  0.0 184.6 jit_solution(8507792272456789573)
XLA Ops:
  0.6 0.0 copy-start.1
  0.6 0.7 copy-done.1
  1.4 0.7 copy-done.2
  2.1 0.0 copy-start.14
  2.1 16.2 %collective-permute-start = (bf16[64,256]{1,0:T(8,128)(2,1)S(1)}, bf16[64,256]{1,0:T(8,128)(2,1)S(1)}, u32[]{:S(2)}, u32[]{:S(2)}) collective-permute-start(bf16[64,256]{1,0:T(8,128)(2,1)S(1)} %tokens_to_quad.1), channel_id=1, source_target_pairs={{0,32},{32,0},{1,33},{33,1},{2,34},{34,2},{3,35},{35,3},{4,36},{36... | collective-permute-start | bytes 98312 | tf_op jit(solution)/shard_map/tokens_to_quad/ppermute | solution.py:218
  18.3 0.8 collective-permute-done
  19.2 1.9 %collective-permute-start.1 = (bf16[128,256]{1,0:T(8,128)(2,1)S(1)}, bf16[128,256]{1,0:T(8,128)(2,1)S(1)}, u32[]{:S(2)}, u32[]{:S(2)}) collective-permute-start(bf16[128,256]{1,0:T(8,128)(2,1)S(1)} %pad_maximum_fusion.2.near_ref), channel_id=1, source_target_pairs={{0,512},{512,0},{1,513},{513,1},{2,514},{514,2},{3,515},{515,3},{4... | collective-permute-start | bytes 196616 | tf_op jit(solution)/shard_map/tokens_to_quad/ppermute | solution.py:219
  21.1 0.8 copy.19.routes_ref
  21.9 0.8 copy.20.probs_ref
  22.6 0.4 dispatch.2
  23.0 1.2 collective-permute-done.1.far_ref
  24.2 1.8 dispatch.3
  25.9 8.7 %all-to-all-start = ((bf16[32,24,256]{2,1,0:T(8,128)(2,1)}), bf16[32,24,256]{2,1,0:T(8,128)(2,1)S(1)}, u32[]{:S(2)}, u32[]{:S(2)}) async-start(bf16[32,24,256]{2,1,0:T(8,128)(2,1)} %bitcast.1), calls=%async_computation | async-start | bytes 786432 | tf_op jit(solution)/shard_map/dispatch/all_to_all | solution.py:242
  34.6 1.1 copy.21
  35.7 0.0 copy-done.10
  35.7 0.0 copy-done.11
  35.7 0.1 pad_maximum_fusion.w0
  35.8 2.2 %collective-permute-start.3 = (bf16[3,128,768]{2,1,0:T(8,128)(2,1)S(1)}, bf16[3,128,768]{2,1,0:T(8,128)(2,1)S(1)}, u32[]{:S(2)}, u32[]{:S(2)}) collective-permute-start(bf16[3,128,768]{2,1,0:T(8,128)(2,1)S(1)} %pad_maximum_fusion.w0), channel_id=1, source_target_pairs={{0,512},{512,0},{1,513},{513,1},{2,514},{514,2},{3,515},{515,3},{4... | collective-permute-start | bytes 1769480 | tf_op jit(solution)/shard_map/weights_to_quad/ppermute | solution.py:223
  38.0 4.0 %collective-permute-start.2 = (bf16[3,128,768]{2,1,0:T(8,128)(2,1)S(1)}, bf16[3,128,768]{2,1,0:T(8,128)(2,1)S(1)}, u32[]{:S(2)}, u32[]{:S(2)}) collective-permute-start(bf16[3,128,768]{2,1,0:T(8,128)(2,1)S(1)} %pad_maximum_fusion.w0), channel_id=1, source_target_pairs={{0,32},{32,0},{1,33},{33,1},{2,34},{34,2},{3,35},{35,3},{4,36},{36... | collective-permute-start | bytes 1769480 | tf_op jit(solution)/shard_map/weights_to_quad/ppermute | solution.py:224
  42.0 12.7 %collective-permute-done.3.w2 = bf16[3,128,768]{2,1,0:T(8,128)(2,1)S(1)} collective-permute-done((bf16[3,128,768]{2,1,0:T(8,128)(2,1)S(1)}, bf16[3,128,768]{2,1,0:T(8,128)(2,1)S(1)}, u32[]{:S(2)}, u32[]{:S(2)}) %collective-permute-start.3) | collective-permute-done | bytes 589856 | tf_op jit(solution)/shard_map/weights_to_quad/ppermute | solution.py:223
  54.7 4.1 %collective-permute-start.4 = (bf16[3,128,768]{2,1,0:T(8,128)(2,1)S(1)}, bf16[3,128,768]{2,1,0:T(8,128)(2,1)S(1)}, u32[]{:S(2)}, u32[]{:S(2)}) collective-permute-start(bf16[3,128,768]{2,1,0:T(8,128)(2,1)S(1)} %collective-permute-done.3.w2), channel_id=1, source_target_pairs={{0,32},{32,0},{1,33},{33,1},{2,34},{34,2},{3,35},{35,3},{4,36},{36... | collective-permute-start | bytes 1769480 | tf_op jit(solution)/shard_map/weights_to_quad/ppermute | solution.py:225
  58.8 0.0 copy-done.12
  58.8 0.0 copy-done.13
  58.8 0.0 copy-done.14
  58.8 1.0 pad_maximum_fusion.1
  59.8 0.0 collective-permute-done.2.w1
  59.8 0.6 collective-permute-done.4.w3
  60.4 0.0 all-to-all-done
  60.4 1.5 partial_sums.1
  61.9 0.0 copy-start
  61.9 0.9 copy-done
  62.8 0.7 copy-done.3
  63.5 0.7 copy-done.5
  64.2 6.8 %all-to-all-start.1 = ((bf16[8,24,2304]{2,1,0:T(8,128)(2,1)}), bf16[8,24,2304]{2,1,0:T(8,128)(2,1)S(1)}, u32[]{:S(2)}, u32[]{:S(2)}) async-start(bf16[8,24,2304]{2,1,0:T(8,128)(2,1)} %bitcast.31), calls=%async_computation.1 | async-start | bytes 1769472 | tf_op jit(solution)/shard_map/partial_sums/all_to_all | solution.py:256
  71.0 4.6 %collective-permute-start.5 = (f32[3,12,2048]{2,0,1:T(4,128)}, f32[3,12,2048]{2,0,1:T(4,128)}, u32[]{:S(2)}, u32[]{:S(2)}) collective-permute-start(f32[3,12,2048]{2,0,1:T(4,128)} %pad_maximum_fusion.1), channel_id=1, source_target_pairs={{0,16},{16,0},{1,17},{17,1},{2,18},{18,2},{3,19},{19,3},{4,20},{20... | collective-permute-start | bytes 884744 | tf_op jit(solution)/shard_map/partial_sums/ppermute | solution.py:257
  75.7 6.5 %collective-permute-done.5 = f32[3,12,2048]{2,0,1:T(4,128)} collective-permute-done((f32[3,12,2048]{2,0,1:T(4,128)}, f32[3,12,2048]{2,0,1:T(4,128)}, u32[]{:S(2)}, u32[]{:S(2)}) %collective-permute-start.5) | collective-permute-done | bytes 294944 | tf_op jit(solution)/shard_map/partial_sums/ppermute | solution.py:257
  82.2 10.9 %all-to-all-done.1 = bf16[8,24,2304]{2,1,0:T(8,128)(2,1)S(1)} async-done(((bf16[8,24,2304]{2,1,0:T(8,128)(2,1)}), bf16[8,24,2304]{2,1,0:T(8,128)(2,1)S(1)}, u32[]{:S(2)}, u32[]{:S(2)}) %all-to-all-start.1) | async-done | bytes 884768 | tf_op jit(solution)/shard_map/partial_sums/all_to_all | solution.py:256
  93.1 0.1 activation.1
  93.2 0.0 copy-start.4
  93.2 0.0 copy-start.6
  93.2 21.1 %all_gather.3.h_ref = bf16[192,2304]{1,0:T(8,128)(2,1)S(1)} all-gather(bf16[24,2304]{1,0:T(8,128)(2,1)S(1)} %activation.1), channel_id=1, replica_groups=mesh['x_lo'=2,'y'=8,'core'=2,'x_hi'=2,'z'=16] {'y'}, dimensions={0}, use_global_device_ids=true | all-gather | bytes 995328 | tf_op jit(solution)/shard_map/activation/all_gather | solution.py:264
  114.3 2.8 %slot_outputs.1 = bf16[768,256]{1,0:T(8,128)(2,1)} custom-call(bf16[192,2304]{1,0:T(8,128)(2,1)S(1)} %all_gather.3.h_ref, bf16[3,128,768]{2,1,0:T(8,128)(2,1)S(1)} %pad_maximum_fusion.w0, bf16[3,128,768]{2,1,0:T(8,128)(2,1)S(1)} %collective-permute-done.2.w1, bf16[3,128,768]{2,1,0:T(8,128)(2,1)S(1)} %collective-permute-done.3.w2, ...), custom_call_target="tpu_custom_call" | custom-call | flops 452984832 | bytes 4000000 | tf_op jit(solution)/shard_map/slot_outputs/pallas_call | solution.py:35
  117.1 1.8 weight_grads.1
  119.0 11.7 %collective-permute-start.6 = (bf16[2,3,128,768]{3,2,1,0:T(8,128)(2,1)}, bf16[2,3,128,768]{3,2,1,0:T(8,128)(2,1)}, u32[]{:S(2)}, u32[]{:S(2)}) collective-permute-start(bf16[2,3,128,768]{3,2,1,0:T(8,128)(2,1)} %get-tuple-element.32), channel_id=1, source_target_pairs={{0,32},{32,0},{1,33},{33,1},{2,34},{34,2},{3,35},{35,3},{4,36},{36... | collective-permute-start | bytes 3538952 | tf_op jit(solution)/shard_map/weight_grads/ppermute | solution.py:285
  130.7 13.6 %all-to-all-start.2 = ((bf16[32,24,256]{2,1,0:T(8,128)(2,1)}), bf16[32,24,256]{2,1,0:T(8,128)(2,1)S(1)}, u32[]{:S(2)}, u32[]{:S(2)}) async-start(bf16[32,24,256]{2,1,0:T(8,128)(2,1)} %bitcast.8), calls=%async_computation.2 | async-start | bytes 786432 | tf_op jit(solution)/shard_map/slot_outputs/all_to_all | solution.py:275
  145.0 0.0 copy-done.8
  145.0 0.9 broadcast_select_fusion
  145.9 0.0 collective-permute-done.6
  145.9 1.5 convert_add_fusion
  147.4 0.0 copy-start.7
  147.4 0.0 copy-start.9
  147.4 0.1 fusion.2
  147.5 1.3 copy-done.7
  148.8 2.2 %collective-permute-start.7 = (bf16[3,128,768]{2,1,0:T(8,128)(2,1)S(1)}, bf16[3,128,768]{2,1,0:T(8,128)(2,1)S(1)}, u32[]{:S(2)}, u32[]{:S(2)}) collective-permute-start(bf16[3,128,768]{2,1,0:T(8,128)(2,1)S(1)} %fusion.2), channel_id=1, source_target_pairs={{0,512},{512,0},{1,513},{513,1},{2,514},{514,2},{3,515},{515,3},{4... | collective-permute-start | bytes 1769480 | tf_op jit(solution)/shard_map/weight_grads/ppermute | solution.py:286
  151.0 20.8 %all-to-all-done.2 = bf16[32,24,256]{2,1,0:T(8,128)(2,1)S(1)} async-done(((bf16[32,24,256]{2,1,0:T(8,128)(2,1)}), bf16[32,24,256]{2,1,0:T(8,128)(2,1)S(1)}, u32[]{:S(2)}, u32[]{:S(2)}) %all-to-all-start.2) | async-done | bytes 393248 | tf_op jit(solution)/shard_map/slot_outputs/all_to_all | solution.py:275
  171.8 1.2 combine.1
  173.1 4.3 %all-to-all-start.3 = ((bf16[4,64,256]{2,1,0:T(8,128)(2,1)}), bf16[4,64,256]{2,1,0:T(8,128)(2,1)S(1)}, u32[]{:S(2)}, u32[]{:S(2)}) async-start(bf16[4,64,256]{2,1,0:T(8,128)(2,1)} %combine.1), calls=%async_computation.3 | async-start | bytes 262144 | tf_op jit(solution)/shard_map/combine/all_to_all | solution.py:297
  177.4 0.9 fusion.3
  178.3 2.7 %all-to-all-done.3 = bf16[4,64,256]{2,1,0:T(8,128)(2,1)S(1)} async-done(((bf16[4,64,256]{2,1,0:T(8,128)(2,1)}), bf16[4,64,256]{2,1,0:T(8,128)(2,1)S(1)}, u32[]{:S(2)}, u32[]{:S(2)}) %all-to-all-start.3) | async-done | bytes 131104 | tf_op jit(solution)/shard_map/combine/all_to_all | solution.py:297
  181.0 0.6 fusion.4
  181.6 0.0 collective-permute-done.7
  181.6 1.4 fusion.1
  183.0 0.8 slice_bitcast_fusion.1
  183.8 0.8 copy.22
  (14 shorter events, 0.1 us)
Async XLA Ops:
  0.6 0.7 copy-start.1
  1.4 0.7 copy-start.2
  2.1 33.6 %copy-start.10 = (bf16[1,128,768]{2,1,0:T(8,128)(2,1)S(1)}, bf16[1,128,768]{2,1,0:T(8,128)(2,1)}, u32[]{:S(2)}) copy-start(bf16[1,128,768]{2,1,0:T(8,128)(2,1)} %param.16) | copy-start | bytes 589828
  2.1 33.6 %copy-start.11 = (bf16[1,128,768]{2,1,0:T(8,128)(2,1)S(1)}, bf16[1,128,768]{2,1,0:T(8,128)(2,1)}, u32[]{:S(2)}) copy-start(bf16[1,128,768]{2,1,0:T(8,128)(2,1)} %param.15) | copy-start | bytes 589828
  2.1 56.7 %copy-start.12 = (f32[1,12,2048]{2,0,1:T(1,128)S(1)}, f32[1,12,2048]{2,0,1:T(1,128)}, u32[]{:S(2)}) copy-start(f32[1,12,2048]{2,0,1:T(1,128)} %param.21) | copy-start | bytes 294916
  2.1 56.7 %copy-start.13 = (f32[1,12,2048]{2,0,1:T(1,128)S(1)}, f32[1,12,2048]{2,0,1:T(1,128)}, u32[]{:S(2)}) copy-start(f32[1,12,2048]{2,0,1:T(1,128)} %param.20) | copy-start | bytes 294916
  2.1 56.7 %copy-start.14 = (f32[1,12,2048]{2,0,1:T(1,128)S(1)}, f32[1,12,2048]{2,0,1:T(1,128)}, u32[]{:S(2)}) copy-start(f32[1,12,2048]{2,0,1:T(1,128)} %param.19) | copy-start | bytes 294916
  2.1 17.0 %collective-permute-start = (bf16[64,256]{1,0:T(8,128)(2,1)S(1)}, bf16[64,256]{1,0:T(8,128)(2,1)S(1)}, u32[]{:S(2)}, u32[]{:S(2)}) collective-permute-start(bf16[64,256]{1,0:T(8,128)(2,1)S(1)} %tokens_to_quad.1), channel_id=1, source_target_pairs={{0,32},{32,0},{1,33},{33,1},{2,34},{34,2},{3,35},{35,3},{4,36},{36... | collective-permute-start | bytes 98312 | tf_op jit(solution)/shard_map/tokens_to_quad/ppermute | solution.py:218
  19.2 5.0 %collective-permute-start.1 = (bf16[128,256]{1,0:T(8,128)(2,1)S(1)}, bf16[128,256]{1,0:T(8,128)(2,1)S(1)}, u32[]{:S(2)}, u32[]{:S(2)}) collective-permute-start(bf16[128,256]{1,0:T(8,128)(2,1)S(1)} %pad_maximum_fusion.2.near_ref), channel_id=1, source_target_pairs={{0,512},{512,0},{1,513},{513,1},{2,514},{514,2},{3,515},{515,3},{4... | collective-permute-start | bytes 196616 | tf_op jit(solution)/shard_map/tokens_to_quad/ppermute | solution.py:219
  25.9 34.4 %all-to-all-start = ((bf16[32,24,256]{2,1,0:T(8,128)(2,1)}), bf16[32,24,256]{2,1,0:T(8,128)(2,1)S(1)}, u32[]{:S(2)}, u32[]{:S(2)}) async-start(bf16[32,24,256]{2,1,0:T(8,128)(2,1)} %bitcast.1), calls=%async_computation | async-start | bytes 786432 | tf_op jit(solution)/shard_map/dispatch/all_to_all | solution.py:242
  35.8 18.9 %collective-permute-start.3 = (bf16[3,128,768]{2,1,0:T(8,128)(2,1)S(1)}, bf16[3,128,768]{2,1,0:T(8,128)(2,1)S(1)}, u32[]{:S(2)}, u32[]{:S(2)}) collective-permute-start(bf16[3,128,768]{2,1,0:T(8,128)(2,1)S(1)} %pad_maximum_fusion.w0), channel_id=1, source_target_pairs={{0,512},{512,0},{1,513},{513,1},{2,514},{514,2},{3,515},{515,3},{4... | collective-permute-start | bytes 1769480 | tf_op jit(solution)/shard_map/weights_to_quad/ppermute | solution.py:223
  38.0 21.8 %collective-permute-start.2 = (bf16[3,128,768]{2,1,0:T(8,128)(2,1)S(1)}, bf16[3,128,768]{2,1,0:T(8,128)(2,1)S(1)}, u32[]{:S(2)}, u32[]{:S(2)}) collective-permute-start(bf16[3,128,768]{2,1,0:T(8,128)(2,1)S(1)} %pad_maximum_fusion.w0), channel_id=1, source_target_pairs={{0,32},{32,0},{1,33},{33,1},{2,34},{34,2},{3,35},{35,3},{4,36},{36... | collective-permute-start | bytes 1769480 | tf_op jit(solution)/shard_map/weights_to_quad/ppermute | solution.py:224
  54.7 5.7 %collective-permute-start.4 = (bf16[3,128,768]{2,1,0:T(8,128)(2,1)S(1)}, bf16[3,128,768]{2,1,0:T(8,128)(2,1)S(1)}, u32[]{:S(2)}, u32[]{:S(2)}) collective-permute-start(bf16[3,128,768]{2,1,0:T(8,128)(2,1)S(1)} %collective-permute-done.3.w2), channel_id=1, source_target_pairs={{0,32},{32,0},{1,33},{33,1},{2,34},{34,2},{3,35},{35,3},{4,36},{36... | collective-permute-start | bytes 1769480 | tf_op jit(solution)/shard_map/weights_to_quad/ppermute | solution.py:225
  61.9 0.9 copy-start
  62.8 0.7 copy-start.3
  63.5 0.7 copy-start.5
  64.2 28.9 %all-to-all-start.1 = ((bf16[8,24,2304]{2,1,0:T(8,128)(2,1)}), bf16[8,24,2304]{2,1,0:T(8,128)(2,1)S(1)}, u32[]{:S(2)}, u32[]{:S(2)}) async-start(bf16[8,24,2304]{2,1,0:T(8,128)(2,1)} %bitcast.31), calls=%async_computation.1 | async-start | bytes 1769472 | tf_op jit(solution)/shard_map/partial_sums/all_to_all | solution.py:256
  71.0 11.2 %collective-permute-start.5 = (f32[3,12,2048]{2,0,1:T(4,128)}, f32[3,12,2048]{2,0,1:T(4,128)}, u32[]{:S(2)}, u32[]{:S(2)}) collective-permute-start(f32[3,12,2048]{2,0,1:T(4,128)} %pad_maximum_fusion.1), channel_id=1, source_target_pairs={{0,16},{16,0},{1,17},{17,1},{2,18},{18,2},{3,19},{19,3},{4,20},{20... | collective-permute-start | bytes 884744 | tf_op jit(solution)/shard_map/partial_sums/ppermute | solution.py:257
  93.2 23.9 %copy-start.4 = (bf16[192,512]{1,0:T(8,128)(2,1)S(1)}, bf16[192,512]{1,0:T(8,128)(2,1)}, u32[]{:S(2)}) copy-start(bf16[192,512]{1,0:T(8,128)(2,1)} %copy-done.3) | copy-start | bytes 589828
  93.2 23.9 %copy-start.6 = (bf16[192,512]{1,0:T(8,128)(2,1)S(1)}, bf16[192,512]{1,0:T(8,128)(2,1)}, u32[]{:S(2)}) copy-start(bf16[192,512]{1,0:T(8,128)(2,1)} %copy-done.5) | copy-start | bytes 589828
  114.3 30.7 %copy-start.8 = (f32[3,12,2048]{2,0,1:T(4,128)S(1)}, f32[3,12,2048]{2,0,1:T(4,128)}, u32[]{:S(2)}) copy-start(f32[3,12,2048]{2,0,1:T(4,128)} %pad_maximum_fusion.1) | copy-start | bytes 884740
  119.0 26.9 %collective-permute-start.6 = (bf16[2,3,128,768]{3,2,1,0:T(8,128)(2,1)}, bf16[2,3,128,768]{3,2,1,0:T(8,128)(2,1)}, u32[]{:S(2)}, u32[]{:S(2)}) collective-permute-start(bf16[2,3,128,768]{3,2,1,0:T(8,128)(2,1)} %get-tuple-element.32), channel_id=1, source_target_pairs={{0,32},{32,0},{1,33},{33,1},{2,34},{34,2},{3,35},{35,3},{4,36},{36... | collective-permute-start | bytes 3538952 | tf_op jit(solution)/shard_map/weight_grads/ppermute | solution.py:285
  130.7 41.1 %all-to-all-start.2 = ((bf16[32,24,256]{2,1,0:T(8,128)(2,1)}), bf16[32,24,256]{2,1,0:T(8,128)(2,1)S(1)}, u32[]{:S(2)}, u32[]{:S(2)}) async-start(bf16[32,24,256]{2,1,0:T(8,128)(2,1)} %bitcast.8), calls=%async_computation.2 | async-start | bytes 786432 | tf_op jit(solution)/shard_map/slot_outputs/all_to_all | solution.py:275
  147.4 1.4 copy-start.7
  147.4 30.0 %copy-start.9 = (f32[3,12,2048]{2,0,1:T(4,128)S(1)}, f32[3,12,2048]{2,0,1:T(4,128)}, u32[]{:S(2)}) copy-start(f32[3,12,2048]{2,0,1:T(4,128)} %broadcast_select_fusion) | copy-start | bytes 884740
  148.8 32.8 %collective-permute-start.7 = (bf16[3,128,768]{2,1,0:T(8,128)(2,1)S(1)}, bf16[3,128,768]{2,1,0:T(8,128)(2,1)S(1)}, u32[]{:S(2)}, u32[]{:S(2)}) collective-permute-start(bf16[3,128,768]{2,1,0:T(8,128)(2,1)S(1)} %fusion.2), channel_id=1, source_target_pairs={{0,512},{512,0},{1,513},{513,1},{2,514},{514,2},{3,515},{515,3},{4... | collective-permute-start | bytes 1769480 | tf_op jit(solution)/shard_map/weight_grads/ppermute | solution.py:286
  173.1 7.9 %all-to-all-start.3 = ((bf16[4,64,256]{2,1,0:T(8,128)(2,1)}), bf16[4,64,256]{2,1,0:T(8,128)(2,1)S(1)}, u32[]{:S(2)}, u32[]{:S(2)}) async-start(bf16[4,64,256]{2,1,0:T(8,128)(2,1)} %combine.1), calls=%async_computation.3 | async-start | bytes 262144 | tf_op jit(solution)/shard_map/combine/all_to_all | solution.py:297

commit v3 on v2

--- a/solution.py
+++ b/solution.py
@@ -9,8 +9,9 @@
 from jax.sharding import PartitionSpec as P
 
 EXPERT = ("x_hi", "z")
-DP = ("x_lo", "y", "core")
-QUAD = ("x_lo", "core")
+DP = ("x_lo", "y1", "y0", "core")
+QUAD = ("y0", "core")
+SUMS = ("x_lo", "y1")
 F32 = jnp.float32
 BF16 = jnp.bfloat16
 SWAP = [(0, 1), (1, 0)]
@@ -25,8 +26,9 @@
 BLK = 128
 FF = 768
 Y = 8
-
-PARAMS = pltpu.CompilerParams(vmem_limit_bytes=48 * 1024 * 1024)
+NEXT = 192
+
+PARAMS = pltpu.CompilerParams(vmem_limit_bytes=16 * 1024 * 1024)
 
 
 def call(kernel, out_shape, operands, flops=0, moved=0):
@@ -36,7 +38,7 @@
         kernel,
         out_shape=out_shape,
         in_specs=[smem if o.dtype == jnp.int32 and o.size == 1 else vmem for o in operands],
-        out_specs=jax.tree.map(lambda _: vmem, out_shape),
+        out_specs=jax.tree.map(lambda _: vmem, out_shape, is_leaf=lambda o: hasattr(o, "shape")),
         compiler_params=PARAMS,
         cost_estimate=pl.CostEstimate(flops=flops, bytes_accessed=moved, transcendentals=0),
     )(*operands)
@@ -66,7 +68,7 @@
     out_ref[:, BLK:] = b_ref[...]
 
 
-def table_kernel(q_ref, routes_ref, probs_ref, mask_ref, prob_ref):
+def table_kernel(q_ref, routes_ref, probs_ref, mask_ref, prob_ref, mask_again, prob_again):
     q = q_ref[0]
     shape = (TOK, WIDE)
     pair, member, slot = row_fields(shape, 1)
@@ -85,6 +87,8 @@
     prob = jnp.where(here, weight, 0.0)
     mask_ref[...] = mask.astype(BF16)
     prob_ref[...] = prob
+    mask_again[...] = mask.astype(BF16)
+    prob_again[...] = prob
 
 
 def dispatch_kernel(mask_ref, prob_ref, near_ref, far_ref, pay_ref):
@@ -177,6 +181,12 @@
                 keep_ref[d // 2, k] = part
 
 
+def add_near_kernel(keep_ref, near_ref, kept_ref, passed_ref):
+    for k in range(3):
+        kept_ref[k] = keep_ref[0, k] + near_ref[0, k].astype(F32)
+        passed_ref[k] = (keep_ref[1, k] + near_ref[1, k].astype(F32)).astype(BF16)
+
+
 def combine_kernel(q_ref, pay_ref, mask_ref, prob_ref, out_ref):
     q = q_ref[0]
     shape = (TOK, WIDE)
@@ -194,8 +204,24 @@
         out_ref[q ^ d] = jnp.concatenate([mixed, grad], axis=1).astype(BF16)
 
 
+def stack_kernel(a_ref, b_ref, c_ref, out_ref):
+    for k, ref in enumerate((a_ref, b_ref, c_ref)):
+        out_ref[k * NEXT : (k + 1) * NEXT] = ref[...]
+
+
+def select_kernel(moving_ref, partner_ref, state_ref, a_ref, b_ref, c_ref):
+    moving = moving_ref[0] != 0
+    for k, ref in enumerate((a_ref, b_ref, c_ref)):
+        rows = slice(k * NEXT, (k + 1) * NEXT)
+        ref[...] = jnp.where(moving, partner_ref[rows], state_ref[rows])
+
+
 def shape_of(*dims, dtype=BF16):
     return jax.ShapeDtypeStruct(dims, dtype)
+
+
+def far_shape(*dims, dtype=BF16):
+    return pltpu.HBM(dims, dtype)
 
 
 def shards(
@@ -211,23 +237,28 @@
     next_first,
     next_second,
 ):
-    quad = (lax.axis_index("x_lo") * 2 + lax.axis_index("core")).astype(jnp.int32).reshape(1)
+    quad = (lax.axis_index("y0") * 2 + lax.axis_index("core")).astype(jnp.int32).reshape(1)
 
     with jax.named_scope("tokens_to_quad"):
         mine = call(join_kernel, shape_of(TOK, 2 * BLK), (tokens, grad_out), moved=65536)
         near = jnp.concatenate([mine, lax.ppermute(mine, "core", SWAP)], axis=0)
-        far = lax.ppermute(near, "x_lo", SWAP)
+        far = lax.ppermute(near, "y0", SWAP)
 
     with jax.named_scope("weights_to_quad"):
         w0 = jnp.stack([w_gate[0], w_up[0], w_down[0].T])
-        w2 = lax.ppermute(w0, "x_lo", SWAP)
+        w2 = lax.ppermute(w0, "y0", SWAP)
         w1 = lax.ppermute(w0, "core", SWAP)
         w3 = lax.ppermute(w2, "core", SWAP)
 
     with jax.named_scope("dispatch"):
-        mask, prob = call(
+        mask, prob, mask_again, prob_again = call(
             table_kernel,
-            (shape_of(TOK, WIDE), shape_of(TOK, WIDE, dtype=F32)),
+            (
+                shape_of(TOK, WIDE),
+                shape_of(TOK, WIDE, dtype=F32),
+                far_shape(TOK, WIDE),
+                far_shape(TOK, WIDE, dtype=F32),
+            ),
             (quad, routes, gate_probs),
             flops=2 * TOK * TOK * WIDE,
             moved=300000,
@@ -242,18 +273,19 @@
         got = lax.all_to_all(pay, EXPERT, split_axis=0, concat_axis=0, tiled=True)
 
     with jax.named_scope("relocate"):
-        state = jnp.concatenate([next_master, next_first, next_second], axis=0)
+        mine_next = [v.reshape(NEXT, BLK) for v in (next_master, next_first, next_second)]
+        state = call(stack_kernel, shape_of(3 * NEXT, BLK, dtype=F32), mine_next, moved=600000)
 
     with jax.named_scope("partial_sums"):
         sums, x_rows, dy_rows = call(
             partial_kernel,
-            (shape_of(ROWS, 3 * FF), shape_of(ROWS, 4 * BLK), shape_of(ROWS, 4 * BLK)),
+            (far_shape(ROWS, 3 * FF), far_shape(ROWS, 4 * BLK), far_shape(ROWS, 4 * BLK)),
             (got, w0, w1, w2, w3),
             flops=2 * 3 * ROWS * FF * 4 * BLK,
             moved=4000000,
         )
         sums, state = lax.optimization_barrier((sums, state))
-        parts = lax.all_to_all(sums, "y", split_axis=0, concat_axis=0, tiled=True)
+        parts = lax.all_to_all(sums, SUMS, split_axis=0, concat_axis=0, tiled=True)
         partner = lax.ppermute(state, "x_hi", SWAP)
         parts, partner = lax.optimization_barrier((parts, partner))
 
@@ -261,12 +293,12 @@
         hidden = call(
             act_kernel, shape_of(ROWS // Y, 3 * FF), (parts,), flops=4000000, moved=1000000
         )
-        whole = lax.all_gather(hidden, "y", axis=0, tiled=True)
+        whole = lax.all_gather(hidden, SUMS, axis=0, tiled=True)
 
     with jax.named_scope("slot_outputs"):
         back = call(
             back_kernel,
-            shape_of(WIDE, 2 * BLK),
+            far_shape(WIDE, 2 * BLK),
             (whole, w0, w1, w2, w3),
             flops=2 * 3 * ROWS * FF * 4 * BLK,
             moved=4000000,
@@ -279,18 +311,23 @@
             grad_kernel,
             (shape_of(2, 3, BLK, FF, dtype=F32), shape_of(2, 3, BLK, FF)),
             (whole, x_rows, dy_rows),
-            flops=2 * 3 * ROWS * FF * 4 * BLK,
-            moved=6000000,
-        )
-        pair = keep + lax.ppermute(send, "core", SWAP).astype(F32)
-        other = lax.ppermute(pair[1].astype(BF16), "x_lo", SWAP)
-        grads = (pair[0] + other.astype(F32)).astype(BF16)
+            flops=40 * 3 * ROWS * FF * 4 * BLK,
+            moved=100000000,
+        )
+        near_part = lax.ppermute(send, "core", SWAP)
+        kept, passed = call(
+            add_near_kernel,
+            (shape_of(3, BLK, FF, dtype=F32), shape_of(3, BLK, FF)),
+            (keep, near_part),
+        )
+        other = lax.ppermute(passed, "y0", SWAP)
+        grads = (kept + other.astype(F32)).astype(BF16)
 
     with jax.named_scope("combine"):
         mixes = call(
             combine_kernel,
             shape_of(QUADS, TOK, 2 * BLK),
-            (quad, returned, mask, prob),
+            (quad, returned, mask_again, prob_again),
             flops=2 * 16 * TOK * WIDE * BLK,
             moved=800000,
         )
@@ -298,9 +335,14 @@
         mixes = jnp.sum(mixes.astype(F32), axis=0).astype(BF16)
 
     with jax.named_scope("relocate"):
-        place_index = lax.axis_index(EXPERT).astype(jnp.int32)
-        moving = dest[0] != place_index
-        moved = jnp.where(moving, partner, state)
+        moving = (dest != lax.axis_index(EXPERT).astype(jnp.int32)).astype(jnp.int32)
+        moved = call(
+            select_kernel,
+            [shape_of(NEXT, BLK, dtype=F32)] * 3,
+            (moving, partner, state),
+            moved=1200000,
+        )
+        moved = [v.reshape(next_master.shape) for v in moved]
 
     return (
         mixes[:, :BLK],
@@ -308,15 +350,15 @@
         grads[0][None],
         grads[1][None],
         grads[2].T[None],
-        moved[0:1],
-        moved[1:2],
-        moved[2:3],
+        moved[0],
+        moved[1],
+        moved[2],
     )
 
 
 def solution(mesh):
     fine = Mesh(
-        mesh.devices.reshape(2, 8, 2, 2, 16), ("x_lo", "y", "core", "x_hi", "z")
+        mesh.devices.reshape(2, 4, 2, 2, 2, 16), ("x_lo", "y1", "y0", "core", "x_hi", "z")
     )
     return jax.shard_map(
         shards,

time: 186 us -> 179 us (0.962)
  waiting for transfers between devices: 56.1 us -> 34.1 us
  blocking collectives: 21.1 us -> 32.4 us
  starting transfers between devices: 80.4 us -> 89.9 us
  other arithmetic: 4.9 us -> 1.27 us
  local copies, waits for them, and re-layouts: 10.9 us -> 7.92 us
    all_to_all x1, waiting for transfers between devices: 20.8 us -> 0.01 us  [shards(): lax.all_to_all(back, EXPERT, split_axis=0, concat_axis=0, tiled=True)]
    all_gather x1, blocking collectives: 21.1 us -> 32.4 us  [shards(): whole = lax.all_gather(hidden, SUMS, axis=0, tiled=True)]
    all_to_all x1, starting transfers between devices: 4.34 us -> 14.5 us  [shards(): mixes = lax.all_to_all(mixes, QUAD, split_axis=0, concat_axis=0, tiled=True)]
    all_to_all x1, waiting for transfers between devices: 10.9 us -> 0.95 us  [shards(): parts = lax.all_to_all(sums, SUMS, split_axis=0, concat_axis=0, tiled=True)]
    all_to_all x1, waiting for transfers between devices: 0.01 us -> 5.17 us  [shards(): got = lax.all_to_all(pay, EXPERT, split_axis=0, concat_axis=0, tiled=True)]
    ppermute x4, starting transfers between devices: 18 us -> 23 us  [the longest x1 10.6 us: shards(): near_part = lax.ppermute(send, 'core', SWAP)]
    ppermute x1, waiting for transfers between devices: 6.51 us -> 11 us  [shards(): partner = lax.ppermute(state, 'x_hi', SWAP)]
    all_to_all x1, starting transfers between devices: 13.6 us -> 11.2 us  [shards(): lax.all_to_all(back, EXPERT, split_axis=0, concat_axis=0, tiled=True)]
  transfers between devices with their start and end apart: 12 -> 12, of which waited for: 8 -> 9; matrix products, arithmetic and copies ran while one was open for 4% -> 1% of each run, Pallas kernels for 1% -> 2%
where the time goes in v3:
time: 179 us; the launch traced here: 178 us
  starting transfers between devices  89.9 us (50%)
  waiting for transfers between devices  34.1 us (19%)
  blocking collectives  32.4 us (18%)
  Pallas kernels  11.3 us (6%)
  local copies, waits for them, and re-layouts  7.92 us (4%)
    all_gather x1, blocking collectives, shards(): whole = lax.all_gather(hidden, SUMS, axis=0, tiled=True)  32.4 us
    ppermute x1, starting transfers between devices, shards(): near = jnp.concatenate([mine, lax.ppermute(mine, 'core', SWAP)], axis=0)  16.2 us
    all_to_all x1, starting transfers between devices, shards(): mixes = lax.all_to_all(mixes, QUAD, split_axis=0, concat_axis=0, tiled=True)  14.5 us
    pallas_call x11, Pallas kernels, call(): pl.pallas_call(kernel, out_shape=out_shape, in_specs=[smem if o.dtype ==...  11.3 us
    all_to_all x1, starting transfers between devices, shards(): lax.all_to_all(back, EXPERT, split_axis=0, concat_axis=0, tiled=True)  11.2 us
    ppermute x1, waiting for transfers between devices, shards(): partner = lax.ppermute(state, 'x_hi', SWAP)  11 us
    ppermute x1, starting transfers between devices, shards(): near_part = lax.ppermute(send, 'core', SWAP)  10.6 us
    all_to_all x1, starting transfers between devices, shards(): got = lax.all_to_all(pay, EXPERT, split_axis=0, concat_axis=0, tiled=True)  9.67 us
  transfers between devices with their start and end apart: 12, of which 9 were waited for; matrix products, arithmetic and copies ran while one was open for 1% of the time, Pallas kernels for 2%

profile of v3, /device:TPU:1, one launch (start us, length us, event | category | flops | bytes accessed | tf_op | source)
XLA Modules:
  0.0 178.4 jit_solution(10188951608295003319)
XLA Ops:
  0.6 0.0 copy-start.7
  0.6 0.7 copy-done.7
  1.4 0.0 copy-start.8
  1.4 0.7 copy-done.8
  2.1 0.0 copy-start.13
  2.1 0.0 copy-start.11
  2.1 0.0 copy-start.12
  2.1 16.2 %collective-permute-start = (bf16[64,256]{1,0:T(8,128)(2,1)S(1)}, bf16[64,256]{1,0:T(8,128)(2,1)S(1)}, u32[]{:S(2)}, u32[]{:S(2)}) collective-permute-start(bf16[64,256]{1,0:T(8,128)(2,1)S(1)} %tokens_to_quad.1), channel_id=1, source_target_pairs={{0,32},{32,0},{1,33},{33,1},{2,34},{34,2},{3,35},{35,3},{4,36},{36... | collective-permute-start | bytes 98312 | tf_op jit(solution)/shard_map/tokens_to_quad/ppermute | solution.py:244
  18.3 0.8 collective-permute-done
  19.1 1.9 %collective-permute-start.1 = (bf16[128,256]{1,0:T(8,128)(2,1)S(1)}, bf16[128,256]{1,0:T(8,128)(2,1)S(1)}, u32[]{:S(2)}, u32[]{:S(2)}) collective-permute-start(bf16[128,256]{1,0:T(8,128)(2,1)S(1)} %pad_maximum_fusion.1.near_ref), channel_id=1, source_target_pairs={{0,64},{64,0},{1,65},{65,1},{2,66},{66,2},{3,67},{67,3},{4,68},{68... | collective-permute-start | bytes 196616 | tf_op jit(solution)/shard_map/tokens_to_quad/ppermute | solution.py:245
  21.1 0.8 copy.26.routes_ref
  21.8 0.8 copy.27.probs_ref
  22.6 1.1 dispatch.2
  23.7 0.4 collective-permute-done.1.far_ref
  24.1 1.8 %dispatch.3 = bf16[768,256]{1,0:T(8,128)(2,1)} custom-call(bf16[64,768]{1,0:T(8,128)(2,1)S(1)} %get-tuple-element.28.mask_ref, f32[64,768]{1,0:T(8,128)S(1)} %get-tuple-element.29.prob_ref, bf16[128,256]{1,0:T(8,128)(2,1)S(1)} %pad_maximum_fusion.1.near_ref, bf16[128,256]{1,0:T(8,128)(2,1)S(1)} %collective-permute-done.1.far_ref), custom_call_target="tpu_custom_call" | custom-call | flops 201326592 | bytes 800000 | tf_op jit(solution)/shard_map/dispatch/pallas_call | solution.py:37
  25.9 0.0 copy-start.3
  25.9 9.7 %all-to-all-start = ((bf16[32,24,256]{2,1,0:T(8,128)(2,1)}), bf16[32,24,256]{2,1,0:T(8,128)(2,1)S(1)}, u32[]{:S(2)}, u32[]{:S(2)}) async-start(bf16[32,24,256]{2,1,0:T(8,128)(2,1)} %bitcast.1), calls=%async_computation | async-start | bytes 786432 | tf_op jit(solution)/shard_map/dispatch/all_to_all | solution.py:273
  35.6 0.0 copy-done.13
  35.6 0.1 copy.28
  35.8 0.0 copy-done.11
  35.8 0.0 copy-done.12
  35.8 0.1 pad_maximum_fusion.w0
  35.9 2.4 %collective-permute-start.3 = (bf16[3,128,768]{2,1,0:T(8,128)(2,1)S(1)}, bf16[3,128,768]{2,1,0:T(8,128)(2,1)S(1)}, u32[]{:S(2)}, u32[]{:S(2)}) collective-permute-start(bf16[3,128,768]{2,1,0:T(8,128)(2,1)S(1)} %pad_maximum_fusion.w0), channel_id=1, source_target_pairs={{0,64},{64,0},{1,65},{65,1},{2,66},{66,2},{3,67},{67,3},{4,68},{68... | collective-permute-start | bytes 1769480 | tf_op jit(solution)/shard_map/weights_to_quad/ppermute | solution.py:249
  38.2 4.0 %collective-permute-start.2 = (bf16[3,128,768]{2,1,0:T(8,128)(2,1)S(1)}, bf16[3,128,768]{2,1,0:T(8,128)(2,1)S(1)}, u32[]{:S(2)}, u32[]{:S(2)}) collective-permute-start(bf16[3,128,768]{2,1,0:T(8,128)(2,1)S(1)} %pad_maximum_fusion.w0), channel_id=1, source_target_pairs={{0,32},{32,0},{1,33},{33,1},{2,34},{34,2},{3,35},{35,3},{4,36},{36... | collective-permute-start | bytes 1769480 | tf_op jit(solution)/shard_map/weights_to_quad/ppermute | solution.py:250
  42.2 9.5 %collective-permute-done.3.w2 = bf16[3,128,768]{2,1,0:T(8,128)(2,1)S(1)} collective-permute-done((bf16[3,128,768]{2,1,0:T(8,128)(2,1)S(1)}, bf16[3,128,768]{2,1,0:T(8,128)(2,1)S(1)}, u32[]{:S(2)}, u32[]{:S(2)}) %collective-permute-start.3) | collective-permute-done | bytes 589856 | tf_op jit(solution)/shard_map/weights_to_quad/ppermute | solution.py:249
  51.7 3.7 %collective-permute-start.4 = (bf16[3,128,768]{2,1,0:T(8,128)(2,1)S(1)}, bf16[3,128,768]{2,1,0:T(8,128)(2,1)S(1)}, u32[]{:S(2)}, u32[]{:S(2)}) collective-permute-start(bf16[3,128,768]{2,1,0:T(8,128)(2,1)S(1)} %collective-permute-done.3.w2), channel_id=1, source_target_pairs={{0,32},{32,0},{1,33},{33,1},{2,34},{34,2},{3,35},{35,3},{4,36},{36... | collective-permute-start | bytes 1769480 | tf_op jit(solution)/shard_map/weights_to_quad/ppermute | solution.py:251
  55.4 0.0 copy-done.3
  55.4 0.0 copy-done.4
  55.4 0.0 copy-done.5
  55.5 0.0 collective-permute-done.2.w1
  55.5 1.5 collective-permute-done.4.w3
  57.0 5.2 %all-to-all-done = bf16[32,24,256]{2,1,0:T(8,128)(2,1)S(1)} async-done(((bf16[32,24,256]{2,1,0:T(8,128)(2,1)}), bf16[32,24,256]{2,1,0:T(8,128)(2,1)S(1)}, u32[]{:S(2)}, u32[]{:S(2)}) %all-to-all-start) | async-done | bytes 393248 | tf_op jit(solution)/shard_map/dispatch/all_to_all | solution.py:273
  62.2 2.5 %partial_sums.1 = (bf16[192,2304]{1,0:T(8,128)(2,1)}, bf16[192,512]{1,0:T(8,128)(2,1)}, bf16[192,512]{1,0:T(8,128)(2,1)}) custom-call(bf16[768,256]{1,0:T(8,128)(2,1)S(1)} %bitcast.27, bf16[3,128,768]{2,1,0:T(8,128)(2,1)S(1)} %pad_maximum_fusion.w0, bf16[3,128,768]{2,1,0:T(8,128)(2,1)S(1)} %collective-permute-done.2.w1, ...), custom_call_target="tpu_custom_call" | custom-call | flops 452984832 | bytes 4000000 | tf_op jit(solution)/shard_map/partial_sums/pallas_call | solution.py:37
  64.6 4.7 %all-to-all-start.1 = ((bf16[8,24,2304]{2,1,0:T(8,128)(2,1)}), bf16[8,24,2304]{2,1,0:T(8,128)(2,1)S(1)}, u32[]{:S(2)}, u32[]{:S(2)}) async-start(bf16[8,24,2304]{2,1,0:T(8,128)(2,1)} %bitcast.32), calls=%async_computation.1 | async-start | bytes 1769472 | tf_op jit(solution)/shard_map/partial_sums/all_to_all | solution.py:288
  69.3 3.0 %collective-permute-start.5 = (f32[576,128]{1,0:T(8,128)S(1)}, f32[576,128]{1,0:T(8,128)S(1)}, u32[]{:S(2)}, u32[]{:S(2)}) collective-permute-start(f32[576,128]{1,0:T(8,128)S(1)} %relocate.2.state_ref), channel_id=1, source_target_pairs={{0,16},{16,0},{1,17},{17,1},{2,18},{18,2},{3,19},{19,3},{4,20},{20... | collective-permute-start | bytes 884744 | tf_op jit(solution)/shard_map/partial_sums/ppermute | solution.py:289
  72.3 11.0 %collective-permute-done.5.partner_ref = f32[576,128]{1,0:T(8,128)S(1)} collective-permute-done((f32[576,128]{1,0:T(8,128)S(1)}, f32[576,128]{1,0:T(8,128)S(1)}, u32[]{:S(2)}, u32[]{:S(2)}) %collective-permute-start.5) | collective-permute-done | bytes 294944 | tf_op jit(solution)/shard_map/partial_sums/ppermute | solution.py:289
  83.4 0.7 copy-done
  84.1 1.0 all-to-all-done.1
  85.0 0.1 activation.1
  85.2 32.4 %all_gather.3.h_ref = bf16[192,2304]{1,0:T(8,128)(2,1)S(1)} all-gather(bf16[24,2304]{1,0:T(8,128)(2,1)S(1)} %activation.1), channel_id=1, replica_groups=mesh['x_lo'=2,'y1'=4,'y0'=2,'core'=2,'x_hi'=2,'z'=16] {'x_lo','y1'}, dimensions={0}, use_global_device_ids=true | all-gather | bytes 995328 | tf_op jit(solution)/shard_map/activation/all_gather | solution.py:296
  117.6 2.8 %slot_outputs.1 = bf16[768,256]{1,0:T(8,128)(2,1)} custom-call(bf16[192,2304]{1,0:T(8,128)(2,1)S(1)} %all_gather.3.h_ref, bf16[3,128,768]{2,1,0:T(8,128)(2,1)S(1)} %pad_maximum_fusion.w0, bf16[3,128,768]{2,1,0:T(8,128)(2,1)S(1)} %collective-permute-done.2.w1, bf16[3,128,768]{2,1,0:T(8,128)(2,1)S(1)} %collective-permute-done.3.w2, ...), custom_call_target="tpu_custom_call" | custom-call | flops 452984832 | bytes 4000000 | tf_op jit(solution)/shard_map/slot_outputs/pallas_call | solution.py:37
  120.4 11.2 %all-to-all-start.2 = ((bf16[32,24,256]{2,1,0:T(8,128)(2,1)}), bf16[32,24,256]{2,1,0:T(8,128)(2,1)S(1)}, u32[]{:S(2)}, u32[]{:S(2)}) async-start(bf16[32,24,256]{2,1,0:T(8,128)(2,1)} %bitcast.31), calls=%async_computation.2 | async-start | bytes 786432 | tf_op jit(solution)/shard_map/slot_outputs/all_to_all | solution.py:307
  131.6 0.0 copy-start.9
  131.6 0.9 copy-done.9
  132.5 0.9 copy-done.10
  133.4 0.8 weight_grads.2
  134.2 10.6 %collective-permute-start.6 = (bf16[2,3,128,768]{3,2,1,0:T(8,128)(2,1)S(1)}, bf16[2,3,128,768]{3,2,1,0:T(8,128)(2,1)S(1)}, u32[]{:S(2)}, u32[]{:S(2)}) collective-permute-start(bf16[2,3,128,768]{3,2,1,0:T(8,128)(2,1)S(1)} %get-tuple-element.41), channel_id=1, source_target_pairs={{0,32},{32,0},{1,33},{33,1},{2,34},{34,2},{3,35},{35,3},{4,36},{36... | collective-permute-start | bytes 3538952 | tf_op jit(solution)/shard_map/weight_grads/ppermute | solution.py:317
  144.8 2.5 %collective-permute-done.6.near_ref = bf16[2,3,128,768]{3,2,1,0:T(8,128)(2,1)S(1)} collective-permute-done((bf16[2,3,128,768]{3,2,1,0:T(8,128)(2,1)S(1)}, bf16[2,3,128,768]{3,2,1,0:T(8,128)(2,1)S(1)}, u32[]{:S(2)}, u32[]{:S(2)}) %collective-permute-start.6) | collective-permute-done | bytes 1179680 | tf_op jit(solution)/shard_map/weight_grads/ppermute | solution.py:317
  147.3 0.2 weight_grads.3
  147.5 0.0 copy-start.1
  147.5 8.1 %collective-permute-start.7 = (bf16[3,128,768]{2,1,0:T(8,128)(2,1)S(1)}, bf16[3,128,768]{2,1,0:T(8,128)(2,1)}, u32[]{:S(2)}, u32[]{:S(2)}) collective-permute-start(bf16[3,128,768]{2,1,0:T(8,128)(2,1)S(1)} %get-tuple-element.43), channel_id=1, source_target_pairs={{0,64},{64,0},{1,65},{65,1},{2,66},{66,2},{3,67},{67,3},{4,68},{68... | collective-permute-start | bytes 1769480 | tf_op jit(solution)/shard_map/weight_grads/ppermute | solution.py:323
  155.6 0.0 all-to-all-done.2
  155.6 0.0 copy-done.2
  155.6 0.0 copy-done.6
  155.6 1.2 combine.1
  156.9 14.5 %all-to-all-start.3 = ((bf16[4,64,256]{2,1,0:T(8,128)(2,1)}), bf16[4,64,256]{2,1,0:T(8,128)(2,1)S(1)}, u32[]{:S(2)}, u32[]{:S(2)}) async-start(bf16[4,64,256]{2,1,0:T(8,128)(2,1)} %combine.1), calls=%async_computation.3 | async-start | bytes 262144 | tf_op jit(solution)/shard_map/combine/all_to_all | solution.py:334
  172.0 0.0 copy-done.1
  172.0 0.7 relocate.3
  172.8 2.2 %all-to-all-done.3 = bf16[4,64,256]{2,1,0:T(8,128)(2,1)S(1)} async-done(((bf16[4,64,256]{2,1,0:T(8,128)(2,1)}), bf16[4,64,256]{2,1,0:T(8,128)(2,1)S(1)}, u32[]{:S(2)}, u32[]{:S(2)}) %all-to-all-start.3) | async-done | bytes 131104 | tf_op jit(solution)/shard_map/combine/all_to_all | solution.py:334
  175.0 0.6 fusion
  175.6 0.0 collective-permute-done.7
  175.6 1.2 add_convert_fusion
  176.8 0.8 slice_bitcast_fusion
  177.6 0.8 copy.29
  (10 shorter events, 0.1 us)
Async XLA Ops:
  0.6 0.7 copy-start.7
  1.4 0.7 copy-start.8
  2.1 33.5 %copy-start.13 = (bf16[1,768,128]{2,1,0:T(8,128)(2,1)S(1)}, bf16[1,768,128]{2,1,0:T(8,128)(2,1)}, u32[]{:S(2)}) copy-start(bf16[1,768,128]{2,1,0:T(8,128)(2,1)} %param.17) | copy-start | bytes 589828
  2.1 33.7 %copy-start.11 = (bf16[1,128,768]{2,1,0:T(8,128)(2,1)S(1)}, bf16[1,128,768]{2,1,0:T(8,128)(2,1)}, u32[]{:S(2)}) copy-start(bf16[1,128,768]{2,1,0:T(8,128)(2,1)} %param.16) | copy-start | bytes 589828
  2.1 33.7 %copy-start.12 = (bf16[1,128,768]{2,1,0:T(8,128)(2,1)S(1)}, bf16[1,128,768]{2,1,0:T(8,128)(2,1)}, u32[]{:S(2)}) copy-start(bf16[1,128,768]{2,1,0:T(8,128)(2,1)} %param.15) | copy-start | bytes 589828
  2.1 17.0 %collective-permute-start = (bf16[64,256]{1,0:T(8,128)(2,1)S(1)}, bf16[64,256]{1,0:T(8,128)(2,1)S(1)}, u32[]{:S(2)}, u32[]{:S(2)}) collective-permute-start(bf16[64,256]{1,0:T(8,128)(2,1)S(1)} %tokens_to_quad.1), channel_id=1, source_target_pairs={{0,32},{32,0},{1,33},{33,1},{2,34},{34,2},{3,35},{35,3},{4,36},{36... | collective-permute-start | bytes 98312 | tf_op jit(solution)/shard_map/tokens_to_quad/ppermute | solution.py:244
  19.1 5.0 %collective-permute-start.1 = (bf16[128,256]{1,0:T(8,128)(2,1)S(1)}, bf16[128,256]{1,0:T(8,128)(2,1)S(1)}, u32[]{:S(2)}, u32[]{:S(2)}) collective-permute-start(bf16[128,256]{1,0:T(8,128)(2,1)S(1)} %pad_maximum_fusion.1.near_ref), channel_id=1, source_target_pairs={{0,64},{64,0},{1,65},{65,1},{2,66},{66,2},{3,67},{67,3},{4,68},{68... | collective-permute-start | bytes 196616 | tf_op jit(solution)/shard_map/tokens_to_quad/ppermute | solution.py:245
  25.9 29.5 %copy-start.3 = (f32[1,12,2048]{2,0,1:T(1,128)S(1)}, f32[1,12,2048]{2,0,1:T(1,128)}, u32[]{:S(2)}) copy-start(f32[1,12,2048]{2,0,1:T(1,128)} %param.19) | copy-start | bytes 294916
  25.9 29.5 %copy-start.4 = (f32[1,12,2048]{2,0,1:T(1,128)S(1)}, f32[1,12,2048]{2,0,1:T(1,128)}, u32[]{:S(2)}) copy-start(f32[1,12,2048]{2,0,1:T(1,128)} %param.20) | copy-start | bytes 294916
  25.9 29.5 %copy-start.5 = (f32[1,12,2048]{2,0,1:T(1,128)S(1)}, f32[1,12,2048]{2,0,1:T(1,128)}, u32[]{:S(2)}) copy-start(f32[1,12,2048]{2,0,1:T(1,128)} %param.21) | copy-start | bytes 294916
  25.9 36.3 %all-to-all-start = ((bf16[32,24,256]{2,1,0:T(8,128)(2,1)}), bf16[32,24,256]{2,1,0:T(8,128)(2,1)S(1)}, u32[]{:S(2)}, u32[]{:S(2)}) async-start(bf16[32,24,256]{2,1,0:T(8,128)(2,1)} %bitcast.1), calls=%async_computation | async-start | bytes 786432 | tf_op jit(solution)/shard_map/dispatch/all_to_all | solution.py:273
  35.9 15.8 %collective-permute-start.3 = (bf16[3,128,768]{2,1,0:T(8,128)(2,1)S(1)}, bf16[3,128,768]{2,1,0:T(8,128)(2,1)S(1)}, u32[]{:S(2)}, u32[]{:S(2)}) collective-permute-start(bf16[3,128,768]{2,1,0:T(8,128)(2,1)S(1)} %pad_maximum_fusion.w0), channel_id=1, source_target_pairs={{0,64},{64,0},{1,65},{65,1},{2,66},{66,2},{3,67},{67,3},{4,68},{68... | collective-permute-start | bytes 1769480 | tf_op jit(solution)/shard_map/weights_to_quad/ppermute | solution.py:249
  38.2 17.2 %collective-permute-start.2 = (bf16[3,128,768]{2,1,0:T(8,128)(2,1)S(1)}, bf16[3,128,768]{2,1,0:T(8,128)(2,1)S(1)}, u32[]{:S(2)}, u32[]{:S(2)}) collective-permute-start(bf16[3,128,768]{2,1,0:T(8,128)(2,1)S(1)} %pad_maximum_fusion.w0), channel_id=1, source_target_pairs={{0,32},{32,0},{1,33},{33,1},{2,34},{34,2},{3,35},{35,3},{4,36},{36... | collective-permute-start | bytes 1769480 | tf_op jit(solution)/shard_map/weights_to_quad/ppermute | solution.py:250
  51.7 5.3 %collective-permute-start.4 = (bf16[3,128,768]{2,1,0:T(8,128)(2,1)S(1)}, bf16[3,128,768]{2,1,0:T(8,128)(2,1)S(1)}, u32[]{:S(2)}, u32[]{:S(2)}) collective-permute-start(bf16[3,128,768]{2,1,0:T(8,128)(2,1)S(1)} %collective-permute-done.3.w2), channel_id=1, source_target_pairs={{0,32},{32,0},{1,33},{33,1},{2,34},{34,2},{3,35},{35,3},{4,36},{36... | collective-permute-start | bytes 1769480 | tf_op jit(solution)/shard_map/weights_to_quad/ppermute | solution.py:251
  64.6 20.4 %all-to-all-start.1 = ((bf16[8,24,2304]{2,1,0:T(8,128)(2,1)}), bf16[8,24,2304]{2,1,0:T(8,128)(2,1)S(1)}, u32[]{:S(2)}, u32[]{:S(2)}) async-start(bf16[8,24,2304]{2,1,0:T(8,128)(2,1)} %bitcast.32), calls=%async_computation.1 | async-start | bytes 1769472 | tf_op jit(solution)/shard_map/partial_sums/all_to_all | solution.py:288
  69.3 14.0 %collective-permute-start.5 = (f32[576,128]{1,0:T(8,128)S(1)}, f32[576,128]{1,0:T(8,128)S(1)}, u32[]{:S(2)}, u32[]{:S(2)}) collective-permute-start(f32[576,128]{1,0:T(8,128)S(1)} %relocate.2.state_ref), channel_id=1, source_target_pairs={{0,16},{16,0},{1,17},{17,1},{2,18},{18,2},{3,19},{19,3},{4,20},{20... | collective-permute-start | bytes 884744 | tf_op jit(solution)/shard_map/partial_sums/ppermute | solution.py:289
  83.4 0.7 copy-start
  120.4 35.2 %all-to-all-start.2 = ((bf16[32,24,256]{2,1,0:T(8,128)(2,1)}), bf16[32,24,256]{2,1,0:T(8,128)(2,1)S(1)}, u32[]{:S(2)}, u32[]{:S(2)}) async-start(bf16[32,24,256]{2,1,0:T(8,128)(2,1)} %bitcast.31), calls=%async_computation.2 | async-start | bytes 786432 | tf_op jit(solution)/shard_map/slot_outputs/all_to_all | solution.py:307
  131.6 0.9 copy-start.9
  132.5 0.9 copy-start.10
  134.2 13.0 %collective-permute-start.6 = (bf16[2,3,128,768]{3,2,1,0:T(8,128)(2,1)S(1)}, bf16[2,3,128,768]{3,2,1,0:T(8,128)(2,1)S(1)}, u32[]{:S(2)}, u32[]{:S(2)}) collective-permute-start(bf16[2,3,128,768]{3,2,1,0:T(8,128)(2,1)S(1)} %get-tuple-element.41), channel_id=1, source_target_pairs={{0,32},{32,0},{1,33},{33,1},{2,34},{34,2},{3,35},{35,3},{4,36},{36... | collective-permute-start | bytes 3538952 | tf_op jit(solution)/shard_map/weight_grads/ppermute | solution.py:317
  147.3 8.3 %copy-start.2 = (f32[64,768]{1,0:T(8,128)S(1)}, f32[64,768]{1,0:T(8,128)}, u32[]{:S(2)}) copy-start(f32[64,768]{1,0:T(8,128)} %get-tuple-element.36.prob_ref) | copy-start | bytes 589828
  147.3 8.3 %copy-start.6 = (bf16[64,768]{1,0:T(8,128)(2,1)S(1)}, bf16[64,768]{1,0:T(8,128)(2,1)}, u32[]{:S(2)}) copy-start(bf16[64,768]{1,0:T(8,128)(2,1)} %get-tuple-element.35.mask_ref) | copy-start | bytes 294916
  147.5 24.6 %copy-start.1 = (f32[576,128]{1,0:T(8,128)S(1)}, f32[576,128]{1,0:T(8,128)}, u32[]{:S(2)}) copy-start(f32[576,128]{1,0:T(8,128)} %copy-done) | copy-start | bytes 884740
  147.5 28.1 %collective-permute-start.7 = (bf16[3,128,768]{2,1,0:T(8,128)(2,1)S(1)}, bf16[3,128,768]{2,1,0:T(8,128)(2,1)}, u32[]{:S(2)}, u32[]{:S(2)}) collective-permute-start(bf16[3,128,768]{2,1,0:T(8,128)(2,1)S(1)} %get-tuple-element.43), channel_id=1, source_target_pairs={{0,64},{64,0},{1,65},{65,1},{2,66},{66,2},{3,67},{67,3},{4,68},{68... | collective-permute-start | bytes 1769480 | tf_op jit(solution)/shard_map/weight_grads/ppermute | solution.py:323
  156.9 18.1 %all-to-all-start.3 = ((bf16[4,64,256]{2,1,0:T(8,128)(2,1)}), bf16[4,64,256]{2,1,0:T(8,128)(2,1)S(1)}, u32[]{:S(2)}, u32[]{:S(2)}) async-start(bf16[4,64,256]{2,1,0:T(8,128)(2,1)} %combine.1), calls=%async_computation.3 | async-start | bytes 262144 | tf_op jit(solution)/shard_map/combine/all_to_all | solution.py:334

commit v4 on v3

--- a/solution.py
+++ b/solution.py
@@ -63,9 +63,28 @@
     return lax.dot_general(a, b, (dims, ((), ())), preferred_element_type=F32)
 
 
-def join_kernel(a_ref, b_ref, out_ref):
-    out_ref[:, :BLK] = a_ref[...]
-    out_ref[:, BLK:] = b_ref[...]
+def join_kernel(a_ref, b_ref, out_ref, sem_a, sem_b):
+    copies = [
+        pltpu.make_async_copy(a_ref, out_ref.at[:, :BLK], sem_a),
+        pltpu.make_async_copy(b_ref, out_ref.at[:, BLK:], sem_b),
+    ]
+    for copy in copies:
+        copy.start()
+    for copy in copies:
+        copy.wait()
+
+
+def join(a, b):
+    hbm = pl.BlockSpec(memory_space=pltpu.HBM)
+    return pl.pallas_call(
+        join_kernel,
+        out_shape=shape_of(TOK, 2 * BLK),
+        in_specs=[hbm, hbm],
+        out_specs=pl.BlockSpec(memory_space=pltpu.VMEM),
+        scratch_shapes=[pltpu.SemaphoreType.DMA, pltpu.SemaphoreType.DMA],
+        compiler_params=PARAMS,
+        cost_estimate=pl.CostEstimate(flops=0, bytes_accessed=65536, transcendentals=0),
+    )(*[pltpu.with_memory_space_constraint(v, pltpu.HBM) for v in (a, b)])
 
 
 def table_kernel(q_ref, routes_ref, probs_ref, mask_ref, prob_ref, mask_again, prob_again):
@@ -74,12 +93,17 @@
     pair, member, slot = row_fields(shape, 1)
     chosen = jnp.zeros(shape, F32)
     weight = jnp.zeros(shape, F32)
-    for k in range(TOP):
-        hit = routes_ref[:, k : k + 1] == pair
-        chosen = jnp.where(hit, 1.0, chosen)
-        weight = jnp.where(hit, probs_ref[:, k : k + 1], weight)
+    expert = pair.astype(F32)
     row = lax.broadcasted_iota(jnp.int32, (TOK, TOK), 0)
     col = lax.broadcasted_iota(jnp.int32, (TOK, TOK), 1)
+    unit = jnp.where(col == row, 1.0, 0.0).astype(BF16)
+    routes = dot(unit, routes_ref[...].astype(F32).astype(BF16), ((1,), (1,)))
+    hi, mid, low = [dot(unit, part, ((1,), (1,))) for part in three(probs_ref[...])]
+    probs = (hi + mid) + low
+    for k in range(TOP):
+        hit = routes[:, k : k + 1] == expert
+        chosen = jnp.where(hit, 1.0, chosen)
+        weight = jnp.where(hit, probs[:, k : k + 1], weight)
     before = jnp.where(col < row, 1.0, 0.0).astype(BF16)
     position = dot(before, chosen.astype(BF16), ((1,), (0,)))
     here = (chosen > 0.5) & (position == (q * PART + slot).astype(F32))
@@ -147,11 +171,18 @@
             vals.append(total)
         gate, up, back = vals
         s = jax.nn.sigmoid(gate)
-        out_ref[:, lo : lo + 256] = (gate * s * up).astype(BF16)
-        out_ref[:, FF + lo : FF + lo + 256] = (
-            back * up * s * (1.0 + gate * (1.0 - s))
-        ).astype(BF16)
-        out_ref[:, 2 * FF + lo : 2 * FF + lo + 256] = (back * gate * s).astype(BF16)
+        act = gate * s * up
+        grad_g = back * up * s * (1.0 + gate * (1.0 - s))
+        grad_u = back * gate * s
+        for k, value in enumerate((act, grad_g, grad_u)):
+            at = slice(k * FF + lo, k * FF + lo + 256)
+            out_ref[:, at] = jnp.concatenate([value] * Y, axis=0).astype(BF16)
+
+
+def place_back(d):
+    pair, member, slot = row_fields((WIDE, ROWS), 0)
+    col = lax.broadcasted_iota(jnp.int32, (WIDE, ROWS), 1)
+    return jnp.where((member == d) & (col == pair * PART + slot), 1.0, 0.0).astype(BF16)
 
 
 def back_kernel(h_ref, w0, w1, w2, w3, pay_ref):
@@ -163,7 +194,7 @@
         y = dot(act, w[2], ((1,), (1,)))
         dx = dot(grad_g, w[0], ((1,), (1,))) + dot(grad_u, w[1], ((1,), (1,)))
         both = jnp.concatenate([y.astype(BF16), dx.astype(BF16)], axis=1)
-        total = total + dot(place(d), both, ((0,), (0,)))
+        total = total + dot(place_back(d), both, ((1,), (0,)))
     pay_ref[...] = total.astype(BF16)
 
 
@@ -185,6 +216,20 @@
     for k in range(3):
         kept_ref[k] = keep_ref[0, k] + near_ref[0, k].astype(F32)
         passed_ref[k] = (keep_ref[1, k] + near_ref[1, k].astype(F32)).astype(BF16)
+
+
+def add_far_kernel(kept_ref, other_ref, gate_ref, up_ref, down_ref):
+    gate_ref[...] = (kept_ref[0] + other_ref[0].astype(F32)).astype(BF16)
+    up_ref[...] = (kept_ref[1] + other_ref[1].astype(F32)).astype(BF16)
+    down_ref[...] = (kept_ref[2] + other_ref[2].astype(F32)).T.astype(BF16)
+
+
+def mix_kernel(in_ref, mixed_ref, grad_ref):
+    total = in_ref[0].astype(F32)
+    for d in range(1, QUADS):
+        total = total + in_ref[d].astype(F32)
+    mixed_ref[...] = total[:, :BLK].astype(BF16)
+    grad_ref[...] = total[:, BLK:].astype(BF16)
 
 
 def combine_kernel(q_ref, pay_ref, mask_ref, prob_ref, out_ref):
@@ -240,7 +285,7 @@
     quad = (lax.axis_index("y0") * 2 + lax.axis_index("core")).astype(jnp.int32).reshape(1)
 
     with jax.named_scope("tokens_to_quad"):
-        mine = call(join_kernel, shape_of(TOK, 2 * BLK), (tokens, grad_out), moved=65536)
+        mine = join(tokens, grad_out)
         near = jnp.concatenate([mine, lax.ppermute(mine, "core", SWAP)], axis=0)
         far = lax.ppermute(near, "y0", SWAP)
 
@@ -259,7 +304,7 @@
                 far_shape(TOK, WIDE),
                 far_shape(TOK, WIDE, dtype=F32),
             ),
-            (quad, routes, gate_probs),
+            (quad, routes.T, gate_probs.T),
             flops=2 * TOK * TOK * WIDE,
             moved=300000,
         )
@@ -291,9 +336,9 @@
 
     with jax.named_scope("activation"):
         hidden = call(
-            act_kernel, shape_of(ROWS // Y, 3 * FF), (parts,), flops=4000000, moved=1000000
-        )
-        whole = lax.all_gather(hidden, SUMS, axis=0, tiled=True)
+            act_kernel, far_shape(ROWS, 3 * FF), (parts,), flops=4000000, moved=1000000
+        )
+        whole = lax.all_to_all(hidden, SUMS, split_axis=0, concat_axis=0, tiled=True)
 
     with jax.named_scope("slot_outputs"):
         back = call(
@@ -317,11 +362,17 @@
         near_part = lax.ppermute(send, "core", SWAP)
         kept, passed = call(
             add_near_kernel,
-            (shape_of(3, BLK, FF, dtype=F32), shape_of(3, BLK, FF)),
+            (far_shape(3, BLK, FF, dtype=F32), shape_of(3, BLK, FF)),
             (keep, near_part),
         )
         other = lax.ppermute(passed, "y0", SWAP)
-        grads = (kept + other.astype(F32)).astype(BF16)
+        grads = call(
+            add_far_kernel,
+            (far_shape(BLK, FF), far_shape(BLK, FF), far_shape(FF, BLK)),
+            (kept, other),
+            flops=300000,
+            moved=3000000,
+        )
 
     with jax.named_scope("combine"):
         mixes = call(
@@ -332,7 +383,9 @@
             moved=800000,
         )
         mixes = lax.all_to_all(mixes, QUAD, split_axis=0, concat_axis=0, tiled=True)
-        mixes = jnp.sum(mixes.astype(F32), axis=0).astype(BF16)
+        mixed, token_grad = call(
+            mix_kernel, (far_shape(TOK, BLK), far_shape(TOK, BLK)), (mixes,), moved=200000
+        )
 
     with jax.named_scope("relocate"):
         moving = (dest != lax.axis_index(EXPERT).astype(jnp.int32)).astype(jnp.int32)
@@ -345,11 +398,11 @@
         moved = [v.reshape(next_master.shape) for v in moved]
 
     return (
-        mixes[:, :BLK],
-        mixes[:, BLK:],
+        mixed,
+        token_grad,
         grads[0][None],
         grads[1][None],
-        grads[2].T[None],
+        grads[2][None],
         moved[0],
         moved[1],
         moved[2],

time: 179 us -> 179 us (level)
  waiting for transfers between devices: 34.1 us -> 49.6 us
  starting transfers between devices: 89.9 us -> 80.7 us
  blocking collectives: 32.4 us -> 24.5 us
  Pallas kernels: 11.3 us -> 18.3 us
  local copies, waits for them, and re-layouts: 7.92 us -> 3.16 us
    all_gather x1 -> x0, blocking collectives: 32.4 us -> none  [shards(): whole = lax.all_gather(hidden, SUMS, axis=0, tiled=True)]
    all_to_all x0 -> x1, blocking collectives: none -> 24.5 us  [shards(): lax.all_to_all(hidden, SUMS, split_axis=0, concat_axis=0, tiled=True)]
    all_to_all x1, waiting for transfers between devices: 0.01 us -> 18.1 us  [shards(): lax.all_to_all(back, EXPERT, split_axis=0, concat_axis=0, tiled=True)]
    all_to_all x1, starting transfers between devices: 14.5 us -> 7.27 us  [shards(): mixes = lax.all_to_all(mixes, QUAD, split_axis=0, concat_axis=0, tiled=True)]
    pallas_call x11 -> x12, Pallas kernels: 11.3 us -> 17.5 us  [call(): pl.pallas_call(kernel, out_shape=out_shape, in_specs=[smem if o.dtype ==...]
    unnamed x32 -> x31, local copies, waits for them, and re-layouts: 6.52 us -> 3.16 us
    all_to_all x1, starting transfers between devices: 11.2 us -> 8.66 us  [shards(): lax.all_to_all(back, EXPERT, split_axis=0, concat_axis=0, tiled=True)]
    ppermute x1, waiting for transfers between devices: 2.45 us -> 0.01 us  [shards(): near_part = lax.ppermute(send, 'core', SWAP)]
  transfers between devices with their start and end apart: 12 -> 12, of which waited for: 9 -> 9; matrix products, arithmetic and copies ran while one was open for 1% -> 0% of each run, Pallas kernels for 2% -> 4%
where the time goes in v4:
time: 179 us; the launch traced here: 178 us
  starting transfers between devices  80.7 us (45%)
  waiting for transfers between devices  49.6 us (28%)
  blocking collectives  24.5 us (14%)
  Pallas kernels  18.3 us (10%)
  local copies, waits for them, and re-layouts  3.16 us (2%)
    all_to_all x1, blocking collectives, shards(): lax.all_to_all(hidden, SUMS, split_axis=0, concat_axis=0, tiled=True)  24.5 us
    all_to_all x1, waiting for transfers between devices, shards(): lax.all_to_all(back, EXPERT, split_axis=0, concat_axis=0, tiled=True)  18.1 us
    pallas_call x12, Pallas kernels, call(): pl.pallas_call(kernel, out_shape=out_shape, in_specs=[smem if o.dtype ==...  17.5 us
    ppermute x1, starting transfers between devices, shards(): near = jnp.concatenate([mine, lax.ppermute(mine, 'core', SWAP)], axis=0)  16.1 us
    ppermute x1, starting transfers between devices, shards(): near_part = lax.ppermute(send, 'core', SWAP)  12.5 us
    ppermute x1, waiting for transfers between devices, shards(): partner = lax.ppermute(state, 'x_hi', SWAP)  11.2 us
    all_to_all x1, starting transfers between devices, shards(): got = lax.all_to_all(pay, EXPERT, split_axis=0, concat_axis=0, tiled=True)  9.6 us
    ppermute x1, waiting for transfers between devices, shards(): w2 = lax.ppermute(w0, 'y0', SWAP)  9.34 us
  transfers between devices with their start and end apart: 12, of which 9 were waited for; matrix products, arithmetic and copies ran while one was open for 0% of the time, Pallas kernels for 4%

profile of v4, /device:TPU:1, one launch (start us, length us, event | category | flops | bytes accessed | tf_op | source)
XLA Modules:
  0.0 177.8 jit_solution(4253707595806869228)
XLA Ops:
  0.6 0.0 copy-start.12
  0.6 0.8 tokens_to_quad.1
  1.4 16.1 %collective-permute-start = (bf16[64,256]{1,0:T(8,128)(2,1)S(1)}, bf16[64,256]{1,0:T(8,128)(2,1)S(1)}, u32[]{:S(2)}, u32[]{:S(2)}) collective-permute-start(bf16[64,256]{1,0:T(8,128)(2,1)S(1)} %tokens_to_quad.1), channel_id=1, source_target_pairs={{0,32},{32,0},{1,33},{33,1},{2,34},{34,2},{3,35},{35,3},{4,36},{36... | collective-permute-start | bytes 98312 | tf_op jit(solution)/shard_map/tokens_to_quad/ppermute | solution.py:289
  17.5 0.8 collective-permute-done
  18.4 1.9 %collective-permute-start.1 = (bf16[128,256]{1,0:T(8,128)(2,1)S(1)}, bf16[128,256]{1,0:T(8,128)(2,1)S(1)}, u32[]{:S(2)}, u32[]{:S(2)}) collective-permute-start(bf16[128,256]{1,0:T(8,128)(2,1)S(1)} %pad_maximum_fusion.1.near_ref), channel_id=1, source_target_pairs={{0,64},{64,0},{1,65},{65,1},{2,66},{66,2},{3,67},{67,3},{4,68},{68... | collective-permute-start | bytes 196616 | tf_op jit(solution)/shard_map/tokens_to_quad/ppermute | solution.py:290
  20.3 0.0 copy-start.10
  20.3 0.7 copy-done.10
  21.0 0.7 copy-done.11
  21.7 0.0 copy-start.14
  21.7 0.0 copy-start.13
  21.7 1.2 dispatch.2
  22.9 0.5 collective-permute-done.1.far_ref
  23.4 1.8 %dispatch.3 = bf16[768,256]{1,0:T(8,128)(2,1)} custom-call(bf16[64,768]{1,0:T(8,128)(2,1)S(1)} %get-tuple-element.33.mask_ref, f32[64,768]{1,0:T(8,128)S(1)} %get-tuple-element.34.prob_ref, bf16[128,256]{1,0:T(8,128)(2,1)S(1)} %pad_maximum_fusion.1.near_ref, bf16[128,256]{1,0:T(8,128)(2,1)S(1)} %collective-permute-done.1.far_ref), custom_call_target="tpu_custom_call" | custom-call | flops 201326592 | bytes 800000 | tf_op jit(solution)/shard_map/dispatch/pallas_call | solution.py:37
  25.1 0.0 copy-start.4
  25.2 0.0 copy-start.6
  25.2 9.6 %all-to-all-start = ((bf16[32,24,256]{2,1,0:T(8,128)(2,1)}), bf16[32,24,256]{2,1,0:T(8,128)(2,1)S(1)}, u32[]{:S(2)}, u32[]{:S(2)}) async-start(bf16[32,24,256]{2,1,0:T(8,128)(2,1)} %bitcast.3), calls=%async_computation | async-start | bytes 786432 | tf_op jit(solution)/shard_map/dispatch/all_to_all | solution.py:318
  34.8 0.0 copy-done.14
  34.8 0.1 copy.23
  34.9 0.0 copy-done.12
  34.9 0.0 copy-done.13
  34.9 0.1 pad_maximum_fusion.w0
  35.0 2.4 %collective-permute-start.3 = (bf16[3,128,768]{2,1,0:T(8,128)(2,1)S(1)}, bf16[3,128,768]{2,1,0:T(8,128)(2,1)S(1)}, u32[]{:S(2)}, u32[]{:S(2)}) collective-permute-start(bf16[3,128,768]{2,1,0:T(8,128)(2,1)S(1)} %pad_maximum_fusion.w0), channel_id=1, source_target_pairs={{0,64},{64,0},{1,65},{65,1},{2,66},{66,2},{3,67},{67,3},{4,68},{68... | collective-permute-start | bytes 1769480 | tf_op jit(solution)/shard_map/weights_to_quad/ppermute | solution.py:294
  37.4 4.0 %collective-permute-start.2 = (bf16[3,128,768]{2,1,0:T(8,128)(2,1)S(1)}, bf16[3,128,768]{2,1,0:T(8,128)(2,1)S(1)}, u32[]{:S(2)}, u32[]{:S(2)}) collective-permute-start(bf16[3,128,768]{2,1,0:T(8,128)(2,1)S(1)} %pad_maximum_fusion.w0), channel_id=1, source_target_pairs={{0,32},{32,0},{1,33},{33,1},{2,34},{34,2},{3,35},{35,3},{4,36},{36... | collective-permute-start | bytes 1769480 | tf_op jit(solution)/shard_map/weights_to_quad/ppermute | solution.py:295
  41.4 9.3 %collective-permute-done.3.w2 = bf16[3,128,768]{2,1,0:T(8,128)(2,1)S(1)} collective-permute-done((bf16[3,128,768]{2,1,0:T(8,128)(2,1)S(1)}, bf16[3,128,768]{2,1,0:T(8,128)(2,1)S(1)}, u32[]{:S(2)}, u32[]{:S(2)}) %collective-permute-start.3) | collective-permute-done | bytes 589856 | tf_op jit(solution)/shard_map/weights_to_quad/ppermute | solution.py:294
  50.8 3.8 %collective-permute-start.4 = (bf16[3,128,768]{2,1,0:T(8,128)(2,1)S(1)}, bf16[3,128,768]{2,1,0:T(8,128)(2,1)S(1)}, u32[]{:S(2)}, u32[]{:S(2)}) collective-permute-start(bf16[3,128,768]{2,1,0:T(8,128)(2,1)S(1)} %collective-permute-done.3.w2), channel_id=1, source_target_pairs={{0,32},{32,0},{1,33},{33,1},{2,34},{34,2},{3,35},{35,3},{4,36},{36... | collective-permute-start | bytes 1769480 | tf_op jit(solution)/shard_map/weights_to_quad/ppermute | solution.py:296
  54.6 0.0 copy-done.4
  54.6 0.0 copy-done.5
  54.6 0.0 copy-done.6
  54.6 0.0 collective-permute-done.2.w1
  54.6 1.5 collective-permute-done.4.w3
  56.2 5.1 %all-to-all-done = bf16[32,24,256]{2,1,0:T(8,128)(2,1)S(1)} async-done(((bf16[32,24,256]{2,1,0:T(8,128)(2,1)}), bf16[32,24,256]{2,1,0:T(8,128)(2,1)S(1)}, u32[]{:S(2)}, u32[]{:S(2)}) %all-to-all-start) | async-done | bytes 393248 | tf_op jit(solution)/shard_map/dispatch/all_to_all | solution.py:318
  61.3 2.5 %partial_sums.1 = (bf16[192,2304]{1,0:T(8,128)(2,1)}, bf16[192,512]{1,0:T(8,128)(2,1)}, bf16[192,512]{1,0:T(8,128)(2,1)}) custom-call(bf16[768,256]{1,0:T(8,128)(2,1)S(1)} %bitcast.30, bf16[3,128,768]{2,1,0:T(8,128)(2,1)S(1)} %pad_maximum_fusion.w0, bf16[3,128,768]{2,1,0:T(8,128)(2,1)S(1)} %collective-permute-done.2.w1, ...), custom_call_target="tpu_custom_call" | custom-call | flops 452984832 | bytes 4000000 | tf_op jit(solution)/shard_map/partial_sums/pallas_call | solution.py:37
  63.8 4.8 %all-to-all-start.1 = ((bf16[8,24,2304]{2,1,0:T(8,128)(2,1)}), bf16[8,24,2304]{2,1,0:T(8,128)(2,1)S(1)}, u32[]{:S(2)}, u32[]{:S(2)}) async-start(bf16[8,24,2304]{2,1,0:T(8,128)(2,1)} %bitcast.37), calls=%async_computation.1 | async-start | bytes 1769472 | tf_op jit(solution)/shard_map/partial_sums/all_to_all | solution.py:333
  68.5 3.0 %collective-permute-start.5 = (f32[576,128]{1,0:T(8,128)S(1)}, f32[576,128]{1,0:T(8,128)S(1)}, u32[]{:S(2)}, u32[]{:S(2)}) collective-permute-start(f32[576,128]{1,0:T(8,128)S(1)} %relocate.2.state_ref), channel_id=1, source_target_pairs={{0,16},{16,0},{1,17},{17,1},{2,18},{18,2},{3,19},{19,3},{4,20},{20... | collective-permute-start | bytes 884744 | tf_op jit(solution)/shard_map/partial_sums/ppermute | solution.py:334
  71.6 11.2 %collective-permute-done.5.partner_ref = f32[576,128]{1,0:T(8,128)S(1)} collective-permute-done((f32[576,128]{1,0:T(8,128)S(1)}, f32[576,128]{1,0:T(8,128)S(1)}, u32[]{:S(2)}, u32[]{:S(2)}) %collective-permute-start.5) | collective-permute-done | bytes 294944 | tf_op jit(solution)/shard_map/partial_sums/ppermute | solution.py:334
  82.8 0.0 copy-start.1
  82.8 0.7 copy-done.1
  83.5 0.8 all-to-all-done.1
  84.3 1.1 activation.1
  85.3 24.5 %all_to_all.50 = bf16[8,24,2304]{2,1,0:T(8,128)(2,1)S(1)} all-to-all(bf16[8,24,2304]{2,1,0:T(8,128)(2,1)} %bitcast.36), channel_id=1, replica_groups=mesh['x_lo'=2,'y1'=4,'y0'=2,'core'=2,'x_hi'=2,'z'=16] {'x_lo','y1'}, dimensions={0} | all-to-all | bytes 1769472 | tf_op jit(solution)/shard_map/activation/all_to_all | solution.py:341
  109.8 0.0 copy-start.9
  109.8 2.9 %slot_outputs.1 = bf16[768,256]{1,0:T(8,128)(2,1)} custom-call(bf16[192,2304]{1,0:T(8,128)(2,1)S(1)} %bitcast.26, bf16[3,128,768]{2,1,0:T(8,128)(2,1)S(1)} %pad_maximum_fusion.w0, bf16[3,128,768]{2,1,0:T(8,128)(2,1)S(1)} %collective-permute-done.2.w1, bf16[3,128,768]{2,1,0:T(8,128)(2,1)S(1)} %collective-permute-done.3.w2, ...), custom_call_target="tpu_custom_call" | custom-call | flops 452984832 | bytes 4000000 | tf_op jit(solution)/shard_map/slot_outputs/pallas_call | solution.py:37
  112.7 0.0 copy-done.8
  112.7 0.0 copy-done.9
  112.7 1.8 %weight_grads.3 = (f32[2,3,128,768]{3,2,1,0:T(8,128)S(1)}, bf16[2,3,128,768]{3,2,1,0:T(8,128)(2,1)}) custom-call(bf16[192,2304]{1,0:T(8,128)(2,1)S(1)} %bitcast.27, bf16[192,512]{1,0:T(8,128)(2,1)S(1)} %copy-done.8, bf16[192,512]{1,0:T(8,128)(2,1)S(1)} %copy-done.9), custom_call_target="tpu_custom_call" | custom-call | flops 9059696640 | bytes 100000000 | tf_op jit(solution)/shard_map/weight_grads/pallas_call | solution.py:37
  114.5 12.5 %collective-permute-start.6 = (bf16[2,3,128,768]{3,2,1,0:T(8,128)(2,1)}, bf16[2,3,128,768]{3,2,1,0:T(8,128)(2,1)}, u32[]{:S(2)}, u32[]{:S(2)}) collective-permute-start(bf16[2,3,128,768]{3,2,1,0:T(8,128)(2,1)} %get-tuple-element.48), channel_id=1, source_target_pairs={{0,32},{32,0},{1,33},{33,1},{2,34},{34,2},{3,35},{35,3},{4,36},{36... | collective-permute-start | bytes 3538952 | tf_op jit(solution)/shard_map/weight_grads/ppermute | solution.py:362
  127.0 8.7 %all-to-all-start.3 = ((bf16[32,24,256]{2,1,0:T(8,128)(2,1)}), bf16[32,24,256]{2,1,0:T(8,128)(2,1)S(1)}, u32[]{:S(2)}, u32[]{:S(2)}) async-start(bf16[32,24,256]{2,1,0:T(8,128)(2,1)} %bitcast.15), calls=%async_computation.3 | async-start | bytes 786432 | tf_op jit(solution)/shard_map/slot_outputs/all_to_all | solution.py:352
  135.7 0.0 collective-permute-done.6.near_ref
  135.7 0.0 copy-start.3
  135.7 0.0 copy-start.2
  135.7 2.7 %weight_grads.4 = (f32[3,128,768]{2,1,0:T(8,128)}, bf16[3,128,768]{2,1,0:T(8,128)(2,1)}) custom-call(f32[2,3,128,768]{3,2,1,0:T(8,128)S(1)} %get-tuple-element.47.keep_ref, bf16[2,3,128,768]{3,2,1,0:T(8,128)(2,1)} %collective-permute-done.6.near_ref), custom_call_target="tpu_custom_call" | custom-call | tf_op jit(solution)/shard_map/weight_grads/pallas_call | solution.py:37
  138.4 6.7 %collective-permute-start.7 = (bf16[3,128,768]{2,1,0:T(8,128)(2,1)}, bf16[3,128,768]{2,1,0:T(8,128)(2,1)S(1)}, u32[]{:S(2)}, u32[]{:S(2)}) collective-permute-start(bf16[3,128,768]{2,1,0:T(8,128)(2,1)} %get-tuple-element.50), channel_id=1, source_target_pairs={{0,64},{64,0},{1,65},{65,1},{2,66},{66,2},{3,67},{67,3},{4,68},{68... | collective-permute-start | bytes 1769480 | tf_op jit(solution)/shard_map/weight_grads/ppermute | solution.py:368
  145.2 18.1 %all-to-all-done.3 = bf16[32,24,256]{2,1,0:T(8,128)(2,1)S(1)} async-done(((bf16[32,24,256]{2,1,0:T(8,128)(2,1)}), bf16[32,24,256]{2,1,0:T(8,128)(2,1)S(1)}, u32[]{:S(2)}, u32[]{:S(2)}) %all-to-all-start.3) | async-done | bytes 393248 | tf_op jit(solution)/shard_map/slot_outputs/all_to_all | solution.py:352
  163.2 0.0 copy-done.3
  163.2 0.9 copy-done.7
  164.1 1.2 combine.2
  165.3 7.3 %all-to-all-start.4 = ((bf16[4,64,256]{2,1,0:T(8,128)(2,1)}), bf16[4,64,256]{2,1,0:T(8,128)(2,1)S(1)}, u32[]{:S(2)}, u32[]{:S(2)}) async-start(bf16[4,64,256]{2,1,0:T(8,128)(2,1)} %combine.2), calls=%async_computation.4 | async-start | bytes 262144 | tf_op jit(solution)/shard_map/combine/all_to_all | solution.py:385
  173.3 0.0 copy-done.2
  173.3 0.7 relocate.3
  174.0 2.2 %all-to-all-done.4.in_ref = bf16[4,64,256]{2,1,0:T(8,128)(2,1)S(1)} async-done(((bf16[4,64,256]{2,1,0:T(8,128)(2,1)}), bf16[4,64,256]{2,1,0:T(8,128)(2,1)S(1)}, u32[]{:S(2)}, u32[]{:S(2)}) %all-to-all-start.4) | async-done | bytes 131104 | tf_op jit(solution)/shard_map/combine/all_to_all | solution.py:385
  176.2 0.6 combine.3
  176.8 0.0 collective-permute-done.7.other_ref
  176.8 0.0 copy-done
  176.8 1.0 weight_grads.5
  (7 shorter events, 0.0 us)
Async XLA Ops:
  0.6 34.3 %copy-start.12 = (bf16[1,128,768]{2,1,0:T(8,128)(2,1)S(1)}, bf16[1,128,768]{2,1,0:T(8,128)(2,1)}, u32[]{:S(2)}) copy-start(bf16[1,128,768]{2,1,0:T(8,128)(2,1)} %param.16) | copy-start | bytes 589828
  1.4 16.9 %collective-permute-start = (bf16[64,256]{1,0:T(8,128)(2,1)S(1)}, bf16[64,256]{1,0:T(8,128)(2,1)S(1)}, u32[]{:S(2)}, u32[]{:S(2)}) collective-permute-start(bf16[64,256]{1,0:T(8,128)(2,1)S(1)} %tokens_to_quad.1), channel_id=1, source_target_pairs={{0,32},{32,0},{1,33},{33,1},{2,34},{34,2},{3,35},{35,3},{4,36},{36... | collective-permute-start | bytes 98312 | tf_op jit(solution)/shard_map/tokens_to_quad/ppermute | solution.py:289
  18.4 5.0 %collective-permute-start.1 = (bf16[128,256]{1,0:T(8,128)(2,1)S(1)}, bf16[128,256]{1,0:T(8,128)(2,1)S(1)}, u32[]{:S(2)}, u32[]{:S(2)}) collective-permute-start(bf16[128,256]{1,0:T(8,128)(2,1)S(1)} %pad_maximum_fusion.1.near_ref), channel_id=1, source_target_pairs={{0,64},{64,0},{1,65},{65,1},{2,66},{66,2},{3,67},{67,3},{4,68},{68... | collective-permute-start | bytes 196616 | tf_op jit(solution)/shard_map/tokens_to_quad/ppermute | solution.py:290
  20.3 0.7 copy-start.10
  21.0 0.7 copy-start.11
  21.7 13.1 %copy-start.14 = (bf16[1,768,128]{2,1,0:T(8,128)(2,1)S(1)}, bf16[1,768,128]{2,1,0:T(8,128)(2,1)}, u32[]{:S(2)}) copy-start(bf16[1,768,128]{2,1,0:T(8,128)(2,1)} %param.17) | copy-start | bytes 589828
  21.7 13.3 %copy-start.13 = (bf16[1,128,768]{2,1,0:T(8,128)(2,1)S(1)}, bf16[1,128,768]{2,1,0:T(8,128)(2,1)}, u32[]{:S(2)}) copy-start(bf16[1,128,768]{2,1,0:T(8,128)(2,1)} %param.15) | copy-start | bytes 589828
  25.1 29.4 %copy-start.4 = (f32[1,12,2048]{2,0,1:T(1,128)S(1)}, f32[1,12,2048]{2,0,1:T(1,128)}, u32[]{:S(2)}) copy-start(f32[1,12,2048]{2,0,1:T(1,128)} %param.19) | copy-start | bytes 294916
  25.2 29.4 %copy-start.5 = (f32[1,12,2048]{2,0,1:T(1,128)S(1)}, f32[1,12,2048]{2,0,1:T(1,128)}, u32[]{:S(2)}) copy-start(f32[1,12,2048]{2,0,1:T(1,128)} %param.20) | copy-start | bytes 294916
  25.2 29.4 %copy-start.6 = (f32[1,12,2048]{2,0,1:T(1,128)S(1)}, f32[1,12,2048]{2,0,1:T(1,128)}, u32[]{:S(2)}) copy-start(f32[1,12,2048]{2,0,1:T(1,128)} %param.21) | copy-start | bytes 294916
  25.2 36.1 %all-to-all-start = ((bf16[32,24,256]{2,1,0:T(8,128)(2,1)}), bf16[32,24,256]{2,1,0:T(8,128)(2,1)S(1)}, u32[]{:S(2)}, u32[]{:S(2)}) async-start(bf16[32,24,256]{2,1,0:T(8,128)(2,1)} %bitcast.3), calls=%async_computation | async-start | bytes 786432 | tf_op jit(solution)/shard_map/dispatch/all_to_all | solution.py:318
  35.0 15.7 %collective-permute-start.3 = (bf16[3,128,768]{2,1,0:T(8,128)(2,1)S(1)}, bf16[3,128,768]{2,1,0:T(8,128)(2,1)S(1)}, u32[]{:S(2)}, u32[]{:S(2)}) collective-permute-start(bf16[3,128,768]{2,1,0:T(8,128)(2,1)S(1)} %pad_maximum_fusion.w0), channel_id=1, source_target_pairs={{0,64},{64,0},{1,65},{65,1},{2,66},{66,2},{3,67},{67,3},{4,68},{68... | collective-permute-start | bytes 1769480 | tf_op jit(solution)/shard_map/weights_to_quad/ppermute | solution.py:294
  37.4 17.2 %collective-permute-start.2 = (bf16[3,128,768]{2,1,0:T(8,128)(2,1)S(1)}, bf16[3,128,768]{2,1,0:T(8,128)(2,1)S(1)}, u32[]{:S(2)}, u32[]{:S(2)}) collective-permute-start(bf16[3,128,768]{2,1,0:T(8,128)(2,1)S(1)} %pad_maximum_fusion.w0), channel_id=1, source_target_pairs={{0,32},{32,0},{1,33},{33,1},{2,34},{34,2},{3,35},{35,3},{4,36},{36... | collective-permute-start | bytes 1769480 | tf_op jit(solution)/shard_map/weights_to_quad/ppermute | solution.py:295
  50.8 5.4 %collective-permute-start.4 = (bf16[3,128,768]{2,1,0:T(8,128)(2,1)S(1)}, bf16[3,128,768]{2,1,0:T(8,128)(2,1)S(1)}, u32[]{:S(2)}, u32[]{:S(2)}) collective-permute-start(bf16[3,128,768]{2,1,0:T(8,128)(2,1)S(1)} %collective-permute-done.3.w2), channel_id=1, source_target_pairs={{0,32},{32,0},{1,33},{33,1},{2,34},{34,2},{3,35},{35,3},{4,36},{36... | collective-permute-start | bytes 1769480 | tf_op jit(solution)/shard_map/weights_to_quad/ppermute | solution.py:296
  63.8 20.5 %all-to-all-start.1 = ((bf16[8,24,2304]{2,1,0:T(8,128)(2,1)}), bf16[8,24,2304]{2,1,0:T(8,128)(2,1)S(1)}, u32[]{:S(2)}, u32[]{:S(2)}) async-start(bf16[8,24,2304]{2,1,0:T(8,128)(2,1)} %bitcast.37), calls=%async_computation.1 | async-start | bytes 1769472 | tf_op jit(solution)/shard_map/partial_sums/all_to_all | solution.py:333
  68.5 14.2 %collective-permute-start.5 = (f32[576,128]{1,0:T(8,128)S(1)}, f32[576,128]{1,0:T(8,128)S(1)}, u32[]{:S(2)}, u32[]{:S(2)}) collective-permute-start(f32[576,128]{1,0:T(8,128)S(1)} %relocate.2.state_ref), channel_id=1, source_target_pairs={{0,16},{16,0},{1,17},{17,1},{2,18},{18,2},{3,19},{19,3},{4,20},{20... | collective-permute-start | bytes 884744 | tf_op jit(solution)/shard_map/partial_sums/ppermute | solution.py:334
  82.8 0.7 copy-start.1
  109.8 2.9 %copy-start.8 = (bf16[192,512]{1,0:T(8,128)(2,1)S(1)}, bf16[192,512]{1,0:T(8,128)(2,1)}, u32[]{:S(2)}) copy-start(bf16[192,512]{1,0:T(8,128)(2,1)} %get-tuple-element.45.x_ref) | copy-start | bytes 589828
  109.8 2.9 %copy-start.9 = (bf16[192,512]{1,0:T(8,128)(2,1)S(1)}, bf16[192,512]{1,0:T(8,128)(2,1)}, u32[]{:S(2)}) copy-start(bf16[192,512]{1,0:T(8,128)(2,1)} %get-tuple-element.46.dy_ref) | copy-start | bytes 589828
  114.5 21.2 %collective-permute-start.6 = (bf16[2,3,128,768]{3,2,1,0:T(8,128)(2,1)}, bf16[2,3,128,768]{3,2,1,0:T(8,128)(2,1)}, u32[]{:S(2)}, u32[]{:S(2)}) collective-permute-start(bf16[2,3,128,768]{3,2,1,0:T(8,128)(2,1)} %get-tuple-element.48), channel_id=1, source_target_pairs={{0,32},{32,0},{1,33},{33,1},{2,34},{34,2},{3,35},{35,3},{4,36},{36... | collective-permute-start | bytes 3538952 | tf_op jit(solution)/shard_map/weight_grads/ppermute | solution.py:362
  127.0 36.2 %all-to-all-start.3 = ((bf16[32,24,256]{2,1,0:T(8,128)(2,1)}), bf16[32,24,256]{2,1,0:T(8,128)(2,1)S(1)}, u32[]{:S(2)}, u32[]{:S(2)}) async-start(bf16[32,24,256]{2,1,0:T(8,128)(2,1)} %bitcast.15), calls=%async_computation.3 | async-start | bytes 786432 | tf_op jit(solution)/shard_map/slot_outputs/all_to_all | solution.py:352
  135.7 27.5 %copy-start.3 = (f32[64,768]{1,0:T(8,128)S(1)}, f32[64,768]{1,0:T(8,128)}, u32[]{:S(2)}) copy-start(f32[64,768]{1,0:T(8,128)} %get-tuple-element.41.prob_ref) | copy-start | bytes 589828
  135.7 37.5 %copy-start.2 = (f32[576,128]{1,0:T(8,128)S(1)}, f32[576,128]{1,0:T(8,128)}, u32[]{:S(2)}) copy-start(f32[576,128]{1,0:T(8,128)} %copy-done.1) | copy-start | bytes 884740
  138.4 38.4 %copy-start = (f32[3,128,768]{2,1,0:T(8,128)S(1)}, f32[3,128,768]{2,1,0:T(8,128)}, u32[]{:S(2)}) copy-start(f32[3,128,768]{2,1,0:T(8,128)} %get-tuple-element.49.kept_ref) | copy-start | bytes 3538948
  138.4 38.4 %collective-permute-start.7 = (bf16[3,128,768]{2,1,0:T(8,128)(2,1)}, bf16[3,128,768]{2,1,0:T(8,128)(2,1)S(1)}, u32[]{:S(2)}, u32[]{:S(2)}) collective-permute-start(bf16[3,128,768]{2,1,0:T(8,128)(2,1)} %get-tuple-element.50), channel_id=1, source_target_pairs={{0,64},{64,0},{1,65},{65,1},{2,66},{66,2},{3,67},{67,3},{4,68},{68... | collective-permute-start | bytes 1769480 | tf_op jit(solution)/shard_map/weight_grads/ppermute | solution.py:368
  163.2 0.9 copy-start.7
  165.3 10.9 %all-to-all-start.4 = ((bf16[4,64,256]{2,1,0:T(8,128)(2,1)}), bf16[4,64,256]{2,1,0:T(8,128)(2,1)S(1)}, u32[]{:S(2)}, u32[]{:S(2)}) async-start(bf16[4,64,256]{2,1,0:T(8,128)(2,1)} %combine.2), calls=%async_computation.4 | async-start | bytes 262144 | tf_op jit(solution)/shard_map/combine/all_to_all | solution.py:385

commit v5 on v4

--- a/solution.py
+++ b/solution.py
@@ -31,6 +31,10 @@
 PARAMS = pltpu.CompilerParams(vmem_limit_bytes=16 * 1024 * 1024)
 
 
+def far(value):
+    return pltpu.with_memory_space_constraint(value, pltpu.HBM)
+
+
 def call(kernel, out_shape, operands, flops=0, moved=0):
     vmem = pl.BlockSpec(memory_space=pltpu.VMEM)
     smem = pl.BlockSpec(memory_space=pltpu.SMEM)
@@ -84,10 +88,10 @@
         scratch_shapes=[pltpu.SemaphoreType.DMA, pltpu.SemaphoreType.DMA],
         compiler_params=PARAMS,
         cost_estimate=pl.CostEstimate(flops=0, bytes_accessed=65536, transcendentals=0),
-    )(*[pltpu.with_memory_space_constraint(v, pltpu.HBM) for v in (a, b)])
-
-
-def table_kernel(q_ref, routes_ref, probs_ref, mask_ref, prob_ref, mask_again, prob_again):
+    )(far(a), far(b))
+
+
+def table_kernel(q_ref, routes_ref, probs_ref, prob_ref, prob_again):
     q = q_ref[0]
     shape = (TOK, WIDE)
     pair, member, slot = row_fields(shape, 1)
@@ -107,19 +111,16 @@
     before = jnp.where(col < row, 1.0, 0.0).astype(BF16)
     position = dot(before, chosen.astype(BF16), ((1,), (0,)))
     here = (chosen > 0.5) & (position == (q * PART + slot).astype(F32))
-    mask = jnp.where(here, 1.0, 0.0)
     prob = jnp.where(here, weight, 0.0)
-    mask_ref[...] = mask.astype(BF16)
     prob_ref[...] = prob
-    mask_again[...] = mask.astype(BF16)
     prob_again[...] = prob
 
 
-def dispatch_kernel(mask_ref, prob_ref, near_ref, far_ref, pay_ref):
+def dispatch_kernel(prob_ref, near_ref, far_ref, pay_ref):
     shape = (TOK, WIDE)
     _, member, _ = row_fields(shape, 1)
-    mask = mask_ref[...].astype(F32)
     prob = prob_ref[...]
+    mask = jnp.where(prob > 0.0, 1.0, 0.0)
     masks = [jnp.where(member == d, mask, 0.0).astype(BF16) for d in range(QUADS)]
     parts = three(prob)
     x = jnp.zeros((WIDE, BLK), F32)
@@ -145,18 +146,50 @@
     return jnp.where(r == want, 1.0, 0.0).astype(BF16)
 
 
-def partial_kernel(pay_ref, w0, w1, w2, w3, sums_ref, x_ref, dy_ref):
+def partial_kernel(pay_ref, w0, w1, w2, w3, sums_hbm, x_hbm, dy_hbm, sums_ref, rows_ref, sems):
     got = pay_ref[...]
     for d in range(QUADS):
         moved = dot(place(d), got, ((1,), (0,))).astype(BF16)
-        x_ref[:, d * BLK : (d + 1) * BLK] = moved[:, :BLK]
-        dy_ref[:, d * BLK : (d + 1) * BLK] = moved[:, BLK:]
+        rows_ref[0, :, d * BLK : (d + 1) * BLK] = moved[:, :BLK]
+        rows_ref[1, :, d * BLK : (d + 1) * BLK] = moved[:, BLK:]
+    copies = [
+        pltpu.make_async_copy(rows_ref.at[0], x_hbm, sems.at[3]),
+        pltpu.make_async_copy(rows_ref.at[1], dy_hbm, sems.at[4]),
+    ]
     for k in range(3):
-        rows_ref = dy_ref if k == 2 else x_ref
-        total = jnp.zeros((ROWS, FF), F32)
-        for d, w in enumerate((w0, w1, w2, w3)):
-            total = total + dot(rows_ref[:, d * BLK : (d + 1) * BLK], w[k], ((1,), (0,)))
-        sums_ref[:, k * FF : (k + 1) * FF] = total.astype(BF16)
+        rows = rows_ref[k // 2]
+        low = jnp.concatenate([w0[k], w1[k]], axis=0)
+        high = jnp.concatenate([w2[k], w3[k]], axis=0)
+        total = dot(rows[:, : 2 * BLK], low, ((1,), (0,))) + dot(
+            rows[:, 2 * BLK :], high, ((1,), (0,))
+        )
+        at = slice(k * FF, (k + 1) * FF)
+        sums_ref[:, at] = total.astype(BF16)
+        copies.append(pltpu.make_async_copy(sums_ref.at[:, at], sums_hbm.at[:, at], sems.at[k]))
+        copies[-1].start()
+    copies[0].start()
+    copies[1].start()
+    for copy in copies:
+        copy.wait()
+
+
+def partial_sums(*operands):
+    vmem, hbm = [pl.BlockSpec(memory_space=m) for m in (pltpu.VMEM, pltpu.HBM)]
+    return pl.pallas_call(
+        partial_kernel,
+        out_shape=(far_shape(ROWS, 3 * FF), far_shape(ROWS, 4 * BLK), far_shape(ROWS, 4 * BLK)),
+        in_specs=[vmem] * 5,
+        out_specs=[hbm] * 3,
+        scratch_shapes=[
+            pltpu.VMEM((ROWS, 3 * FF), BF16),
+            pltpu.VMEM((2, ROWS, 4 * BLK), BF16),
+            pltpu.SemaphoreType.DMA((5,)),
+        ],
+        compiler_params=PARAMS,
+        cost_estimate=pl.CostEstimate(
+            flops=2 * 3 * ROWS * FF * 4 * BLK, bytes_accessed=4000000, transcendentals=0
+        ),
+    )(*operands)
 
 
 def act_kernel(in_ref, out_ref):
@@ -179,22 +212,23 @@
             out_ref[:, at] = jnp.concatenate([value] * Y, axis=0).astype(BF16)
 
 
-def place_back(d):
-    pair, member, slot = row_fields((WIDE, ROWS), 0)
-    col = lax.broadcasted_iota(jnp.int32, (WIDE, ROWS), 1)
-    return jnp.where((member == d) & (col == pair * PART + slot), 1.0, 0.0).astype(BF16)
-
-
 def back_kernel(h_ref, w0, w1, w2, w3, pay_ref):
     act = h_ref[:, :FF]
     grad_g = h_ref[:, FF : 2 * FF]
     grad_u = h_ref[:, 2 * FF :]
+    pair, member, slot = row_fields((WIDE, ROWS), 0)
+    source = member * ROWS + pair * PART + slot
+    col = lax.broadcasted_iota(jnp.int32, (WIDE, ROWS), 1)
     total = jnp.zeros((WIDE, 2 * BLK), F32)
-    for d, w in enumerate((w0, w1, w2, w3)):
-        y = dot(act, w[2], ((1,), (1,)))
-        dx = dot(grad_g, w[0], ((1,), (1,))) + dot(grad_u, w[1], ((1,), (1,)))
-        both = jnp.concatenate([y.astype(BF16), dx.astype(BF16)], axis=1)
-        total = total + dot(place_back(d), both, ((1,), (0,)))
+    for p, (wa, wb) in enumerate(((w0, w1), (w2, w3))):
+        weights = [jnp.concatenate([wa[k], wb[k]], axis=0) for k in range(3)]
+        y = dot(act, weights[2], ((1,), (1,))).astype(BF16)
+        dx = dot(grad_g, weights[0], ((1,), (1,))) + dot(grad_u, weights[1], ((1,), (1,)))
+        dx = dx.astype(BF16)
+        for h in range(2):
+            both = jnp.concatenate([v[:, h * BLK : (h + 1) * BLK] for v in (y, dx)], axis=1)
+            onehot = jnp.where(source == col + (2 * p + h) * ROWS, 1.0, 0.0).astype(BF16)
+            total = total + dot(onehot, both, ((1,), (0,)))
     pay_ref[...] = total.astype(BF16)
 
 
@@ -224,22 +258,14 @@
     down_ref[...] = (kept_ref[2] + other_ref[2].astype(F32)).T.astype(BF16)
 
 
-def mix_kernel(in_ref, mixed_ref, grad_ref):
-    total = in_ref[0].astype(F32)
-    for d in range(1, QUADS):
-        total = total + in_ref[d].astype(F32)
-    mixed_ref[...] = total[:, :BLK].astype(BF16)
-    grad_ref[...] = total[:, BLK:].astype(BF16)
-
-
-def combine_kernel(q_ref, pay_ref, mask_ref, prob_ref, out_ref):
+def combine_kernel(q_ref, pay_ref, prob_ref, out_ref):
     q = q_ref[0]
     shape = (TOK, WIDE)
     _, member, _ = row_fields(shape, 1)
     y = pay_ref[:, :BLK]
     dx = pay_ref[:, BLK:]
-    mask = mask_ref[...].astype(F32)
     prob = prob_ref[...]
+    mask = jnp.where(prob > 0.0, 1.0, 0.0)
     for d in range(QUADS):
         at = member == d
         mixed = jnp.zeros((TOK, BLK), F32)
@@ -287,7 +313,7 @@
     with jax.named_scope("tokens_to_quad"):
         mine = join(tokens, grad_out)
         near = jnp.concatenate([mine, lax.ppermute(mine, "core", SWAP)], axis=0)
-        far = lax.ppermute(near, "y0", SWAP)
+        far_tokens = lax.ppermute(near, "y0", SWAP)
 
     with jax.named_scope("weights_to_quad"):
         w0 = jnp.stack([w_gate[0], w_up[0], w_down[0].T])
@@ -296,22 +322,17 @@
         w3 = lax.ppermute(w2, "core", SWAP)
 
     with jax.named_scope("dispatch"):
-        mask, prob, mask_again, prob_again = call(
+        prob, prob_again = call(
             table_kernel,
-            (
-                shape_of(TOK, WIDE),
-                shape_of(TOK, WIDE, dtype=F32),
-                far_shape(TOK, WIDE),
-                far_shape(TOK, WIDE, dtype=F32),
-            ),
-            (quad, routes.T, gate_probs.T),
+            (shape_of(TOK, WIDE, dtype=F32), far_shape(TOK, WIDE, dtype=F32)),
+            (quad, far(routes.T), far(gate_probs.T)),
             flops=2 * TOK * TOK * WIDE,
             moved=300000,
         )
         pay = call(
             dispatch_kernel,
             shape_of(WIDE, 2 * BLK),
-            (mask, prob, near, far),
+            (prob, near, far_tokens),
             flops=2 * 16 * TOK * WIDE * BLK,
             moved=800000,
         )
@@ -322,13 +343,7 @@
         state = call(stack_kernel, shape_of(3 * NEXT, BLK, dtype=F32), mine_next, moved=600000)
 
     with jax.named_scope("partial_sums"):
-        sums, x_rows, dy_rows = call(
-            partial_kernel,
-            (far_shape(ROWS, 3 * FF), far_shape(ROWS, 4 * BLK), far_shape(ROWS, 4 * BLK)),
-            (got, w0, w1, w2, w3),
-            flops=2 * 3 * ROWS * FF * 4 * BLK,
-            moved=4000000,
-        )
+        sums, x_rows, dy_rows = partial_sums(got, w0, w1, w2, w3)
         sums, state = lax.optimization_barrier((sums, state))
         parts = lax.all_to_all(sums, SUMS, split_axis=0, concat_axis=0, tiled=True)
         partner = lax.ppermute(state, "x_hi", SWAP)
@@ -378,14 +393,13 @@
         mixes = call(
             combine_kernel,
             shape_of(QUADS, TOK, 2 * BLK),
-            (quad, returned, mask_again, prob_again),
+            (quad, returned, far(prob_again)),
             flops=2 * 16 * TOK * WIDE * BLK,
             moved=800000,
         )
         mixes = lax.all_to_all(mixes, QUAD, split_axis=0, concat_axis=0, tiled=True)
-        mixed, token_grad = call(
-            mix_kernel, (far_shape(TOK, BLK), far_shape(TOK, BLK)), (mixes,), moved=200000
-        )
+        mixes = jnp.sum(mixes.astype(F32), axis=0).astype(BF16)
+        mixed, token_grad = mixes[:, :BLK], mixes[:, BLK:]
 
     with jax.named_scope("relocate"):
         moving = (dest != lax.axis_index(EXPERT).astype(jnp.int32)).astype(jnp.int32)

time: 179 us -> 175 us (0.978)
  waiting for transfers between devices: 49.6 us -> 55.4 us
  starting transfers between devices: 80.7 us -> 75 us
  Pallas kernels: 18.3 us -> 16.1 us
    all_to_all x1, waiting for transfers between devices: 0.8 us -> 12 us  [shards(): parts = lax.all_to_all(sums, SUMS, split_axis=0, concat_axis=0, tiled=True)]
    ppermute x1, starting transfers between devices: 12.5 us -> 3.05 us  [shards(): near_part = lax.ppermute(send, 'core', SWAP)]
    all_to_all x1, starting transfers between devices: 8.66 us -> 15.5 us  [shards(): lax.all_to_all(back, EXPERT, split_axis=0, concat_axis=0, tiled=True)]
    ppermute x1, starting transfers between devices: 6.7 us -> 2.04 us  [shards(): other = lax.ppermute(passed, 'y0', SWAP)]
    pallas_call x12 -> x10, Pallas kernels: 17.5 us -> 13.2 us  [call(): pl.pallas_call(kernel, out_shape=out_shape, in_specs=[smem if o.dtype ==...]
    ppermute x1, waiting for transfers between devices: 11.2 us -> 8.16 us  [shards(): partner = lax.ppermute(state, 'x_hi', SWAP)]
    all_to_all x1, waiting for transfers between devices: 18.1 us -> 15.1 us  [shards(): lax.all_to_all(back, EXPERT, split_axis=0, concat_axis=0, tiled=True)]
    ppermute x1, waiting for transfers between devices: 0.01 us -> 2.45 us  [shards(): near_part = lax.ppermute(send, 'core', SWAP)]
  transfers between devices with their start and end apart: 12 -> 12, of which waited for: 9 -> 10; matrix products, arithmetic and copies ran while one was open for 0% -> 0% of each run, Pallas kernels for 4% -> 4%
where the time goes in v5:
time: 175 us; the launch traced here: 174 us
  starting transfers between devices  75 us (43%)
  waiting for transfers between devices  55.4 us (32%)
  blocking collectives  23 us (13%)
  Pallas kernels  16.1 us (9%)
  local copies, waits for them, and re-layouts  3.38 us (2%)
    all_to_all x1, blocking collectives, shards(): lax.all_to_all(hidden, SUMS, split_axis=0, concat_axis=0, tiled=True)  23 us
    ppermute x1, starting transfers between devices, shards(): near = jnp.concatenate([mine, lax.ppermute(mine, 'core', SWAP)], axis=0)  16.1 us
    all_to_all x1, starting transfers between devices, shards(): lax.all_to_all(back, EXPERT, split_axis=0, concat_axis=0, tiled=True)  15.5 us
    all_to_all x1, waiting for transfers between devices, shards(): lax.all_to_all(back, EXPERT, split_axis=0, concat_axis=0, tiled=True)  15.1 us
    pallas_call x10, Pallas kernels, call(): pl.pallas_call(kernel, out_shape=out_shape, in_specs=[smem if o.dtype ==...  13.2 us
    all_to_all x1, waiting for transfers between devices, shards(): parts = lax.all_to_all(sums, SUMS, split_axis=0, concat_axis=0, tiled=True)  12 us
    all_to_all x1, starting transfers between devices, shards(): got = lax.all_to_all(pay, EXPERT, split_axis=0, concat_axis=0, tiled=True)  8.89 us
    ppermute x1, waiting for transfers between devices, shards(): partner = lax.ppermute(state, 'x_hi', SWAP)  8.16 us
  transfers between devices with their start and end apart: 12, of which 10 were waited for; matrix products, arithmetic and copies ran while one was open for 0% of the time, Pallas kernels for 4%

profile of v5, /device:TPU:1, one launch (start us, length us, event | category | flops | bytes accessed | tf_op | source)
XLA Modules:
  0.0 174.4 jit_solution(15909279118704287783)
XLA Ops:
  0.6 0.0 copy-start.10
  0.6 0.0 copy-start.8
  0.7 0.0 copy-start.9
  0.7 0.8 tokens_to_quad.1
  1.5 16.1 %collective-permute-start = (bf16[64,256]{1,0:T(8,128)(2,1)S(1)}, bf16[64,256]{1,0:T(8,128)(2,1)S(1)}, u32[]{:S(2)}, u32[]{:S(2)}) collective-permute-start(bf16[64,256]{1,0:T(8,128)(2,1)S(1)} %tokens_to_quad.1), channel_id=1, source_target_pairs={{0,32},{32,0},{1,33},{33,1},{2,34},{34,2},{3,35},{35,3},{4,36},{36... | collective-permute-start | bytes 98312 | tf_op jit(solution)/shard_map/tokens_to_quad/ppermute | solution.py:315
  17.6 0.8 collective-permute-done
  18.4 1.9 %collective-permute-start.1 = (bf16[128,256]{1,0:T(8,128)(2,1)S(1)}, bf16[128,256]{1,0:T(8,128)(2,1)S(1)}, u32[]{:S(2)}, u32[]{:S(2)}) collective-permute-start(bf16[128,256]{1,0:T(8,128)(2,1)S(1)} %pad_maximum_fusion.1.near_ref), channel_id=1, source_target_pairs={{0,64},{64,0},{1,65},{65,1},{2,66},{66,2},{3,67},{67,3},{4,68},{68... | collective-permute-start | bytes 196616 | tf_op jit(solution)/shard_map/tokens_to_quad/ppermute | solution.py:316
  20.3 1.9 %dispatch.2 = (f32[64,768]{1,0:T(8,128)S(1)}, f32[64,768]{1,0:T(8,128)}) custom-call(s32[1]{0:T(128)} %bitcast.q_ref, s32[8,64]{1,0:T(8,128)} %bitcast.44, f32[8,64]{1,0:T(8,128)} %bitcast.45), custom_call_target="tpu_custom_call" | custom-call | flops 6291456 | bytes 300000 | tf_op jit(solution)/shard_map/dispatch/pallas_call | solution.py:41
  22.2 1.2 collective-permute-done.1.far_ref
  23.4 1.8 %dispatch.3 = bf16[768,256]{1,0:T(8,128)(2,1)} custom-call(f32[64,768]{1,0:T(8,128)S(1)} %get-tuple-element.29.prob_ref, bf16[128,256]{1,0:T(8,128)(2,1)S(1)} %pad_maximum_fusion.1.near_ref, bf16[128,256]{1,0:T(8,128)(2,1)S(1)} %collective-permute-done.1.far_ref), custom_call_target="tpu_custom_call" | custom-call | flops 201326592 | bytes 800000 | tf_op jit(solution)/shard_map/dispatch/pallas_call | solution.py:41
  25.2 0.0 copy-start.3
  25.2 0.0 copy-start.4
  25.2 0.0 copy-start.5
  25.2 8.9 %all-to-all-start = ((bf16[32,24,256]{2,1,0:T(8,128)(2,1)}), bf16[32,24,256]{2,1,0:T(8,128)(2,1)S(1)}, u32[]{:S(2)}, u32[]{:S(2)}) async-start(bf16[32,24,256]{2,1,0:T(8,128)(2,1)} %bitcast.3), calls=%async_computation | async-start | bytes 786432 | tf_op jit(solution)/shard_map/dispatch/all_to_all | solution.py:339
  34.1 0.0 copy-done.10
  34.1 0.1 copy.23
  34.3 0.0 copy-done.8
  34.3 0.0 copy-done.9
  34.3 0.1 pad_maximum_fusion.w0
  34.4 3.1 %collective-permute-start.3 = (bf16[3,128,768]{2,1,0:T(8,128)(2,1)S(1)}, bf16[3,128,768]{2,1,0:T(8,128)(2,1)S(1)}, u32[]{:S(2)}, u32[]{:S(2)}) collective-permute-start(bf16[3,128,768]{2,1,0:T(8,128)(2,1)S(1)} %pad_maximum_fusion.w0), channel_id=1, source_target_pairs={{0,64},{64,0},{1,65},{65,1},{2,66},{66,2},{3,67},{67,3},{4,68},{68... | collective-permute-start | bytes 1769480 | tf_op jit(solution)/shard_map/weights_to_quad/ppermute | solution.py:320
  37.5 4.0 %collective-permute-start.2 = (bf16[3,128,768]{2,1,0:T(8,128)(2,1)S(1)}, bf16[3,128,768]{2,1,0:T(8,128)(2,1)S(1)}, u32[]{:S(2)}, u32[]{:S(2)}) collective-permute-start(bf16[3,128,768]{2,1,0:T(8,128)(2,1)S(1)} %pad_maximum_fusion.w0), channel_id=1, source_target_pairs={{0,32},{32,0},{1,33},{33,1},{2,34},{34,2},{3,35},{35,3},{4,36},{36... | collective-permute-start | bytes 1769480 | tf_op jit(solution)/shard_map/weights_to_quad/ppermute | solution.py:321
  41.5 7.9 %collective-permute-done.3.w2 = bf16[3,128,768]{2,1,0:T(8,128)(2,1)S(1)} collective-permute-done((bf16[3,128,768]{2,1,0:T(8,128)(2,1)S(1)}, bf16[3,128,768]{2,1,0:T(8,128)(2,1)S(1)}, u32[]{:S(2)}, u32[]{:S(2)}) %collective-permute-start.3) | collective-permute-done | bytes 589856 | tf_op jit(solution)/shard_map/weights_to_quad/ppermute | solution.py:320
  49.4 4.5 %collective-permute-start.4 = (bf16[3,128,768]{2,1,0:T(8,128)(2,1)S(1)}, bf16[3,128,768]{2,1,0:T(8,128)(2,1)S(1)}, u32[]{:S(2)}, u32[]{:S(2)}) collective-permute-start(bf16[3,128,768]{2,1,0:T(8,128)(2,1)S(1)} %collective-permute-done.3.w2), channel_id=1, source_target_pairs={{0,32},{32,0},{1,33},{33,1},{2,34},{34,2},{3,35},{35,3},{4,36},{36... | collective-permute-start | bytes 1769480 | tf_op jit(solution)/shard_map/weights_to_quad/ppermute | solution.py:322
  53.9 0.0 copy-done.3
  53.9 0.0 copy-done.4
  53.9 0.0 copy-done.5
  54.0 0.0 collective-permute-done.2.w1
  54.0 1.5 collective-permute-done.4.w3
  55.5 4.0 %all-to-all-done = bf16[32,24,256]{2,1,0:T(8,128)(2,1)S(1)} async-done(((bf16[32,24,256]{2,1,0:T(8,128)(2,1)}), bf16[32,24,256]{2,1,0:T(8,128)(2,1)S(1)}, u32[]{:S(2)}, u32[]{:S(2)}) %all-to-all-start) | async-done | bytes 393248 | tf_op jit(solution)/shard_map/dispatch/all_to_all | solution.py:339
  59.5 2.1 %partial_sums.1 = (bf16[192,2304]{1,0:T(8,128)(2,1)}, bf16[192,512]{1,0:T(8,128)(2,1)}, bf16[192,512]{1,0:T(8,128)(2,1)}) custom-call(bf16[768,256]{1,0:T(8,128)(2,1)S(1)} %bitcast.29, bf16[3,128,768]{2,1,0:T(8,128)(2,1)S(1)} %pad_maximum_fusion.w0, bf16[3,128,768]{2,1,0:T(8,128)(2,1)S(1)} %collective-permute-done.2.w1, ...), custom_call_target="tpu_custom_call" | custom-call | flops 452984832 | bytes 4000000 | tf_op jit(solution)/shard_map/partial_sums/pallas_call | solution.py:178
  61.6 6.6 %all-to-all-start.1 = ((bf16[8,24,2304]{2,1,0:T(8,128)(2,1)}), bf16[8,24,2304]{2,1,0:T(8,128)(2,1)S(1)}, u32[]{:S(2)}, u32[]{:S(2)}) async-start(bf16[8,24,2304]{2,1,0:T(8,128)(2,1)} %bitcast.36), calls=%async_computation.1 | async-start | bytes 1769472 | tf_op jit(solution)/shard_map/partial_sums/all_to_all | solution.py:348
  68.2 3.0 %collective-permute-start.5 = (f32[576,128]{1,0:T(8,128)S(1)}, f32[576,128]{1,0:T(8,128)S(1)}, u32[]{:S(2)}, u32[]{:S(2)}) collective-permute-start(f32[576,128]{1,0:T(8,128)S(1)} %relocate.2.state_ref), channel_id=1, source_target_pairs={{0,16},{16,0},{1,17},{17,1},{2,18},{18,2},{3,19},{19,3},{4,20},{20... | collective-permute-start | bytes 884744 | tf_op jit(solution)/shard_map/partial_sums/ppermute | solution.py:349
  71.2 8.2 %collective-permute-done.5.partner_ref = f32[576,128]{1,0:T(8,128)S(1)} collective-permute-done((f32[576,128]{1,0:T(8,128)S(1)}, f32[576,128]{1,0:T(8,128)S(1)}, u32[]{:S(2)}, u32[]{:S(2)}) %collective-permute-start.5) | collective-permute-done | bytes 294944 | tf_op jit(solution)/shard_map/partial_sums/ppermute | solution.py:349
  79.4 0.0 copy-start.1
  79.4 0.7 copy-done.1
  80.1 12.0 %all-to-all-done.1 = bf16[8,24,2304]{2,1,0:T(8,128)(2,1)S(1)} async-done(((bf16[8,24,2304]{2,1,0:T(8,128)(2,1)}), bf16[8,24,2304]{2,1,0:T(8,128)(2,1)S(1)}, u32[]{:S(2)}, u32[]{:S(2)}) %all-to-all-start.1) | async-done | bytes 884768 | tf_op jit(solution)/shard_map/partial_sums/all_to_all | solution.py:348
  92.1 1.1 activation.1
  93.2 23.0 %all_to_all.50 = bf16[8,24,2304]{2,1,0:T(8,128)(2,1)S(1)} all-to-all(bf16[8,24,2304]{2,1,0:T(8,128)(2,1)} %bitcast.34), channel_id=1, replica_groups=mesh['x_lo'=2,'y1'=4,'y0'=2,'core'=2,'x_hi'=2,'z'=16] {'x_lo','y1'}, dimensions={0} | all-to-all | bytes 1769472 | tf_op jit(solution)/shard_map/activation/all_to_all | solution.py:356
  116.2 2.6 %slot_outputs.1 = bf16[768,256]{1,0:T(8,128)(2,1)} custom-call(bf16[192,2304]{1,0:T(8,128)(2,1)S(1)} %bitcast.26, bf16[3,128,768]{2,1,0:T(8,128)(2,1)S(1)} %pad_maximum_fusion.w0, bf16[3,128,768]{2,1,0:T(8,128)(2,1)S(1)} %collective-permute-done.2.w1, bf16[3,128,768]{2,1,0:T(8,128)(2,1)S(1)} %collective-permute-done.3.w2, ...), custom_call_target="tpu_custom_call" | custom-call | flops 452984832 | bytes 4000000 | tf_op jit(solution)/shard_map/slot_outputs/pallas_call | solution.py:41
  118.8 15.5 %all-to-all-start.3 = ((bf16[32,24,256]{2,1,0:T(8,128)(2,1)}), bf16[32,24,256]{2,1,0:T(8,128)(2,1)S(1)}, u32[]{:S(2)}, u32[]{:S(2)}) async-start(bf16[32,24,256]{2,1,0:T(8,128)(2,1)} %bitcast.35), calls=%async_computation.3 | async-start | bytes 786432 | tf_op jit(solution)/shard_map/slot_outputs/all_to_all | solution.py:367
  134.3 0.0 copy-start.6
  134.3 0.9 copy-done.6
  135.2 0.0 copy-start.7
  135.2 0.9 copy-done.7
  136.2 0.8 weight_grads.3
  137.0 3.0 %collective-permute-start.6 = (bf16[2,3,128,768]{3,2,1,0:T(8,128)(2,1)S(1)}, bf16[2,3,128,768]{3,2,1,0:T(8,128)(2,1)S(1)}, u32[]{:S(2)}, u32[]{:S(2)}) collective-permute-start(bf16[2,3,128,768]{3,2,1,0:T(8,128)(2,1)S(1)} %get-tuple-element.40), channel_id=1, source_target_pairs={{0,32},{32,0},{1,33},{33,1},{2,34},{34,2},{3,35},{35,3},{4,36},{36... | collective-permute-start | bytes 3538952 | tf_op jit(solution)/shard_map/weight_grads/ppermute | solution.py:377
  140.0 2.5 %collective-permute-done.6.near_ref = bf16[2,3,128,768]{3,2,1,0:T(8,128)(2,1)S(1)} collective-permute-done((bf16[2,3,128,768]{3,2,1,0:T(8,128)(2,1)S(1)}, bf16[2,3,128,768]{3,2,1,0:T(8,128)(2,1)S(1)}, u32[]{:S(2)}, u32[]{:S(2)}) %collective-permute-start.6) | collective-permute-done | bytes 1179680 | tf_op jit(solution)/shard_map/weight_grads/ppermute | solution.py:377
  142.5 0.0 copy-start.2
  142.5 1.2 weight_grads.4
  143.7 0.0 copy-start
  143.7 2.0 %collective-permute-start.7 = (bf16[3,128,768]{2,1,0:T(8,128)(2,1)S(1)}, bf16[3,128,768]{2,1,0:T(8,128)(2,1)S(1)}, u32[]{:S(2)}, u32[]{:S(2)}) collective-permute-start(bf16[3,128,768]{2,1,0:T(8,128)(2,1)S(1)} %get-tuple-element.42), channel_id=1, source_target_pairs={{0,64},{64,0},{1,65},{65,1},{2,66},{66,2},{3,67},{67,3},{4,68},{68... | collective-permute-start | bytes 1769480 | tf_op jit(solution)/shard_map/weight_grads/ppermute | solution.py:383
  145.7 15.1 %all-to-all-done.3 = bf16[32,24,256]{2,1,0:T(8,128)(2,1)S(1)} async-done(((bf16[32,24,256]{2,1,0:T(8,128)(2,1)}), bf16[32,24,256]{2,1,0:T(8,128)(2,1)S(1)}, u32[]{:S(2)}, u32[]{:S(2)}) %all-to-all-start.3) | async-done | bytes 393248 | tf_op jit(solution)/shard_map/slot_outputs/all_to_all | solution.py:367
  160.8 2.2 %combine.1 = bf16[4,64,256]{2,1,0:T(8,128)(2,1)} custom-call(s32[1]{0:T(128)} %bitcast.q_ref, bf16[768,256]{1,0:T(8,128)(2,1)S(1)} %bitcast.30, f32[64,768]{1,0:T(8,128)} %get-tuple-element.35.prob_ref), custom_call_target="tpu_custom_call" | custom-call | flops 201326592 | bytes 800000 | tf_op jit(solution)/shard_map/combine/pallas_call | solution.py:41
  162.9 6.3 %all-to-all-start.4 = ((bf16[4,64,256]{2,1,0:T(8,128)(2,1)}), bf16[4,64,256]{2,1,0:T(8,128)(2,1)S(1)}, u32[]{:S(2)}, u32[]{:S(2)}) async-start(bf16[4,64,256]{2,1,0:T(8,128)(2,1)} %combine.1), calls=%async_computation.4 | async-start | bytes 262144 | tf_op jit(solution)/shard_map/combine/all_to_all | solution.py:400
  169.9 0.0 copy-done.2
  169.9 0.7 relocate.3
  170.6 2.2 %all-to-all-done.4 = bf16[4,64,256]{2,1,0:T(8,128)(2,1)S(1)} async-done(((bf16[4,64,256]{2,1,0:T(8,128)(2,1)}), bf16[4,64,256]{2,1,0:T(8,128)(2,1)S(1)}, u32[]{:S(2)}, u32[]{:S(2)}) %all-to-all-start.4) | async-done | bytes 131104 | tf_op jit(solution)/shard_map/combine/all_to_all | solution.py:400
  172.9 0.6 fusion
  173.5 0.0 collective-permute-done.7.other_ref
  173.5 0.0 copy-done
  173.5 1.0 weight_grads.5
  (3 shorter events, 0.0 us)
Async XLA Ops:
  0.6 33.5 %copy-start.10 = (bf16[1,768,128]{2,1,0:T(8,128)(2,1)S(1)}, bf16[1,768,128]{2,1,0:T(8,128)(2,1)}, u32[]{:S(2)}) copy-start(bf16[1,768,128]{2,1,0:T(8,128)(2,1)} %param.17) | copy-start | bytes 589828
  0.6 33.6 %copy-start.8 = (bf16[1,128,768]{2,1,0:T(8,128)(2,1)S(1)}, bf16[1,128,768]{2,1,0:T(8,128)(2,1)}, u32[]{:S(2)}) copy-start(bf16[1,128,768]{2,1,0:T(8,128)(2,1)} %param.16) | copy-start | bytes 589828
  0.7 33.6 %copy-start.9 = (bf16[1,128,768]{2,1,0:T(8,128)(2,1)S(1)}, bf16[1,128,768]{2,1,0:T(8,128)(2,1)}, u32[]{:S(2)}) copy-start(bf16[1,128,768]{2,1,0:T(8,128)(2,1)} %param.15) | copy-start | bytes 589828
  1.5 16.9 %collective-permute-start = (bf16[64,256]{1,0:T(8,128)(2,1)S(1)}, bf16[64,256]{1,0:T(8,128)(2,1)S(1)}, u32[]{:S(2)}, u32[]{:S(2)}) collective-permute-start(bf16[64,256]{1,0:T(8,128)(2,1)S(1)} %tokens_to_quad.1), channel_id=1, source_target_pairs={{0,32},{32,0},{1,33},{33,1},{2,34},{34,2},{3,35},{35,3},{4,36},{36... | collective-permute-start | bytes 98312 | tf_op jit(solution)/shard_map/tokens_to_quad/ppermute | solution.py:315
  18.4 5.0 %collective-permute-start.1 = (bf16[128,256]{1,0:T(8,128)(2,1)S(1)}, bf16[128,256]{1,0:T(8,128)(2,1)S(1)}, u32[]{:S(2)}, u32[]{:S(2)}) collective-permute-start(bf16[128,256]{1,0:T(8,128)(2,1)S(1)} %pad_maximum_fusion.1.near_ref), channel_id=1, source_target_pairs={{0,64},{64,0},{1,65},{65,1},{2,66},{66,2},{3,67},{67,3},{4,68},{68... | collective-permute-start | bytes 196616 | tf_op jit(solution)/shard_map/tokens_to_quad/ppermute | solution.py:316
  25.2 28.7 %copy-start.3 = (f32[1,12,2048]{2,0,1:T(1,128)S(1)}, f32[1,12,2048]{2,0,1:T(1,128)}, u32[]{:S(2)}) copy-start(f32[1,12,2048]{2,0,1:T(1,128)} %param.19) | copy-start | bytes 294916
  25.2 28.7 %copy-start.4 = (f32[1,12,2048]{2,0,1:T(1,128)S(1)}, f32[1,12,2048]{2,0,1:T(1,128)}, u32[]{:S(2)}) copy-start(f32[1,12,2048]{2,0,1:T(1,128)} %param.20) | copy-start | bytes 294916
  25.2 28.7 %copy-start.5 = (f32[1,12,2048]{2,0,1:T(1,128)S(1)}, f32[1,12,2048]{2,0,1:T(1,128)}, u32[]{:S(2)}) copy-start(f32[1,12,2048]{2,0,1:T(1,128)} %param.21) | copy-start | bytes 294916
  25.2 34.3 %all-to-all-start = ((bf16[32,24,256]{2,1,0:T(8,128)(2,1)}), bf16[32,24,256]{2,1,0:T(8,128)(2,1)S(1)}, u32[]{:S(2)}, u32[]{:S(2)}) async-start(bf16[32,24,256]{2,1,0:T(8,128)(2,1)} %bitcast.3), calls=%async_computation | async-start | bytes 786432 | tf_op jit(solution)/shard_map/dispatch/all_to_all | solution.py:339
  34.4 15.0 %collective-permute-start.3 = (bf16[3,128,768]{2,1,0:T(8,128)(2,1)S(1)}, bf16[3,128,768]{2,1,0:T(8,128)(2,1)S(1)}, u32[]{:S(2)}, u32[]{:S(2)}) collective-permute-start(bf16[3,128,768]{2,1,0:T(8,128)(2,1)S(1)} %pad_maximum_fusion.w0), channel_id=1, source_target_pairs={{0,64},{64,0},{1,65},{65,1},{2,66},{66,2},{3,67},{67,3},{4,68},{68... | collective-permute-start | bytes 1769480 | tf_op jit(solution)/shard_map/weights_to_quad/ppermute | solution.py:320
  37.5 16.5 %collective-permute-start.2 = (bf16[3,128,768]{2,1,0:T(8,128)(2,1)S(1)}, bf16[3,128,768]{2,1,0:T(8,128)(2,1)S(1)}, u32[]{:S(2)}, u32[]{:S(2)}) collective-permute-start(bf16[3,128,768]{2,1,0:T(8,128)(2,1)S(1)} %pad_maximum_fusion.w0), channel_id=1, source_target_pairs={{0,32},{32,0},{1,33},{33,1},{2,34},{34,2},{3,35},{35,3},{4,36},{36... | collective-permute-start | bytes 1769480 | tf_op jit(solution)/shard_map/weights_to_quad/ppermute | solution.py:321
  49.4 6.1 %collective-permute-start.4 = (bf16[3,128,768]{2,1,0:T(8,128)(2,1)S(1)}, bf16[3,128,768]{2,1,0:T(8,128)(2,1)S(1)}, u32[]{:S(2)}, u32[]{:S(2)}) collective-permute-start(bf16[3,128,768]{2,1,0:T(8,128)(2,1)S(1)} %collective-permute-done.3.w2), channel_id=1, source_target_pairs={{0,32},{32,0},{1,33},{33,1},{2,34},{34,2},{3,35},{35,3},{4,36},{36... | collective-permute-start | bytes 1769480 | tf_op jit(solution)/shard_map/weights_to_quad/ppermute | solution.py:322
  61.6 30.5 %all-to-all-start.1 = ((bf16[8,24,2304]{2,1,0:T(8,128)(2,1)}), bf16[8,24,2304]{2,1,0:T(8,128)(2,1)S(1)}, u32[]{:S(2)}, u32[]{:S(2)}) async-start(bf16[8,24,2304]{2,1,0:T(8,128)(2,1)} %bitcast.36), calls=%async_computation.1 | async-start | bytes 1769472 | tf_op jit(solution)/shard_map/partial_sums/all_to_all | solution.py:348
  68.2 11.2 %collective-permute-start.5 = (f32[576,128]{1,0:T(8,128)S(1)}, f32[576,128]{1,0:T(8,128)S(1)}, u32[]{:S(2)}, u32[]{:S(2)}) collective-permute-start(f32[576,128]{1,0:T(8,128)S(1)} %relocate.2.state_ref), channel_id=1, source_target_pairs={{0,16},{16,0},{1,17},{17,1},{2,18},{18,2},{3,19},{19,3},{4,20},{20... | collective-permute-start | bytes 884744 | tf_op jit(solution)/shard_map/partial_sums/ppermute | solution.py:349
  79.4 0.7 copy-start.1
  118.8 42.0 %all-to-all-start.3 = ((bf16[32,24,256]{2,1,0:T(8,128)(2,1)}), bf16[32,24,256]{2,1,0:T(8,128)(2,1)S(1)}, u32[]{:S(2)}, u32[]{:S(2)}) async-start(bf16[32,24,256]{2,1,0:T(8,128)(2,1)} %bitcast.35), calls=%async_computation.3 | async-start | bytes 786432 | tf_op jit(solution)/shard_map/slot_outputs/all_to_all | solution.py:367
  134.3 0.9 copy-start.6
  135.2 0.9 copy-start.7
  137.0 5.5 %collective-permute-start.6 = (bf16[2,3,128,768]{3,2,1,0:T(8,128)(2,1)S(1)}, bf16[2,3,128,768]{3,2,1,0:T(8,128)(2,1)S(1)}, u32[]{:S(2)}, u32[]{:S(2)}) collective-permute-start(bf16[2,3,128,768]{3,2,1,0:T(8,128)(2,1)S(1)} %get-tuple-element.40), channel_id=1, source_target_pairs={{0,32},{32,0},{1,33},{33,1},{2,34},{34,2},{3,35},{35,3},{4,36},{36... | collective-permute-start | bytes 3538952 | tf_op jit(solution)/shard_map/weight_grads/ppermute | solution.py:377
  142.5 27.4 %copy-start.2 = (f32[576,128]{1,0:T(8,128)S(1)}, f32[576,128]{1,0:T(8,128)}, u32[]{:S(2)}) copy-start(f32[576,128]{1,0:T(8,128)} %copy-done.1) | copy-start | bytes 884740
  143.7 29.8 %copy-start = (f32[3,128,768]{2,1,0:T(8,128)S(1)}, f32[3,128,768]{2,1,0:T(8,128)}, u32[]{:S(2)}) copy-start(f32[3,128,768]{2,1,0:T(8,128)} %get-tuple-element.41.kept_ref) | copy-start | bytes 3538948
  143.7 29.8 %collective-permute-start.7 = (bf16[3,128,768]{2,1,0:T(8,128)(2,1)S(1)}, bf16[3,128,768]{2,1,0:T(8,128)(2,1)S(1)}, u32[]{:S(2)}, u32[]{:S(2)}) collective-permute-start(bf16[3,128,768]{2,1,0:T(8,128)(2,1)S(1)} %get-tuple-element.42), channel_id=1, source_target_pairs={{0,64},{64,0},{1,65},{65,1},{2,66},{66,2},{3,67},{67,3},{4,68},{68... | collective-permute-start | bytes 1769480 | tf_op jit(solution)/shard_map/weight_grads/ppermute | solution.py:383
  162.9 9.9 %all-to-all-start.4 = ((bf16[4,64,256]{2,1,0:T(8,128)(2,1)}), bf16[4,64,256]{2,1,0:T(8,128)(2,1)S(1)}, u32[]{:S(2)}, u32[]{:S(2)}) async-start(bf16[4,64,256]{2,1,0:T(8,128)(2,1)} %combine.1), calls=%async_computation.4 | async-start | bytes 262144 | tf_op jit(solution)/shard_map/combine/all_to_all | solution.py:400

commit v6 on v5

--- a/solution.py
+++ b/solution.py
@@ -67,27 +67,28 @@
     return lax.dot_general(a, b, (dims, ((), ())), preferred_element_type=F32)
 
 
-def join_kernel(a_ref, b_ref, out_ref, sem_a, sem_b):
-    copies = [
-        pltpu.make_async_copy(a_ref, out_ref.at[:, :BLK], sem_a),
-        pltpu.make_async_copy(b_ref, out_ref.at[:, BLK:], sem_b),
-    ]
+def blocks_kernel(a_ref, b_ref, out_ref, sems):
+    copies = []
+    for d in range(QUADS):
+        rows = slice(d * TOK, (d + 1) * TOK)
+        copies.append(pltpu.make_async_copy(a_ref, out_ref.at[rows, :BLK], sems.at[2 * d]))
+        copies.append(pltpu.make_async_copy(b_ref, out_ref.at[rows, BLK:], sems.at[2 * d + 1]))
     for copy in copies:
         copy.start()
     for copy in copies:
         copy.wait()
 
 
-def join(a, b):
+def blocks(a, b):
     hbm = pl.BlockSpec(memory_space=pltpu.HBM)
     return pl.pallas_call(
-        join_kernel,
-        out_shape=shape_of(TOK, 2 * BLK),
+        blocks_kernel,
+        out_shape=far_shape(QUADS * TOK, 2 * BLK),
         in_specs=[hbm, hbm],
-        out_specs=pl.BlockSpec(memory_space=pltpu.VMEM),
-        scratch_shapes=[pltpu.SemaphoreType.DMA, pltpu.SemaphoreType.DMA],
+        out_specs=hbm,
+        scratch_shapes=[pltpu.SemaphoreType.DMA((2 * QUADS,))],
         compiler_params=PARAMS,
-        cost_estimate=pl.CostEstimate(flops=0, bytes_accessed=65536, transcendentals=0),
+        cost_estimate=pl.CostEstimate(flops=0, bytes_accessed=262144, transcendentals=0),
     )(far(a), far(b))
 
 
@@ -116,7 +117,7 @@
     prob_again[...] = prob
 
 
-def dispatch_kernel(prob_ref, near_ref, far_ref, pay_ref):
+def dispatch_kernel(q_ref, prob_ref, tok_ref, pay_ref):
     shape = (TOK, WIDE)
     _, member, _ = row_fields(shape, 1)
     prob = prob_ref[...]
@@ -127,10 +128,9 @@
     dy = jnp.zeros((WIDE, BLK), F32)
     zero = jnp.zeros(shape, BF16)
     for d in range(QUADS):
-        source = near_ref if d < 2 else far_ref
-        lo = (d % 2) * TOK
-        x_tok = source[lo : lo + TOK, :BLK]
-        dy_tok = source[lo : lo + TOK, BLK:]
+        rows = pl.ds(pl.multiple_of((q_ref[0] ^ d) * TOK, TOK), TOK)
+        x_tok = tok_ref[rows, :BLK]
+        dy_tok = tok_ref[rows, BLK:]
         x = x + dot(masks[d], x_tok, ((0,), (0,)))
         for part in parts:
             dy = dy + dot(jnp.where(member == d, part, zero), dy_tok, ((0,), (0,)))
@@ -275,16 +275,23 @@
         out_ref[q ^ d] = jnp.concatenate([mixed, grad], axis=1).astype(BF16)
 
 
-def stack_kernel(a_ref, b_ref, c_ref, out_ref):
-    for k, ref in enumerate((a_ref, b_ref, c_ref)):
-        out_ref[k * NEXT : (k + 1) * NEXT] = ref[...]
-
-
-def select_kernel(moving_ref, partner_ref, state_ref, a_ref, b_ref, c_ref):
+def stack_kernel(a_ref, b_ref, c_ref, low_ref, high_ref):
+    half = NEXT // 2
+    low_ref[:NEXT] = a_ref[...]
+    low_ref[NEXT:] = b_ref[:half]
+    high_ref[:half] = b_ref[half:]
+    high_ref[half:] = c_ref[...]
+
+
+def select_kernel(moving_ref, low_new, high_new, low_old, high_old, a_ref, b_ref, c_ref):
+    half = NEXT // 2
     moving = moving_ref[0] != 0
-    for k, ref in enumerate((a_ref, b_ref, c_ref)):
-        rows = slice(k * NEXT, (k + 1) * NEXT)
-        ref[...] = jnp.where(moving, partner_ref[rows], state_ref[rows])
+    low = jnp.where(moving, low_new[...], low_old[...])
+    high = jnp.where(moving, high_new[...], high_old[...])
+    a_ref[...] = low[:NEXT]
+    b_ref[:half] = low[NEXT:]
+    b_ref[half:] = high[:half]
+    c_ref[...] = high[half:]
 
 
 def shape_of(*dims, dtype=BF16):
@@ -311,9 +318,9 @@
     quad = (lax.axis_index("y0") * 2 + lax.axis_index("core")).astype(jnp.int32).reshape(1)
 
     with jax.named_scope("tokens_to_quad"):
-        mine = join(tokens, grad_out)
-        near = jnp.concatenate([mine, lax.ppermute(mine, "core", SWAP)], axis=0)
-        far_tokens = lax.ppermute(near, "y0", SWAP)
+        shared = lax.all_to_all(
+            blocks(tokens, grad_out), QUAD, split_axis=0, concat_axis=0, tiled=True
+        )
 
     with jax.named_scope("weights_to_quad"):
         w0 = jnp.stack([w_gate[0], w_up[0], w_down[0].T])
@@ -332,7 +339,7 @@
         pay = call(
             dispatch_kernel,
             shape_of(WIDE, 2 * BLK),
-            (prob, near, far_tokens),
+            (quad, prob, shared),
             flops=2 * 16 * TOK * WIDE * BLK,
             moved=800000,
         )
@@ -340,20 +347,24 @@
 
     with jax.named_scope("relocate"):
         mine_next = [v.reshape(NEXT, BLK) for v in (next_master, next_first, next_second)]
-        state = call(stack_kernel, shape_of(3 * NEXT, BLK, dtype=F32), mine_next, moved=600000)
+        halves = [shape_of(3 * NEXT // 2, BLK, dtype=F32)] * 2
+        low, high = call(stack_kernel, halves, mine_next, moved=600000)
 
     with jax.named_scope("partial_sums"):
         sums, x_rows, dy_rows = partial_sums(got, w0, w1, w2, w3)
-        sums, state = lax.optimization_barrier((sums, state))
+        sums, low = lax.optimization_barrier((sums, low))
         parts = lax.all_to_all(sums, SUMS, split_axis=0, concat_axis=0, tiled=True)
-        partner = lax.ppermute(state, "x_hi", SWAP)
-        parts, partner = lax.optimization_barrier((parts, partner))
+        low_new = lax.ppermute(low, "x_hi", SWAP)
+        parts, low_new = lax.optimization_barrier((parts, low_new))
 
     with jax.named_scope("activation"):
         hidden = call(
             act_kernel, far_shape(ROWS, 3 * FF), (parts,), flops=4000000, moved=1000000
         )
+        hidden, high = lax.optimization_barrier((hidden, high))
         whole = lax.all_to_all(hidden, SUMS, split_axis=0, concat_axis=0, tiled=True)
+        high_new = lax.ppermute(high, "x_hi", SWAP)
+        whole, high_new = lax.optimization_barrier((whole, high_new))
 
     with jax.named_scope("slot_outputs"):
         back = call(
@@ -366,6 +377,15 @@
         back, whole = lax.optimization_barrier((back, whole))
         returned = lax.all_to_all(back, EXPERT, split_axis=0, concat_axis=0, tiled=True)
 
+    with jax.named_scope("relocate"):
+        moving = (dest != lax.axis_index(EXPERT).astype(jnp.int32)).astype(jnp.int32)
+        moved = call(
+            select_kernel,
+            [far_shape(NEXT, BLK, dtype=F32)] * 3,
+            (moving, low_new, high_new, low, high),
+            moved=1200000,
+        )
+
     with jax.named_scope("weight_grads"):
         keep, send = call(
             grad_kernel,
@@ -380,6 +400,7 @@
             (far_shape(3, BLK, FF, dtype=F32), shape_of(3, BLK, FF)),
             (keep, near_part),
         )
+        passed, moved = lax.optimization_barrier((passed, moved))
         other = lax.ppermute(passed, "y0", SWAP)
         grads = call(
             add_far_kernel,
@@ -401,25 +422,13 @@
         mixes = jnp.sum(mixes.astype(F32), axis=0).astype(BF16)
         mixed, token_grad = mixes[:, :BLK], mixes[:, BLK:]
 
-    with jax.named_scope("relocate"):
-        moving = (dest != lax.axis_index(EXPERT).astype(jnp.int32)).astype(jnp.int32)
-        moved = call(
-            select_kernel,
-            [shape_of(NEXT, BLK, dtype=F32)] * 3,
-            (moving, partner, state),
-            moved=1200000,
-        )
-        moved = [v.reshape(next_master.shape) for v in moved]
-
     return (
         mixed,
         token_grad,
         grads[0][None],
         grads[1][None],
         grads[2][None],
-        moved[0],
-        moved[1],
-        moved[2],
+        *[v.reshape(next_master.shape) for v in moved],
     )
 
 

time: 175 us -> 178 us (1.017)
  blocking collectives: 23 us -> 8.99 us
  starting transfers between devices: 75 us -> 83.6 us
  Pallas kernels: 16.1 us -> 20.8 us
  local copies, waits for them, and re-layouts: 3.38 us -> 7.05 us
    ppermute x3 -> x2, starting transfers between devices: 21 us -> 4.66 us  [the longest x1 2.76 us: shards(): low_new = lax.ppermute(low, 'x_hi', SWAP)]
    all_to_all x1 -> x2, starting transfers between devices: 6.3 us -> 22.1 us  [the longest x1 17.5 us: shards(): lax.all_to_all(blocks(tokens, grad_out), QUAD, split_axis=0, concat_axis=...]
    all_to_all x1, blocking collectives: 23 us -> 8.99 us  [shards(): mixes = lax.all_to_all(mixes, QUAD, split_axis=0, concat_axis=0, tiled=True)]
    all_to_all x1, starting transfers between devices: 15.5 us -> 26.5 us  [shards(): lax.all_to_all(back, EXPERT, split_axis=0, concat_axis=0, tiled=True)]
    ppermute x3 -> x2, waiting for transfers between devices: 10.2 us -> 16.4 us  [the longest x1 8.66 us: shards(): high_new = lax.ppermute(high, 'x_hi', SWAP)]
    all_to_all x1, waiting for transfers between devices: 12 us -> 6.86 us  [shards(): parts = lax.all_to_all(sums, SUMS, split_axis=0, concat_axis=0, tiled=True)]
    pallas_call x1, Pallas kernels: 0.81 us -> 5.14 us  [blocks(): pl.pallas_call(blocks_kernel, out_shape=far_shape(QUADS * TOK, 2 * BLK),...]
    all_to_all x1, waiting for transfers between devices: 15.1 us -> 10.7 us  [shards(): lax.all_to_all(back, EXPERT, split_axis=0, concat_axis=0, tiled=True)]
where the time goes in v6:
time: 178 us
  starting transfers between devices  83.6 us (47%)
  waiting for transfers between devices  55.5 us (31%)
  Pallas kernels  20.8 us (12%)
  blocking collectives  8.99 us (5%)
  local copies, waits for them, and re-layouts  7.05 us (4%)
    all_to_all x1, starting transfers between devices, shards(): lax.all_to_all(back, EXPERT, split_axis=0, concat_axis=0, tiled=True)  26.5 us
    all_to_all x1, starting transfers between devices, shards(): lax.all_to_all(blocks(tokens, grad_out), QUAD, split_axis=0, concat_axis=...  17.5 us
    pallas_call x10, Pallas kernels, call(): pl.pallas_call(kernel, out_shape=out_shape, in_specs=[smem if o.dtype ==...  13.6 us
    all_to_all x1, waiting for transfers between devices, shards(): lax.all_to_all(back, EXPERT, split_axis=0, concat_axis=0, tiled=True)  10.7 us
    ppermute x1, waiting for transfers between devices, shards(): w2 = lax.ppermute(w0, 'y0', SWAP)  9.88 us
    all_to_all x1, blocking collectives, shards(): mixes = lax.all_to_all(mixes, QUAD, split_axis=0, concat_axis=0, tiled=True)  8.99 us
    all_to_all x1, starting transfers between devices, shards(): got = lax.all_to_all(pay, EXPERT, split_axis=0, concat_axis=0, tiled=True)  8.81 us
    ppermute x1, waiting for transfers between devices, shards(): high_new = lax.ppermute(high, 'x_hi', SWAP)  8.66 us
  transfers between devices with their start and end apart: 12, of which 10 were waited for; matrix products, arithmetic and copies ran while one was open for 0% of the time, Pallas kernels for 4%

profile of v6, /device:TPU:1, one launch (start us, length us, event | category | flops | bytes accessed | tf_op | source)
XLA Modules:
  0.0 177.5 jit_solution(18027913954591514935)
XLA Ops:
  0.6 0.0 copy-start.14
  0.6 0.0 copy-start.12
  0.7 0.0 copy-start.13
  0.7 5.1 %tokens_to_quad.1 = bf16[256,256]{1,0:T(8,128)(2,1)} custom-call(bf16[64,128]{1,0:T(8,128)(2,1)} %a_ref.1, bf16[64,128]{1,0:T(8,128)(2,1)} %b_ref.1), custom_call_target="tpu_custom_call" | custom-call | bytes 262144 | tf_op jit(solution)/shard_map/tokens_to_quad/pallas_call | solution.py:84
  5.8 17.5 %all-to-all-start = ((bf16[4,64,256]{2,1,0:T(8,128)(2,1)}), bf16[4,64,256]{2,1,0:T(8,128)(2,1)S(1)}, u32[]{:S(2)}, u32[]{:S(2)}) async-start(bf16[4,64,256]{2,1,0:T(8,128)(2,1)} %bitcast.41), calls=%async_computation | async-start | bytes 262144 | tf_op jit(solution)/shard_map/tokens_to_quad/all_to_all | solution.py:321
  23.3 1.9 %dispatch.2 = (f32[64,768]{1,0:T(8,128)S(1)}, f32[64,768]{1,0:T(8,128)}) custom-call(s32[1]{0:T(128)} %bitcast.q_ref, s32[8,64]{1,0:T(8,128)} %bitcast.48, f32[8,64]{1,0:T(8,128)} %bitcast.49), custom_call_target="tpu_custom_call" | custom-call | flops 6291456 | bytes 300000 | tf_op jit(solution)/shard_map/dispatch/pallas_call | solution.py:41
  25.1 1.7 all-to-all-done
  26.9 1.8 %dispatch.3 = bf16[768,256]{1,0:T(8,128)(2,1)} custom-call(s32[1]{0:T(128)} %bitcast.q_ref, f32[64,768]{1,0:T(8,128)S(1)} %get-tuple-element.39.prob_ref, bf16[256,256]{1,0:T(8,128)(2,1)S(1)} %bitcast.33), custom_call_target="tpu_custom_call" | custom-call | flops 201326592 | bytes 800000 | tf_op jit(solution)/shard_map/dispatch/pallas_call | solution.py:41
  28.7 0.0 copy-start.7
  28.7 0.0 copy-start.8
  28.7 8.8 %all-to-all-start.1 = ((bf16[32,24,256]{2,1,0:T(8,128)(2,1)}), bf16[32,24,256]{2,1,0:T(8,128)(2,1)S(1)}, u32[]{:S(2)}, u32[]{:S(2)}) async-start(bf16[32,24,256]{2,1,0:T(8,128)(2,1)} %bitcast.5), calls=%async_computation.1 | async-start | bytes 786432 | tf_op jit(solution)/shard_map/dispatch/all_to_all | solution.py:346
  37.5 0.0 copy-done.14
  37.5 0.1 copy.23
  37.7 0.0 copy-done.12
  37.7 0.0 copy-done.13
  37.7 0.1 pad_maximum_fusion.w0
  37.7 2.4 %collective-permute-start.1 = (bf16[3,128,768]{2,1,0:T(8,128)(2,1)S(1)}, bf16[3,128,768]{2,1,0:T(8,128)(2,1)S(1)}, u32[]{:S(2)}, u32[]{:S(2)}) collective-permute-start(bf16[3,128,768]{2,1,0:T(8,128)(2,1)S(1)} %pad_maximum_fusion.w0), channel_id=1, source_target_pairs={{0,64},{64,0},{1,65},{65,1},{2,66},{66,2},{3,67},{67,3},{4,68},{68... | collective-permute-start | bytes 1769480 | tf_op jit(solution)/shard_map/weights_to_quad/ppermute | solution.py:327
  40.2 3.1 %collective-permute-start = (bf16[3,128,768]{2,1,0:T(8,128)(2,1)S(1)}, bf16[3,128,768]{2,1,0:T(8,128)(2,1)S(1)}, u32[]{:S(2)}, u32[]{:S(2)}) collective-permute-start(bf16[3,128,768]{2,1,0:T(8,128)(2,1)S(1)} %pad_maximum_fusion.w0), channel_id=1, source_target_pairs={{0,32},{32,0},{1,33},{33,1},{2,34},{34,2},{3,35},{35,3},{4,36},{36... | collective-permute-start | bytes 1769480 | tf_op jit(solution)/shard_map/weights_to_quad/ppermute | solution.py:328
  43.3 9.9 %collective-permute-done.1.w2 = bf16[3,128,768]{2,1,0:T(8,128)(2,1)S(1)} collective-permute-done((bf16[3,128,768]{2,1,0:T(8,128)(2,1)S(1)}, bf16[3,128,768]{2,1,0:T(8,128)(2,1)S(1)}, u32[]{:S(2)}, u32[]{:S(2)}) %collective-permute-start.1) | collective-permute-done | bytes 589856 | tf_op jit(solution)/shard_map/weights_to_quad/ppermute | solution.py:327
  53.1 4.1 %collective-permute-start.2 = (bf16[3,128,768]{2,1,0:T(8,128)(2,1)S(1)}, bf16[3,128,768]{2,1,0:T(8,128)(2,1)S(1)}, u32[]{:S(2)}, u32[]{:S(2)}) collective-permute-start(bf16[3,128,768]{2,1,0:T(8,128)(2,1)S(1)} %collective-permute-done.1.w2), channel_id=1, source_target_pairs={{0,32},{32,0},{1,33},{33,1},{2,34},{34,2},{3,35},{35,3},{4,36},{36... | collective-permute-start | bytes 1769480 | tf_op jit(solution)/shard_map/weights_to_quad/ppermute | solution.py:329
  57.3 0.0 copy-done.7
  57.3 0.0 copy-done.8
  57.3 0.0 copy-done.9
  57.4 0.0 collective-permute-done.w1
  57.4 1.5 collective-permute-done.2.w3
  58.9 4.6 %all-to-all-done.1 = bf16[32,24,256]{2,1,0:T(8,128)(2,1)S(1)} async-done(((bf16[32,24,256]{2,1,0:T(8,128)(2,1)}), bf16[32,24,256]{2,1,0:T(8,128)(2,1)S(1)}, u32[]{:S(2)}, u32[]{:S(2)}) %all-to-all-start.1) | async-done | bytes 393248 | tf_op jit(solution)/shard_map/dispatch/all_to_all | solution.py:346
  63.5 2.1 %partial_sums.1 = (bf16[192,2304]{1,0:T(8,128)(2,1)}, bf16[192,512]{1,0:T(8,128)(2,1)}, bf16[192,512]{1,0:T(8,128)(2,1)}) custom-call(bf16[768,256]{1,0:T(8,128)(2,1)S(1)} %bitcast.31, bf16[3,128,768]{2,1,0:T(8,128)(2,1)S(1)} %pad_maximum_fusion.w0, bf16[3,128,768]{2,1,0:T(8,128)(2,1)S(1)} %collective-permute-done.w1, ...), custom_call_target="tpu_custom_call" | custom-call | flops 452984832 | bytes 4000000 | tf_op jit(solution)/shard_map/partial_sums/pallas_call | solution.py:178
  65.6 6.8 %all-to-all-start.2 = ((bf16[8,24,2304]{2,1,0:T(8,128)(2,1)}), bf16[8,24,2304]{2,1,0:T(8,128)(2,1)S(1)}, u32[]{:S(2)}, u32[]{:S(2)}) async-start(bf16[8,24,2304]{2,1,0:T(8,128)(2,1)} %bitcast.39), calls=%async_computation.2 | async-start | bytes 1769472 | tf_op jit(solution)/shard_map/partial_sums/all_to_all | solution.py:356
  72.5 2.8 %collective-permute-start.3 = (f32[288,128]{1,0:T(8,128)S(1)}, f32[288,128]{1,0:T(8,128)S(1)}, u32[]{:S(2)}, u32[]{:S(2)}) collective-permute-start(f32[288,128]{1,0:T(8,128)S(1)} %get-tuple-element.43.low_old), channel_id=1, source_target_pairs={{0,16},{16,0},{1,17},{17,1},{2,18},{18,2},{3,19},{19,3},{4,20},{20... | collective-permute-start | bytes 442376 | tf_op jit(solution)/shard_map/partial_sums/ppermute | solution.py:357
  75.2 7.7 %collective-permute-done.3.low_new = f32[288,128]{1,0:T(8,128)S(1)} collective-permute-done((f32[288,128]{1,0:T(8,128)S(1)}, f32[288,128]{1,0:T(8,128)S(1)}, u32[]{:S(2)}, u32[]{:S(2)}) %collective-permute-start.3) | collective-permute-done | bytes 147488 | tf_op jit(solution)/shard_map/partial_sums/ppermute | solution.py:357
  83.0 0.0 copy-start.3
  83.0 0.7 copy-done.3
  83.6 6.9 %all-to-all-done.2 = bf16[8,24,2304]{2,1,0:T(8,128)(2,1)S(1)} async-done(((bf16[8,24,2304]{2,1,0:T(8,128)(2,1)}), bf16[8,24,2304]{2,1,0:T(8,128)(2,1)S(1)}, u32[]{:S(2)}, u32[]{:S(2)}) %all-to-all-start.2) | async-done | bytes 884768 | tf_op jit(solution)/shard_map/partial_sums/all_to_all | solution.py:356
  90.5 1.1 activation.1
  91.6 4.6 %all-to-all-start.3 = ((bf16[8,24,2304]{2,1,0:T(8,128)(2,1)}), bf16[8,24,2304]{2,1,0:T(8,128)(2,1)S(1)}, u32[]{:S(2)}, u32[]{:S(2)}) async-start(bf16[8,24,2304]{2,1,0:T(8,128)(2,1)} %bitcast.37), calls=%async_computation.3 | async-start | bytes 1769472 | tf_op jit(solution)/shard_map/activation/all_to_all | solution.py:365
  96.2 1.9 %collective-permute-start.4 = (f32[288,128]{1,0:T(8,128)S(1)}, f32[288,128]{1,0:T(8,128)S(1)}, u32[]{:S(2)}, u32[]{:S(2)}) collective-permute-start(f32[288,128]{1,0:T(8,128)S(1)} %get-tuple-element.47.high_old), channel_id=1, source_target_pairs={{0,16},{16,0},{1,17},{17,1},{2,18},{18,2},{3,19},{19,3},{4,20},{20... | collective-permute-start | bytes 442376 | tf_op jit(solution)/shard_map/activation/ppermute | solution.py:366
  98.1 8.7 %collective-permute-done.4.high_new = f32[288,128]{1,0:T(8,128)S(1)} collective-permute-done((f32[288,128]{1,0:T(8,128)S(1)}, f32[288,128]{1,0:T(8,128)S(1)}, u32[]{:S(2)}, u32[]{:S(2)}) %collective-permute-start.4) | collective-permute-done | bytes 147488 | tf_op jit(solution)/shard_map/activation/ppermute | solution.py:366
  106.8 0.0 copy-start.5
  106.8 0.7 copy-done.5
  107.4 2.4 %all-to-all-done.3 = bf16[8,24,2304]{2,1,0:T(8,128)(2,1)S(1)} async-done(((bf16[8,24,2304]{2,1,0:T(8,128)(2,1)}), bf16[8,24,2304]{2,1,0:T(8,128)(2,1)S(1)}, u32[]{:S(2)}, u32[]{:S(2)}) %all-to-all-start.3) | async-done | bytes 884768 | tf_op jit(solution)/shard_map/activation/all_to_all | solution.py:365
  109.9 2.6 %slot_outputs.1 = bf16[768,256]{1,0:T(8,128)(2,1)} custom-call(bf16[192,2304]{1,0:T(8,128)(2,1)S(1)} %bitcast.28, bf16[3,128,768]{2,1,0:T(8,128)(2,1)S(1)} %pad_maximum_fusion.w0, bf16[3,128,768]{2,1,0:T(8,128)(2,1)S(1)} %collective-permute-done.w1, bf16[3,128,768]{2,1,0:T(8,128)(2,1)S(1)} %collective-permute-done.1.w2, ...), custom_call_target="tpu_custom_call" | custom-call | flops 452984832 | bytes 4000000 | tf_op jit(solution)/shard_map/slot_outputs/pallas_call | solution.py:41
  112.4 26.5 %all-to-all-start.4 = ((bf16[32,24,256]{2,1,0:T(8,128)(2,1)}), bf16[32,24,256]{2,1,0:T(8,128)(2,1)S(1)}, u32[]{:S(2)}, u32[]{:S(2)}) async-start(bf16[32,24,256]{2,1,0:T(8,128)(2,1)} %bitcast.38), calls=%async_computation.4 | async-start | bytes 786432 | tf_op jit(solution)/shard_map/slot_outputs/all_to_all | solution.py:378
  138.9 0.0 copy-start.10
  139.0 0.9 copy-done.10
  139.9 0.0 copy-start.11
  139.9 0.9 copy-done.11
  140.8 0.0 copy-start.4
  140.8 1.8 %weight_grads.3 = (f32[2,3,128,768]{3,2,1,0:T(8,128)S(1)}, bf16[2,3,128,768]{3,2,1,0:T(8,128)(2,1)}) custom-call(bf16[192,2304]{1,0:T(8,128)(2,1)S(1)} %bitcast.29, bf16[192,512]{1,0:T(8,128)(2,1)S(1)} %copy-done.10, bf16[192,512]{1,0:T(8,128)(2,1)S(1)} %copy-done.11), custom_call_target="tpu_custom_call" | custom-call | flops 9059696640 | bytes 100000000 | tf_op jit(solution)/shard_map/weight_grads/pallas_call | solution.py:41
  142.7 1.4 copy-done
  144.1 3.0 %collective-permute-start.5 = (bf16[2,3,128,768]{3,2,1,0:T(8,128)(2,1)}, bf16[2,3,128,768]{3,2,1,0:T(8,128)(2,1)S(1)}, u32[]{:S(2)}, u32[]{:S(2)}) collective-permute-start(bf16[2,3,128,768]{3,2,1,0:T(8,128)(2,1)} %get-tuple-element.55), channel_id=1, source_target_pairs={{0,32},{32,0},{1,33},{33,1},{2,34},{34,2},{3,35},{35,3},{4,36},{36... | collective-permute-start | bytes 3538952 | tf_op jit(solution)/shard_map/weight_grads/ppermute | solution.py:397
  147.7 0.0 copy-done.4
  147.7 0.0 copy-done.6
  147.7 0.7 relocate.3
  148.5 1.2 collective-permute-done.5.near_ref
  149.7 1.7 copy-done.1
  151.4 1.2 weight_grads.4
  152.6 2.0 %collective-permute-start.6 = (bf16[3,128,768]{2,1,0:T(8,128)(2,1)S(1)}, bf16[3,128,768]{2,1,0:T(8,128)(2,1)S(1)}, u32[]{:S(2)}, u32[]{:S(2)}) collective-permute-start(bf16[3,128,768]{2,1,0:T(8,128)(2,1)S(1)} %get-tuple-element.63), channel_id=1, source_target_pairs={{0,64},{64,0},{1,65},{65,1},{2,66},{66,2},{3,67},{67,3},{4,68},{68... | collective-permute-start | bytes 1769480 | tf_op jit(solution)/shard_map/weight_grads/ppermute | solution.py:404
  154.7 10.7 %all-to-all-done.4 = bf16[32,24,256]{2,1,0:T(8,128)(2,1)S(1)} async-done(((bf16[32,24,256]{2,1,0:T(8,128)(2,1)}), bf16[32,24,256]{2,1,0:T(8,128)(2,1)S(1)}, u32[]{:S(2)}, u32[]{:S(2)}) %all-to-all-start.4) | async-done | bytes 393248 | tf_op jit(solution)/shard_map/slot_outputs/all_to_all | solution.py:378
  165.4 1.5 combine.1
  166.9 9.0 %all_to_all.62 = bf16[4,64,256]{2,1,0:T(8,128)(2,1)S(1)} all-to-all(bf16[4,64,256]{2,1,0:T(8,128)(2,1)S(1)} %combine.1), channel_id=1, replica_groups=mesh['x_lo'=2,'y1'=4,'y0'=2,'core'=2,'x_hi'=2,'z'=16] {'y0','core'}, dimensions={0} | all-to-all | bytes 262144 | tf_op jit(solution)/shard_map/combine/all_to_all | solution.py:421
  175.9 0.6 fusion
  176.5 0.0 collective-permute-done.6.other_ref
  176.6 0.0 copy-done.2
  176.6 1.0 weight_grads.5
  (7 shorter events, 0.1 us)
Async XLA Ops:
  0.6 36.9 %copy-start.14 = (bf16[1,768,128]{2,1,0:T(8,128)(2,1)S(1)}, bf16[1,768,128]{2,1,0:T(8,128)(2,1)}, u32[]{:S(2)}) copy-start(bf16[1,768,128]{2,1,0:T(8,128)(2,1)} %param.17) | copy-start | bytes 589828
  0.6 37.0 %copy-start.12 = (bf16[1,128,768]{2,1,0:T(8,128)(2,1)S(1)}, bf16[1,128,768]{2,1,0:T(8,128)(2,1)}, u32[]{:S(2)}) copy-start(bf16[1,128,768]{2,1,0:T(8,128)(2,1)} %param.16) | copy-start | bytes 589828
  0.7 37.0 %copy-start.13 = (bf16[1,128,768]{2,1,0:T(8,128)(2,1)S(1)}, bf16[1,128,768]{2,1,0:T(8,128)(2,1)}, u32[]{:S(2)}) copy-start(bf16[1,128,768]{2,1,0:T(8,128)(2,1)} %param.15) | copy-start | bytes 589828
  5.8 21.1 %all-to-all-start = ((bf16[4,64,256]{2,1,0:T(8,128)(2,1)}), bf16[4,64,256]{2,1,0:T(8,128)(2,1)S(1)}, u32[]{:S(2)}, u32[]{:S(2)}) async-start(bf16[4,64,256]{2,1,0:T(8,128)(2,1)} %bitcast.41), calls=%async_computation | async-start | bytes 262144 | tf_op jit(solution)/shard_map/tokens_to_quad/all_to_all | solution.py:321
  28.7 28.6 %copy-start.7 = (f32[1,12,2048]{2,0,1:T(1,128)S(1)}, f32[1,12,2048]{2,0,1:T(1,128)}, u32[]{:S(2)}) copy-start(f32[1,12,2048]{2,0,1:T(1,128)} %param.19) | copy-start | bytes 294916
  28.7 28.6 %copy-start.8 = (f32[1,12,2048]{2,0,1:T(1,128)S(1)}, f32[1,12,2048]{2,0,1:T(1,128)}, u32[]{:S(2)}) copy-start(f32[1,12,2048]{2,0,1:T(1,128)} %param.20) | copy-start | bytes 294916
  28.7 28.6 %copy-start.9 = (f32[1,12,2048]{2,0,1:T(1,128)S(1)}, f32[1,12,2048]{2,0,1:T(1,128)}, u32[]{:S(2)}) copy-start(f32[1,12,2048]{2,0,1:T(1,128)} %param.21) | copy-start | bytes 294916
  28.7 34.9 %all-to-all-start.1 = ((bf16[32,24,256]{2,1,0:T(8,128)(2,1)}), bf16[32,24,256]{2,1,0:T(8,128)(2,1)S(1)}, u32[]{:S(2)}, u32[]{:S(2)}) async-start(bf16[32,24,256]{2,1,0:T(8,128)(2,1)} %bitcast.5), calls=%async_computation.1 | async-start | bytes 786432 | tf_op jit(solution)/shard_map/dispatch/all_to_all | solution.py:346
  37.7 15.4 %collective-permute-start.1 = (bf16[3,128,768]{2,1,0:T(8,128)(2,1)S(1)}, bf16[3,128,768]{2,1,0:T(8,128)(2,1)S(1)}, u32[]{:S(2)}, u32[]{:S(2)}) collective-permute-start(bf16[3,128,768]{2,1,0:T(8,128)(2,1)S(1)} %pad_maximum_fusion.w0), channel_id=1, source_target_pairs={{0,64},{64,0},{1,65},{65,1},{2,66},{66,2},{3,67},{67,3},{4,68},{68... | collective-permute-start | bytes 1769480 | tf_op jit(solution)/shard_map/weights_to_quad/ppermute | solution.py:327
  40.2 17.2 %collective-permute-start = (bf16[3,128,768]{2,1,0:T(8,128)(2,1)S(1)}, bf16[3,128,768]{2,1,0:T(8,128)(2,1)S(1)}, u32[]{:S(2)}, u32[]{:S(2)}) collective-permute-start(bf16[3,128,768]{2,1,0:T(8,128)(2,1)S(1)} %pad_maximum_fusion.w0), channel_id=1, source_target_pairs={{0,32},{32,0},{1,33},{33,1},{2,34},{34,2},{3,35},{35,3},{4,36},{36... | collective-permute-start | bytes 1769480 | tf_op jit(solution)/shard_map/weights_to_quad/ppermute | solution.py:328
  53.1 5.8 %collective-permute-start.2 = (bf16[3,128,768]{2,1,0:T(8,128)(2,1)S(1)}, bf16[3,128,768]{2,1,0:T(8,128)(2,1)S(1)}, u32[]{:S(2)}, u32[]{:S(2)}) collective-permute-start(bf16[3,128,768]{2,1,0:T(8,128)(2,1)S(1)} %collective-permute-done.1.w2), channel_id=1, source_target_pairs={{0,32},{32,0},{1,33},{33,1},{2,34},{34,2},{3,35},{35,3},{4,36},{36... | collective-permute-start | bytes 1769480 | tf_op jit(solution)/shard_map/weights_to_quad/ppermute | solution.py:329
  65.6 24.9 %all-to-all-start.2 = ((bf16[8,24,2304]{2,1,0:T(8,128)(2,1)}), bf16[8,24,2304]{2,1,0:T(8,128)(2,1)S(1)}, u32[]{:S(2)}, u32[]{:S(2)}) async-start(bf16[8,24,2304]{2,1,0:T(8,128)(2,1)} %bitcast.39), calls=%async_computation.2 | async-start | bytes 1769472 | tf_op jit(solution)/shard_map/partial_sums/all_to_all | solution.py:356
  72.5 10.5 %collective-permute-start.3 = (f32[288,128]{1,0:T(8,128)S(1)}, f32[288,128]{1,0:T(8,128)S(1)}, u32[]{:S(2)}, u32[]{:S(2)}) collective-permute-start(f32[288,128]{1,0:T(8,128)S(1)} %get-tuple-element.43.low_old), channel_id=1, source_target_pairs={{0,16},{16,0},{1,17},{17,1},{2,18},{18,2},{3,19},{19,3},{4,20},{20... | collective-permute-start | bytes 442376 | tf_op jit(solution)/shard_map/partial_sums/ppermute | solution.py:357
  83.0 0.7 copy-start.3
  91.6 18.3 %all-to-all-start.3 = ((bf16[8,24,2304]{2,1,0:T(8,128)(2,1)}), bf16[8,24,2304]{2,1,0:T(8,128)(2,1)S(1)}, u32[]{:S(2)}, u32[]{:S(2)}) async-start(bf16[8,24,2304]{2,1,0:T(8,128)(2,1)} %bitcast.37), calls=%async_computation.3 | async-start | bytes 1769472 | tf_op jit(solution)/shard_map/activation/all_to_all | solution.py:365
  96.2 10.6 %collective-permute-start.4 = (f32[288,128]{1,0:T(8,128)S(1)}, f32[288,128]{1,0:T(8,128)S(1)}, u32[]{:S(2)}, u32[]{:S(2)}) collective-permute-start(f32[288,128]{1,0:T(8,128)S(1)} %get-tuple-element.47.high_old), channel_id=1, source_target_pairs={{0,16},{16,0},{1,17},{17,1},{2,18},{18,2},{3,19},{19,3},{4,20},{20... | collective-permute-start | bytes 442376 | tf_op jit(solution)/shard_map/activation/ppermute | solution.py:366
  106.8 0.7 copy-start.5
  112.4 53.0 %all-to-all-start.4 = ((bf16[32,24,256]{2,1,0:T(8,128)(2,1)}), bf16[32,24,256]{2,1,0:T(8,128)(2,1)S(1)}, u32[]{:S(2)}, u32[]{:S(2)}) async-start(bf16[32,24,256]{2,1,0:T(8,128)(2,1)} %bitcast.38), calls=%async_computation.4 | async-start | bytes 786432 | tf_op jit(solution)/shard_map/slot_outputs/all_to_all | solution.py:378
  138.9 0.9 copy-start.10
  139.9 0.9 copy-start.11
  140.8 6.9 %copy-start.4 = (f32[288,128]{1,0:T(8,128)S(1)}, f32[288,128]{1,0:T(8,128)}, u32[]{:S(2)}) copy-start(f32[288,128]{1,0:T(8,128)} %copy-done.3) | copy-start | bytes 442372
  140.8 6.9 %copy-start.6 = (f32[288,128]{1,0:T(8,128)S(1)}, f32[288,128]{1,0:T(8,128)}, u32[]{:S(2)}) copy-start(f32[288,128]{1,0:T(8,128)} %copy-done.5) | copy-start | bytes 442372
  142.6 1.4 copy-start
  144.1 5.7 %collective-permute-start.5 = (bf16[2,3,128,768]{3,2,1,0:T(8,128)(2,1)}, bf16[2,3,128,768]{3,2,1,0:T(8,128)(2,1)S(1)}, u32[]{:S(2)}, u32[]{:S(2)}) collective-permute-start(bf16[2,3,128,768]{3,2,1,0:T(8,128)(2,1)} %get-tuple-element.55), channel_id=1, source_target_pairs={{0,32},{32,0},{1,33},{33,1},{2,34},{34,2},{3,35},{35,3},{4,36},{36... | collective-permute-start | bytes 3538952 | tf_op jit(solution)/shard_map/weight_grads/ppermute | solution.py:397
  149.7 1.7 copy-start.1
  152.6 23.9 %copy-start.2 = (f32[3,128,768]{2,1,0:T(8,128)S(1)}, f32[3,128,768]{2,1,0:T(8,128)}, u32[]{:S(2)}) copy-start(f32[3,128,768]{2,1,0:T(8,128)} %get-tuple-element.56.kept_ref) | copy-start | bytes 3538948
  152.6 23.9 %collective-permute-start.6 = (bf16[3,128,768]{2,1,0:T(8,128)(2,1)S(1)}, bf16[3,128,768]{2,1,0:T(8,128)(2,1)S(1)}, u32[]{:S(2)}, u32[]{:S(2)}) collective-permute-start(bf16[3,128,768]{2,1,0:T(8,128)(2,1)S(1)} %get-tuple-element.63), channel_id=1, source_target_pairs={{0,64},{64,0},{1,65},{65,1},{2,66},{66,2},{3,67},{67,3},{4,68},{68... | collective-permute-start | bytes 1769480 | tf_op jit(solution)/shard_map/weight_grads/ppermute | solution.py:404

commit v7 on v6

--- a/solution.py
+++ b/solution.py
@@ -67,29 +67,10 @@
     return lax.dot_general(a, b, (dims, ((), ())), preferred_element_type=F32)
 
 
-def blocks_kernel(a_ref, b_ref, out_ref, sems):
-    copies = []
+def blocks_kernel(a_ref, b_ref, out_ref):
+    both = jnp.concatenate([a_ref[...], b_ref[...]], axis=1)
     for d in range(QUADS):
-        rows = slice(d * TOK, (d + 1) * TOK)
-        copies.append(pltpu.make_async_copy(a_ref, out_ref.at[rows, :BLK], sems.at[2 * d]))
-        copies.append(pltpu.make_async_copy(b_ref, out_ref.at[rows, BLK:], sems.at[2 * d + 1]))
-    for copy in copies:
-        copy.start()
-    for copy in copies:
-        copy.wait()
-
-
-def blocks(a, b):
-    hbm = pl.BlockSpec(memory_space=pltpu.HBM)
-    return pl.pallas_call(
-        blocks_kernel,
-        out_shape=far_shape(QUADS * TOK, 2 * BLK),
-        in_specs=[hbm, hbm],
-        out_specs=hbm,
-        scratch_shapes=[pltpu.SemaphoreType.DMA((2 * QUADS,))],
-        compiler_params=PARAMS,
-        cost_estimate=pl.CostEstimate(flops=0, bytes_accessed=262144, transcendentals=0),
-    )(far(a), far(b))
+        out_ref[d * TOK : (d + 1) * TOK] = both
 
 
 def table_kernel(q_ref, routes_ref, probs_ref, prob_ref, prob_again):
@@ -275,23 +256,16 @@
         out_ref[q ^ d] = jnp.concatenate([mixed, grad], axis=1).astype(BF16)
 
 
-def stack_kernel(a_ref, b_ref, c_ref, low_ref, high_ref):
-    half = NEXT // 2
-    low_ref[:NEXT] = a_ref[...]
-    low_ref[NEXT:] = b_ref[:half]
-    high_ref[:half] = b_ref[half:]
-    high_ref[half:] = c_ref[...]
-
-
-def select_kernel(moving_ref, low_new, high_new, low_old, high_old, a_ref, b_ref, c_ref):
-    half = NEXT // 2
+def stack_kernel(a_ref, b_ref, c_ref, out_ref):
+    for k, ref in enumerate((a_ref, b_ref, c_ref)):
+        out_ref[k * NEXT : (k + 1) * NEXT] = ref[...]
+
+
+def select_kernel(moving_ref, partner_ref, state_ref, a_ref, b_ref, c_ref):
     moving = moving_ref[0] != 0
-    low = jnp.where(moving, low_new[...], low_old[...])
-    high = jnp.where(moving, high_new[...], high_old[...])
-    a_ref[...] = low[:NEXT]
-    b_ref[:half] = low[NEXT:]
-    b_ref[half:] = high[:half]
-    c_ref[...] = high[half:]
+    for k, ref in enumerate((a_ref, b_ref, c_ref)):
+        rows = slice(k * NEXT, (k + 1) * NEXT)
+        ref[...] = jnp.where(moving, partner_ref[rows], state_ref[rows])
 
 
 def shape_of(*dims, dtype=BF16):
@@ -319,13 +293,28 @@
 
     with jax.named_scope("tokens_to_quad"):
         shared = lax.all_to_all(
-            blocks(tokens, grad_out), QUAD, split_axis=0, concat_axis=0, tiled=True
-        )
+            call(
+                blocks_kernel,
+                far_shape(QUADS * TOK, 2 * BLK),
+                (far(tokens), far(grad_out)),
+                moved=200000,
+            ),
+            QUAD,
+            split_axis=0,
+            concat_axis=0,
+            tiled=True,
+        )
+
+    with jax.named_scope("relocate"):
+        mine_next = [v.reshape(NEXT, BLK) for v in (next_master, next_first, next_second)]
+        state = call(stack_kernel, shape_of(3 * NEXT, BLK, dtype=F32), mine_next, moved=600000)
+        partner = lax.ppermute(state, "x_hi", SWAP)
 
     with jax.named_scope("weights_to_quad"):
         w0 = jnp.stack([w_gate[0], w_up[0], w_down[0].T])
         w2 = lax.ppermute(w0, "y0", SWAP)
         w1 = lax.ppermute(w0, "core", SWAP)
+        w2, partner, state = lax.optimization_barrier((w2, partner, state))
         w3 = lax.ppermute(w2, "core", SWAP)
 
     with jax.named_scope("dispatch"):
@@ -345,26 +334,15 @@
         )
         got = lax.all_to_all(pay, EXPERT, split_axis=0, concat_axis=0, tiled=True)
 
-    with jax.named_scope("relocate"):
-        mine_next = [v.reshape(NEXT, BLK) for v in (next_master, next_first, next_second)]
-        halves = [shape_of(3 * NEXT // 2, BLK, dtype=F32)] * 2
-        low, high = call(stack_kernel, halves, mine_next, moved=600000)
-
     with jax.named_scope("partial_sums"):
         sums, x_rows, dy_rows = partial_sums(got, w0, w1, w2, w3)
-        sums, low = lax.optimization_barrier((sums, low))
         parts = lax.all_to_all(sums, SUMS, split_axis=0, concat_axis=0, tiled=True)
-        low_new = lax.ppermute(low, "x_hi", SWAP)
-        parts, low_new = lax.optimization_barrier((parts, low_new))
 
     with jax.named_scope("activation"):
         hidden = call(
             act_kernel, far_shape(ROWS, 3 * FF), (parts,), flops=4000000, moved=1000000
         )
-        hidden, high = lax.optimization_barrier((hidden, high))
         whole = lax.all_to_all(hidden, SUMS, split_axis=0, concat_axis=0, tiled=True)
-        high_new = lax.ppermute(high, "x_hi", SWAP)
-        whole, high_new = lax.optimization_barrier((whole, high_new))
 
     with jax.named_scope("slot_outputs"):
         back = call(
@@ -382,7 +360,7 @@
         moved = call(
             select_kernel,
             [far_shape(NEXT, BLK, dtype=F32)] * 3,
-            (moving, low_new, high_new, low, high),
+            (moving, partner, state),
             moved=1200000,
         )
 

time: 178 us -> 173 us (0.972)
  blocking collectives: 8.99 us -> 53.5 us
  waiting for transfers between devices: 55.5 us -> 22.9 us
  starting transfers between devices: 83.6 us -> 71.7 us
  Pallas kernels: 20.8 us -> 17.1 us
    all_to_all x0 -> x2, blocking collectives: none -> 42.9 us  [the longest x1 24.8 us: shards(): parts = lax.all_to_all(sums, SUMS, split_axis=0, concat_axis=0, tiled=True)]
    ppermute x2 -> x1, waiting for transfers between devices: 16.4 us -> 4.68 us  [shards(): partner = lax.ppermute(state, 'x_hi', SWAP)]
    all_to_all x3 -> x1, starting transfers between devices: 28.9 us -> 17.4 us  [shards(): lax.all_to_all(call(blocks_kernel, far_shape(QUADS * TOK, 2 * BLK), (far(...]
    ppermute x1, waiting for transfers between devices: 9.88 us -> 0.01 us  [shards(): w2 = lax.ppermute(w0, 'y0', SWAP)]
    all_to_all x3 -> x1, waiting for transfers between devices: 11 us -> 1.73 us  [shards(): lax.all_to_all(call(blocks_kernel, far_shape(QUADS * TOK, 2 * BLK), (far(...]
    pallas_call x1 -> x0, Pallas kernels: 5.14 us -> none  [blocks(): pl.pallas_call(blocks_kernel, out_shape=far_shape(QUADS * TOK, 2 * BLK),...]
    pallas_call x10 -> x11, Pallas kernels: 13.6 us -> 15 us  [call(): pl.pallas_call(kernel, out_shape=out_shape, in_specs=[smem if o.dtype ==...]
    unnamed x31 -> x27, local copies, waits for them, and re-layouts: 6.43 us -> 5.12 us
  transfers between devices with their start and end apart: 12 -> 9, of which waited for: 10 -> 6; matrix products, arithmetic and copies ran while one was open for 0% -> 0% of each run, Pallas kernels for 4% -> 4%
where the time goes in v7:
time: 173 us
  starting transfers between devices  71.7 us (41%)
  blocking collectives  53.5 us (31%)
  waiting for transfers between devices  22.9 us (13%)
  Pallas kernels  17.1 us (10%)
  local copies, waits for them, and re-layouts  5.74 us (3%)
    all_to_all x1, starting transfers between devices, shards(): lax.all_to_all(back, EXPERT, split_axis=0, concat_axis=0, tiled=True)  24.9 us
    all_to_all x1, blocking collectives, shards(): parts = lax.all_to_all(sums, SUMS, split_axis=0, concat_axis=0, tiled=True)  24.8 us
    all_to_all x1, blocking collectives, shards(): lax.all_to_all(hidden, SUMS, split_axis=0, concat_axis=0, tiled=True)  18.1 us
    all_to_all x1, starting transfers between devices, shards(): lax.all_to_all(call(blocks_kernel, far_shape(QUADS * TOK, 2 * BLK), (far(...  17.4 us
    pallas_call x11, Pallas kernels, call(): pl.pallas_call(kernel, out_shape=out_shape, in_specs=[smem if o.dtype ==...  15 us
    all_to_all x1, blocking collectives, shards(): mixes = lax.all_to_all(mixes, QUAD, split_axis=0, concat_axis=0, tiled=True)  10.6 us
    all_to_all x1, waiting for transfers between devices, shards(): lax.all_to_all(back, EXPERT, split_axis=0, concat_axis=0, tiled=True)  9 us
    all_to_all x1, starting transfers between devices, shards(): got = lax.all_to_all(pay, EXPERT, split_axis=0, concat_axis=0, tiled=True)  8.81 us
  transfers between devices with their start and end apart: 9, of which 6 were waited for; matrix products, arithmetic and copies ran while one was open for 0% of the time, Pallas kernels for 4%

profile of v7, /device:TPU:1, one launch (start us, length us, event | category | flops | bytes accessed | tf_op | source)
XLA Modules:
  0.0 172.5 jit_solution(8051795434347002857)
XLA Ops:
  0.6 0.0 copy-start.12
  0.6 0.0 copy-start.10
  0.7 0.0 copy-start.11
  0.7 1.5 tokens_to_quad.1
  2.1 17.4 %all-to-all-start = ((bf16[4,64,256]{2,1,0:T(8,128)(2,1)}), bf16[4,64,256]{2,1,0:T(8,128)(2,1)S(1)}, u32[]{:S(2)}, u32[]{:S(2)}) async-start(bf16[4,64,256]{2,1,0:T(8,128)(2,1)} %bitcast.41), calls=%async_computation | async-start | bytes 262144 | tf_op jit(solution)/shard_map/tokens_to_quad/all_to_all | solution.py:295
  19.6 1.9 %dispatch.2 = (f32[64,768]{1,0:T(8,128)S(1)}, f32[64,768]{1,0:T(8,128)}) custom-call(s32[1]{0:T(128)} %bitcast.q_ref, s32[8,64]{1,0:T(8,128)} %bitcast.48, f32[8,64]{1,0:T(8,128)} %bitcast.49), custom_call_target="tpu_custom_call" | custom-call | flops 6291456 | bytes 300000 | tf_op jit(solution)/shard_map/dispatch/pallas_call | solution.py:41
  21.4 1.7 %all-to-all-done = bf16[4,64,256]{2,1,0:T(8,128)(2,1)S(1)} async-done(((bf16[4,64,256]{2,1,0:T(8,128)(2,1)}), bf16[4,64,256]{2,1,0:T(8,128)(2,1)S(1)}, u32[]{:S(2)}, u32[]{:S(2)}) %all-to-all-start) | async-done | bytes 131104 | tf_op jit(solution)/shard_map/tokens_to_quad/all_to_all | solution.py:295
  23.2 1.8 %dispatch.3 = bf16[768,256]{1,0:T(8,128)(2,1)} custom-call(s32[1]{0:T(128)} %bitcast.q_ref, f32[64,768]{1,0:T(8,128)S(1)} %get-tuple-element.32.prob_ref, bf16[256,256]{1,0:T(8,128)(2,1)S(1)} %bitcast.33), custom_call_target="tpu_custom_call" | custom-call | flops 201326592 | bytes 800000 | tf_op jit(solution)/shard_map/dispatch/pallas_call | solution.py:41
  25.0 0.0 copy-start.5
  25.0 0.0 copy-start.6
  25.0 0.0 copy-start.7
  25.0 8.8 %all-to-all-start.1 = ((bf16[32,24,256]{2,1,0:T(8,128)(2,1)}), bf16[32,24,256]{2,1,0:T(8,128)(2,1)S(1)}, u32[]{:S(2)}, u32[]{:S(2)}) async-start(bf16[32,24,256]{2,1,0:T(8,128)(2,1)} %bitcast.5), calls=%async_computation.1 | async-start | bytes 786432 | tf_op jit(solution)/shard_map/dispatch/all_to_all | solution.py:335
  33.8 0.0 copy-done.12
  33.8 0.1 copy.23
  34.0 0.0 copy-done.10
  34.0 0.0 copy-done.11
  34.0 0.1 pad_maximum_fusion.w0
  34.1 2.4 %collective-permute-start.1 = (bf16[3,128,768]{2,1,0:T(8,128)(2,1)S(1)}, bf16[3,128,768]{2,1,0:T(8,128)(2,1)S(1)}, u32[]{:S(2)}, u32[]{:S(2)}) collective-permute-start(bf16[3,128,768]{2,1,0:T(8,128)(2,1)S(1)} %pad_maximum_fusion.w0), channel_id=1, source_target_pairs={{0,64},{64,0},{1,65},{65,1},{2,66},{66,2},{3,67},{67,3},{4,68},{68... | collective-permute-start | bytes 1769480 | tf_op jit(solution)/shard_map/weights_to_quad/ppermute | solution.py:315
  36.5 0.0 copy-done.5
  36.5 0.0 copy-done.6
  36.5 0.0 copy-done.7
  36.5 4.7 %collective-permute-start.2 = (f32[576,128]{1,0:T(8,128)S(1)}, f32[576,128]{1,0:T(8,128)S(1)}, u32[]{:S(2)}, u32[]{:S(2)}) collective-permute-start(f32[576,128]{1,0:T(8,128)S(1)} %relocate.2.state_ref), channel_id=1, source_target_pairs={{0,16},{16,0},{1,17},{17,1},{2,18},{18,2},{3,19},{19,3},{4,20},{20... | collective-permute-start | bytes 884744 | tf_op jit(solution)/shard_map/relocate/ppermute | solution.py:311
  41.2 3.6 %collective-permute-start = (bf16[3,128,768]{2,1,0:T(8,128)(2,1)S(1)}, bf16[3,128,768]{2,1,0:T(8,128)(2,1)S(1)}, u32[]{:S(2)}, u32[]{:S(2)}) collective-permute-start(bf16[3,128,768]{2,1,0:T(8,128)(2,1)S(1)} %pad_maximum_fusion.w0), channel_id=1, source_target_pairs={{0,32},{32,0},{1,33},{33,1},{2,34},{34,2},{3,35},{35,3},{4,36},{36... | collective-permute-start | bytes 1769480 | tf_op jit(solution)/shard_map/weights_to_quad/ppermute | solution.py:316
  44.8 4.7 %collective-permute-done.2.partner_ref = f32[576,128]{1,0:T(8,128)S(1)} collective-permute-done((f32[576,128]{1,0:T(8,128)S(1)}, f32[576,128]{1,0:T(8,128)S(1)}, u32[]{:S(2)}, u32[]{:S(2)}) %collective-permute-start.2) | collective-permute-done | bytes 294944 | tf_op jit(solution)/shard_map/relocate/ppermute | solution.py:311
  49.5 0.0 copy-start.3
  49.5 0.0 collective-permute-done.1.w2
  49.5 4.1 %collective-permute-start.3 = (bf16[3,128,768]{2,1,0:T(8,128)(2,1)S(1)}, bf16[3,128,768]{2,1,0:T(8,128)(2,1)S(1)}, u32[]{:S(2)}, u32[]{:S(2)}) collective-permute-start(bf16[3,128,768]{2,1,0:T(8,128)(2,1)S(1)} %collective-permute-done.1.w2), channel_id=1, source_target_pairs={{0,32},{32,0},{1,33},{33,1},{2,34},{34,2},{3,35},{35,3},{4,36},{36... | collective-permute-start | bytes 1769480 | tf_op jit(solution)/shard_map/weights_to_quad/ppermute | solution.py:318
  53.6 0.0 collective-permute-done.w1
  53.6 1.6 collective-permute-done.3.w3
  55.2 4.7 %all-to-all-done.1 = bf16[32,24,256]{2,1,0:T(8,128)(2,1)S(1)} async-done(((bf16[32,24,256]{2,1,0:T(8,128)(2,1)}), bf16[32,24,256]{2,1,0:T(8,128)(2,1)S(1)}, u32[]{:S(2)}, u32[]{:S(2)}) %all-to-all-start.1) | async-done | bytes 393248 | tf_op jit(solution)/shard_map/dispatch/all_to_all | solution.py:335
  59.9 2.1 %partial_sums.1 = (bf16[192,2304]{1,0:T(8,128)(2,1)}, bf16[192,512]{1,0:T(8,128)(2,1)}, bf16[192,512]{1,0:T(8,128)(2,1)}) custom-call(bf16[768,256]{1,0:T(8,128)(2,1)S(1)} %bitcast.31, bf16[3,128,768]{2,1,0:T(8,128)(2,1)S(1)} %pad_maximum_fusion.w0, bf16[3,128,768]{2,1,0:T(8,128)(2,1)S(1)} %collective-permute-done.w1, ...), custom_call_target="tpu_custom_call" | custom-call | flops 452984832 | bytes 4000000 | tf_op jit(solution)/shard_map/partial_sums/pallas_call | solution.py:159
  61.9 0.0 copy-done.3
  61.9 24.8 %all_to_all.60 = bf16[8,24,2304]{2,1,0:T(8,128)(2,1)S(1)} all-to-all(bf16[8,24,2304]{2,1,0:T(8,128)(2,1)} %bitcast.39), channel_id=1, replica_groups=mesh['x_lo'=2,'y1'=4,'y0'=2,'core'=2,'x_hi'=2,'z'=16] {'x_lo','y1'}, dimensions={0} | all-to-all | bytes 1769472 | tf_op jit(solution)/shard_map/partial_sums/all_to_all | solution.py:339
  86.7 1.1 activation.1
  87.8 18.1 %all_to_all.61 = bf16[8,24,2304]{2,1,0:T(8,128)(2,1)S(1)} all-to-all(bf16[8,24,2304]{2,1,0:T(8,128)(2,1)} %bitcast.37), channel_id=1, replica_groups=mesh['x_lo'=2,'y1'=4,'y0'=2,'core'=2,'x_hi'=2,'z'=16] {'x_lo','y1'}, dimensions={0} | all-to-all | bytes 1769472 | tf_op jit(solution)/shard_map/activation/all_to_all | solution.py:345
  105.9 2.6 %slot_outputs.1 = bf16[768,256]{1,0:T(8,128)(2,1)} custom-call(bf16[192,2304]{1,0:T(8,128)(2,1)S(1)} %bitcast.28, bf16[3,128,768]{2,1,0:T(8,128)(2,1)S(1)} %pad_maximum_fusion.w0, bf16[3,128,768]{2,1,0:T(8,128)(2,1)S(1)} %collective-permute-done.w1, bf16[3,128,768]{2,1,0:T(8,128)(2,1)S(1)} %collective-permute-done.1.w2, ...), custom_call_target="tpu_custom_call" | custom-call | flops 452984832 | bytes 4000000 | tf_op jit(solution)/shard_map/slot_outputs/pallas_call | solution.py:41
  108.4 24.9 %all-to-all-start.4 = ((bf16[32,24,256]{2,1,0:T(8,128)(2,1)}), bf16[32,24,256]{2,1,0:T(8,128)(2,1)S(1)}, u32[]{:S(2)}, u32[]{:S(2)}) async-start(bf16[32,24,256]{2,1,0:T(8,128)(2,1)} %bitcast.38), calls=%async_computation.4 | async-start | bytes 786432 | tf_op jit(solution)/shard_map/slot_outputs/all_to_all | solution.py:356
  133.4 0.0 copy-start.8
  133.4 0.9 copy-done.8
  134.3 0.0 copy-start.9
  134.3 0.9 copy-done.9
  135.2 0.0 copy-start.4
  135.2 1.8 %weight_grads.3 = (f32[2,3,128,768]{3,2,1,0:T(8,128)S(1)}, bf16[2,3,128,768]{3,2,1,0:T(8,128)(2,1)}) custom-call(bf16[192,2304]{1,0:T(8,128)(2,1)S(1)} %bitcast.29, bf16[192,512]{1,0:T(8,128)(2,1)S(1)} %copy-done.8, bf16[192,512]{1,0:T(8,128)(2,1)S(1)} %copy-done.9), custom_call_target="tpu_custom_call" | custom-call | flops 9059696640 | bytes 100000000 | tf_op jit(solution)/shard_map/weight_grads/pallas_call | solution.py:41
  137.0 0.0 copy-start
  137.0 1.4 copy-done
  138.5 3.6 %collective-permute-start.4 = (bf16[2,3,128,768]{3,2,1,0:T(8,128)(2,1)}, bf16[2,3,128,768]{3,2,1,0:T(8,128)(2,1)S(1)}, u32[]{:S(2)}, u32[]{:S(2)}) collective-permute-start(bf16[2,3,128,768]{3,2,1,0:T(8,128)(2,1)} %get-tuple-element.41), channel_id=1, source_target_pairs={{0,32},{32,0},{1,33},{33,1},{2,34},{34,2},{3,35},{35,3},{4,36},{36... | collective-permute-start | bytes 3538952 | tf_op jit(solution)/shard_map/weight_grads/ppermute | solution.py:375
  142.7 0.0 copy-done.4
  142.7 0.7 relocate.3
  143.5 1.3 collective-permute-done.4.near_ref
  144.7 0.0 copy-start.1
  144.7 1.7 copy-done.1
  146.4 1.2 weight_grads.4
  147.6 0.0 copy-start.2
  147.6 2.2 %collective-permute-start.5 = (bf16[3,128,768]{2,1,0:T(8,128)(2,1)S(1)}, bf16[3,128,768]{2,1,0:T(8,128)(2,1)S(1)}, u32[]{:S(2)}, u32[]{:S(2)}) collective-permute-start(bf16[3,128,768]{2,1,0:T(8,128)(2,1)S(1)} %get-tuple-element.49), channel_id=1, source_target_pairs={{0,64},{64,0},{1,65},{65,1},{2,66},{66,2},{3,67},{67,3},{4,68},{68... | collective-permute-start | bytes 1769480 | tf_op jit(solution)/shard_map/weight_grads/ppermute | solution.py:382
  149.8 9.0 %all-to-all-done.4 = bf16[32,24,256]{2,1,0:T(8,128)(2,1)S(1)} async-done(((bf16[32,24,256]{2,1,0:T(8,128)(2,1)}), bf16[32,24,256]{2,1,0:T(8,128)(2,1)S(1)}, u32[]{:S(2)}, u32[]{:S(2)}) %all-to-all-start.4) | async-done | bytes 393248 | tf_op jit(solution)/shard_map/slot_outputs/all_to_all | solution.py:356
  158.8 1.5 combine.1
  160.3 10.6 %all_to_all.62 = bf16[4,64,256]{2,1,0:T(8,128)(2,1)S(1)} all-to-all(bf16[4,64,256]{2,1,0:T(8,128)(2,1)S(1)} %combine.1), channel_id=1, replica_groups=mesh['x_lo'=2,'y1'=4,'y0'=2,'core'=2,'x_hi'=2,'z'=16] {'y0','core'}, dimensions={0} | all-to-all | bytes 262144 | tf_op jit(solution)/shard_map/combine/all_to_all | solution.py:399
  170.9 0.6 fusion
  171.6 0.0 collective-permute-done.5.other_ref
  171.6 0.0 copy-done.2
  171.6 1.0 weight_grads.5
  (2 shorter events, 0.0 us)
Async XLA Ops:
  0.6 33.2 %copy-start.12 = (bf16[1,768,128]{2,1,0:T(8,128)(2,1)S(1)}, bf16[1,768,128]{2,1,0:T(8,128)(2,1)}, u32[]{:S(2)}) copy-start(bf16[1,768,128]{2,1,0:T(8,128)(2,1)} %param.17) | copy-start | bytes 589828
  0.6 33.3 %copy-start.10 = (bf16[1,128,768]{2,1,0:T(8,128)(2,1)S(1)}, bf16[1,128,768]{2,1,0:T(8,128)(2,1)}, u32[]{:S(2)}) copy-start(bf16[1,128,768]{2,1,0:T(8,128)(2,1)} %param.16) | copy-start | bytes 589828
  0.7 33.3 %copy-start.11 = (bf16[1,128,768]{2,1,0:T(8,128)(2,1)S(1)}, bf16[1,128,768]{2,1,0:T(8,128)(2,1)}, u32[]{:S(2)}) copy-start(bf16[1,128,768]{2,1,0:T(8,128)(2,1)} %param.15) | copy-start | bytes 589828
  2.1 21.0 %all-to-all-start = ((bf16[4,64,256]{2,1,0:T(8,128)(2,1)}), bf16[4,64,256]{2,1,0:T(8,128)(2,1)S(1)}, u32[]{:S(2)}, u32[]{:S(2)}) async-start(bf16[4,64,256]{2,1,0:T(8,128)(2,1)} %bitcast.41), calls=%async_computation | async-start | bytes 262144 | tf_op jit(solution)/shard_map/tokens_to_quad/all_to_all | solution.py:295
  25.0 11.5 %copy-start.5 = (f32[1,12,2048]{2,0,1:T(1,128)S(1)}, f32[1,12,2048]{2,0,1:T(1,128)}, u32[]{:S(2)}) copy-start(f32[1,12,2048]{2,0,1:T(1,128)} %param.19) | copy-start | bytes 294916
  25.0 11.5 %copy-start.6 = (f32[1,12,2048]{2,0,1:T(1,128)S(1)}, f32[1,12,2048]{2,0,1:T(1,128)}, u32[]{:S(2)}) copy-start(f32[1,12,2048]{2,0,1:T(1,128)} %param.20) | copy-start | bytes 294916
  25.0 11.5 %copy-start.7 = (f32[1,12,2048]{2,0,1:T(1,128)S(1)}, f32[1,12,2048]{2,0,1:T(1,128)}, u32[]{:S(2)}) copy-start(f32[1,12,2048]{2,0,1:T(1,128)} %param.21) | copy-start | bytes 294916
  25.0 34.9 %all-to-all-start.1 = ((bf16[32,24,256]{2,1,0:T(8,128)(2,1)}), bf16[32,24,256]{2,1,0:T(8,128)(2,1)S(1)}, u32[]{:S(2)}, u32[]{:S(2)}) async-start(bf16[32,24,256]{2,1,0:T(8,128)(2,1)} %bitcast.5), calls=%async_computation.1 | async-start | bytes 786432 | tf_op jit(solution)/shard_map/dispatch/all_to_all | solution.py:335
  34.1 15.5 %collective-permute-start.1 = (bf16[3,128,768]{2,1,0:T(8,128)(2,1)S(1)}, bf16[3,128,768]{2,1,0:T(8,128)(2,1)S(1)}, u32[]{:S(2)}, u32[]{:S(2)}) collective-permute-start(bf16[3,128,768]{2,1,0:T(8,128)(2,1)S(1)} %pad_maximum_fusion.w0), channel_id=1, source_target_pairs={{0,64},{64,0},{1,65},{65,1},{2,66},{66,2},{3,67},{67,3},{4,68},{68... | collective-permute-start | bytes 1769480 | tf_op jit(solution)/shard_map/weights_to_quad/ppermute | solution.py:315
  36.5 13.0 %collective-permute-start.2 = (f32[576,128]{1,0:T(8,128)S(1)}, f32[576,128]{1,0:T(8,128)S(1)}, u32[]{:S(2)}, u32[]{:S(2)}) collective-permute-start(f32[576,128]{1,0:T(8,128)S(1)} %relocate.2.state_ref), channel_id=1, source_target_pairs={{0,16},{16,0},{1,17},{17,1},{2,18},{18,2},{3,19},{19,3},{4,20},{20... | collective-permute-start | bytes 884744 | tf_op jit(solution)/shard_map/relocate/ppermute | solution.py:311
  41.2 12.4 %collective-permute-start = (bf16[3,128,768]{2,1,0:T(8,128)(2,1)S(1)}, bf16[3,128,768]{2,1,0:T(8,128)(2,1)S(1)}, u32[]{:S(2)}, u32[]{:S(2)}) collective-permute-start(bf16[3,128,768]{2,1,0:T(8,128)(2,1)S(1)} %pad_maximum_fusion.w0), channel_id=1, source_target_pairs={{0,32},{32,0},{1,33},{33,1},{2,34},{34,2},{3,35},{35,3},{4,36},{36... | collective-permute-start | bytes 1769480 | tf_op jit(solution)/shard_map/weights_to_quad/ppermute | solution.py:316
  49.5 12.4 %copy-start.3 = (f32[576,128]{1,0:T(8,128)}, f32[576,128]{1,0:T(8,128)S(1)}, u32[]{:S(2)}) copy-start(f32[576,128]{1,0:T(8,128)S(1)} %collective-permute-done.2.partner_ref) | copy-start | bytes 884740
  49.5 5.7 %collective-permute-start.3 = (bf16[3,128,768]{2,1,0:T(8,128)(2,1)S(1)}, bf16[3,128,768]{2,1,0:T(8,128)(2,1)S(1)}, u32[]{:S(2)}, u32[]{:S(2)}) collective-permute-start(bf16[3,128,768]{2,1,0:T(8,128)(2,1)S(1)} %collective-permute-done.1.w2), channel_id=1, source_target_pairs={{0,32},{32,0},{1,33},{33,1},{2,34},{34,2},{3,35},{35,3},{4,36},{36... | collective-permute-start | bytes 1769480 | tf_op jit(solution)/shard_map/weights_to_quad/ppermute | solution.py:318
  108.4 50.3 %all-to-all-start.4 = ((bf16[32,24,256]{2,1,0:T(8,128)(2,1)}), bf16[32,24,256]{2,1,0:T(8,128)(2,1)S(1)}, u32[]{:S(2)}, u32[]{:S(2)}) async-start(bf16[32,24,256]{2,1,0:T(8,128)(2,1)} %bitcast.38), calls=%async_computation.4 | async-start | bytes 786432 | tf_op jit(solution)/shard_map/slot_outputs/all_to_all | solution.py:356
  133.4 0.9 copy-start.8
  134.3 0.9 copy-start.9
  135.2 7.5 %copy-start.4 = (f32[576,128]{1,0:T(8,128)S(1)}, f32[576,128]{1,0:T(8,128)}, u32[]{:S(2)}) copy-start(f32[576,128]{1,0:T(8,128)} %copy-done.3) | copy-start | bytes 884740
  137.0 1.4 copy-start
  138.5 6.3 %collective-permute-start.4 = (bf16[2,3,128,768]{3,2,1,0:T(8,128)(2,1)}, bf16[2,3,128,768]{3,2,1,0:T(8,128)(2,1)S(1)}, u32[]{:S(2)}, u32[]{:S(2)}) collective-permute-start(bf16[2,3,128,768]{3,2,1,0:T(8,128)(2,1)} %get-tuple-element.41), channel_id=1, source_target_pairs={{0,32},{32,0},{1,33},{33,1},{2,34},{34,2},{3,35},{35,3},{4,36},{36... | collective-permute-start | bytes 3538952 | tf_op jit(solution)/shard_map/weight_grads/ppermute | solution.py:375
  144.7 1.7 copy-start.1
  147.6 24.0 %copy-start.2 = (f32[3,128,768]{2,1,0:T(8,128)S(1)}, f32[3,128,768]{2,1,0:T(8,128)}, u32[]{:S(2)}) copy-start(f32[3,128,768]{2,1,0:T(8,128)} %get-tuple-element.42.kept_ref) | copy-start | bytes 3538948
  147.6 24.0 %collective-permute-start.5 = (bf16[3,128,768]{2,1,0:T(8,128)(2,1)S(1)}, bf16[3,128,768]{2,1,0:T(8,128)(2,1)S(1)}, u32[]{:S(2)}, u32[]{:S(2)}) collective-permute-start(bf16[3,128,768]{2,1,0:T(8,128)(2,1)S(1)} %get-tuple-element.49), channel_id=1, source_target_pairs={{0,64},{64,0},{1,65},{65,1},{2,66},{66,2},{3,67},{67,3},{4,68},{68... | collective-permute-start | bytes 1769480 | tf_op jit(solution)/shard_map/weight_grads/ppermute | solution.py:382

commit v8 on v7

--- a/solution.py
+++ b/solution.py
@@ -98,41 +98,42 @@
     prob_again[...] = prob
 
 
+def stacked(value, q):
+    _, member, _ = row_fields(value.shape, 1)
+    own = member ^ q
+    return jnp.concatenate([jnp.where(own == m, value, 0.0) for m in range(QUADS)], axis=0)
+
+
 def dispatch_kernel(q_ref, prob_ref, tok_ref, pay_ref):
-    shape = (TOK, WIDE)
-    _, member, _ = row_fields(shape, 1)
-    prob = prob_ref[...]
-    mask = jnp.where(prob > 0.0, 1.0, 0.0)
-    masks = [jnp.where(member == d, mask, 0.0).astype(BF16) for d in range(QUADS)]
-    parts = three(prob)
-    x = jnp.zeros((WIDE, BLK), F32)
-    dy = jnp.zeros((WIDE, BLK), F32)
-    zero = jnp.zeros(shape, BF16)
+    prob = stacked(prob_ref[...], q_ref[0])
+    mask = jnp.where(prob > 0.0, 1.0, 0.0).astype(BF16)
+    pay_ref[:, :BLK] = dot(mask, tok_ref[:, :BLK], ((0,), (0,))).astype(BF16)
+    parts = jnp.concatenate(three(prob), axis=0)
+    cotangents = jnp.concatenate([tok_ref[:, BLK:]] * 3, axis=0)
+    pay_ref[:, BLK:] = dot(parts, cotangents, ((0,), (0,))).astype(BF16)
+
+
+def equal_to(want, width):
+    lane = lax.broadcasted_iota(jnp.int32, want.shape, 1)
+    return jnp.concatenate(
+        [jnp.where(want == lane + at, 1.0, 0.0).astype(BF16) for at in range(0, width, BLK)],
+        axis=1,
+    )
+
+
+def place():
+    i = lax.broadcasted_iota(jnp.int32, (ROWS, BLK), 0)
+    group = (i * 10923) >> 16
+    first = group * (QUADS * PART) + (i - group * PART)
+    return jnp.concatenate([equal_to(first + d * PART, WIDE) for d in range(QUADS)], axis=0)
+
+
+def partial_kernel(pay_ref, w0, w1, w2, w3, sums_hbm, x_hbm, dy_hbm, sums_ref, rows_ref, sems):
+    moved = dot(place(), pay_ref[...], ((1,), (0,))).astype(BF16)
     for d in range(QUADS):
-        rows = pl.ds(pl.multiple_of((q_ref[0] ^ d) * TOK, TOK), TOK)
-        x_tok = tok_ref[rows, :BLK]
-        dy_tok = tok_ref[rows, BLK:]
-        x = x + dot(masks[d], x_tok, ((0,), (0,)))
-        for part in parts:
-            dy = dy + dot(jnp.where(member == d, part, zero), dy_tok, ((0,), (0,)))
-    pay_ref[:, :BLK] = x.astype(BF16)
-    pay_ref[:, BLK:] = dy.astype(BF16)
-
-
-def place(d):
-    i = lax.broadcasted_iota(jnp.int32, (ROWS, WIDE), 0)
-    r = lax.broadcasted_iota(jnp.int32, (ROWS, WIDE), 1)
-    group = (i * 10923) >> 16
-    want = group * (QUADS * PART) + d * PART + (i - group * PART)
-    return jnp.where(r == want, 1.0, 0.0).astype(BF16)
-
-
-def partial_kernel(pay_ref, w0, w1, w2, w3, sums_hbm, x_hbm, dy_hbm, sums_ref, rows_ref, sems):
-    got = pay_ref[...]
-    for d in range(QUADS):
-        moved = dot(place(d), got, ((1,), (0,))).astype(BF16)
-        rows_ref[0, :, d * BLK : (d + 1) * BLK] = moved[:, :BLK]
-        rows_ref[1, :, d * BLK : (d + 1) * BLK] = moved[:, BLK:]
+        block = moved[d * ROWS : (d + 1) * ROWS]
+        rows_ref[0, :, d * BLK : (d + 1) * BLK] = block[:, :BLK]
+        rows_ref[1, :, d * BLK : (d + 1) * BLK] = block[:, BLK:]
     copies = [
         pltpu.make_async_copy(rows_ref.at[0], x_hbm, sems.at[3]),
         pltpu.make_async_copy(rows_ref.at[1], dy_hbm, sems.at[4]),
@@ -197,19 +198,18 @@
     act = h_ref[:, :FF]
     grad_g = h_ref[:, FF : 2 * FF]
     grad_u = h_ref[:, 2 * FF :]
-    pair, member, slot = row_fields((WIDE, ROWS), 0)
-    source = member * ROWS + pair * PART + slot
-    col = lax.broadcasted_iota(jnp.int32, (WIDE, ROWS), 1)
-    total = jnp.zeros((WIDE, 2 * BLK), F32)
-    for p, (wa, wb) in enumerate(((w0, w1), (w2, w3))):
+    outputs = []
+    for wa, wb in ((w0, w1), (w2, w3)):
         weights = [jnp.concatenate([wa[k], wb[k]], axis=0) for k in range(3)]
         y = dot(act, weights[2], ((1,), (1,))).astype(BF16)
         dx = dot(grad_g, weights[0], ((1,), (1,))) + dot(grad_u, weights[1], ((1,), (1,)))
         dx = dx.astype(BF16)
         for h in range(2):
-            both = jnp.concatenate([v[:, h * BLK : (h + 1) * BLK] for v in (y, dx)], axis=1)
-            onehot = jnp.where(source == col + (2 * p + h) * ROWS, 1.0, 0.0).astype(BF16)
-            total = total + dot(onehot, both, ((1,), (0,)))
+            at = slice(h * BLK, (h + 1) * BLK)
+            outputs.append(jnp.concatenate([y[:, at], dx[:, at]], axis=1))
+    pair, member, slot = row_fields((WIDE, BLK), 0)
+    source = member * ROWS + pair * PART + slot
+    total = dot(equal_to(source, WIDE), jnp.concatenate(outputs, axis=0), ((1,), (0,)))
     pay_ref[...] = total.astype(BF16)
 
 
@@ -240,20 +240,14 @@
 
 
 def combine_kernel(q_ref, pay_ref, prob_ref, out_ref):
-    q = q_ref[0]
-    shape = (TOK, WIDE)
-    _, member, _ = row_fields(shape, 1)
-    y = pay_ref[:, :BLK]
-    dx = pay_ref[:, BLK:]
-    prob = prob_ref[...]
-    mask = jnp.where(prob > 0.0, 1.0, 0.0)
-    for d in range(QUADS):
-        at = member == d
-        mixed = jnp.zeros((TOK, BLK), F32)
-        for part in three(jnp.where(at, prob, 0.0)):
-            mixed = mixed + dot(part, y, ((1,), (0,)))
-        grad = dot(jnp.where(at, mask, 0.0).astype(BF16), dx, ((1,), (0,)))
-        out_ref[q ^ d] = jnp.concatenate([mixed, grad], axis=1).astype(BF16)
+    prob = stacked(prob_ref[...], q_ref[0])
+    mask = jnp.where(prob > 0.0, 1.0, 0.0).astype(BF16)
+    parts = dot(jnp.concatenate(three(prob), axis=0), pay_ref[:, :BLK], ((1,), (0,)))
+    size = QUADS * TOK
+    mixed = (parts[:size] + parts[size : 2 * size]) + parts[2 * size :]
+    grad = dot(mask, pay_ref[:, BLK:], ((1,), (0,)))
+    out_ref[:, :BLK] = mixed.astype(BF16)
+    out_ref[:, BLK:] = grad.astype(BF16)
 
 
 def stack_kernel(a_ref, b_ref, c_ref, out_ref):
@@ -391,13 +385,13 @@
     with jax.named_scope("combine"):
         mixes = call(
             combine_kernel,
-            shape_of(QUADS, TOK, 2 * BLK),
+            far_shape(QUADS * TOK, 2 * BLK),
             (quad, returned, far(prob_again)),
             flops=2 * 16 * TOK * WIDE * BLK,
             moved=800000,
         )
         mixes = lax.all_to_all(mixes, QUAD, split_axis=0, concat_axis=0, tiled=True)
-        mixes = jnp.sum(mixes.astype(F32), axis=0).astype(BF16)
+        mixes = jnp.sum(mixes.reshape(QUADS, TOK, 2 * BLK).astype(F32), axis=0).astype(BF16)
         mixed, token_grad = mixes[:, :BLK], mixes[:, BLK:]
 
     return (

time: 173 us -> 175 us (1.012)
  transfers between devices with their start and end apart: 9 -> 9, of which waited for: 6 -> 6; matrix products, arithmetic and copies ran while one was open for 0% -> 0% of each run, Pallas kernels for 4% -> 5%
where the time goes in v8:
time: 175 us; the launch traced here: 174 us
  starting transfers between devices  71.6 us (41%)
  blocking collectives  54.6 us (31%)
  waiting for transfers between devices  22.7 us (13%)
  Pallas kernels  17.5 us (10%)
  local copies, waits for them, and re-layouts  5.74 us (3%)
    all_to_all x1, blocking collectives, shards(): parts = lax.all_to_all(sums, SUMS, split_axis=0, concat_axis=0, tiled=True)  24.9 us
    all_to_all x1, starting transfers between devices, shards(): lax.all_to_all(back, EXPERT, split_axis=0, concat_axis=0, tiled=True)  24.8 us
    all_to_all x1, blocking collectives, shards(): lax.all_to_all(hidden, SUMS, split_axis=0, concat_axis=0, tiled=True)  18 us
    all_to_all x1, starting transfers between devices, shards(): lax.all_to_all(call(blocks_kernel, far_shape(QUADS * TOK, 2 * BLK), (far(...  17.4 us
    pallas_call x11, Pallas kernels, call(): pl.pallas_call(kernel, out_shape=out_shape, in_specs=[smem if o.dtype ==...  15.1 us
    all_to_all x1, blocking collectives, shards(): mixes = lax.all_to_all(mixes, QUAD, split_axis=0, concat_axis=0, tiled=True)  11.7 us
    all_to_all x1, starting transfers between devices, shards(): got = lax.all_to_all(pay, EXPERT, split_axis=0, concat_axis=0, tiled=True)  8.81 us
    all_to_all x1, waiting for transfers between devices, shards(): lax.all_to_all(back, EXPERT, split_axis=0, concat_axis=0, tiled=True)  8.78 us
  transfers between devices with their start and end apart: 9, of which 6 were waited for; matrix products, arithmetic and copies ran while one was open for 0% of the time, Pallas kernels for 5%

profile of v8, /device:TPU:1, one launch (start us, length us, event | category | flops | bytes accessed | tf_op | source)
XLA Modules:
  0.0 173.7 jit_solution(1916067294989785233)
XLA Ops:
  0.6 0.0 copy-start.12
  0.6 0.0 copy-start.10
  0.7 0.0 copy-start.11
  0.7 1.5 tokens_to_quad.1
  2.1 17.4 %all-to-all-start = ((bf16[4,64,256]{2,1,0:T(8,128)(2,1)}), bf16[4,64,256]{2,1,0:T(8,128)(2,1)S(1)}, u32[]{:S(2)}, u32[]{:S(2)}) async-start(bf16[4,64,256]{2,1,0:T(8,128)(2,1)} %bitcast.42), calls=%async_computation | async-start | bytes 262144 | tf_op jit(solution)/shard_map/tokens_to_quad/all_to_all | solution.py:289
  19.6 1.9 %dispatch.2 = (f32[64,768]{1,0:T(8,128)S(1)}, f32[64,768]{1,0:T(8,128)}) custom-call(s32[1]{0:T(128)} %bitcast.q_ref, s32[8,64]{1,0:T(8,128)} %bitcast.50, f32[8,64]{1,0:T(8,128)} %bitcast.51), custom_call_target="tpu_custom_call" | custom-call | flops 6291456 | bytes 300000 | tf_op jit(solution)/shard_map/dispatch/pallas_call | solution.py:41
  21.4 1.7 all-to-all-done
  23.2 1.4 dispatch.3
  24.6 0.0 copy-start.5
  24.6 0.0 copy-start.6
  24.6 0.0 copy-start.7
  24.6 8.8 %all-to-all-start.1 = ((bf16[32,24,256]{2,1,0:T(8,128)(2,1)}), bf16[32,24,256]{2,1,0:T(8,128)(2,1)S(1)}, u32[]{:S(2)}, u32[]{:S(2)}) async-start(bf16[32,24,256]{2,1,0:T(8,128)(2,1)} %bitcast.5), calls=%async_computation.1 | async-start | bytes 786432 | tf_op jit(solution)/shard_map/dispatch/all_to_all | solution.py:329
  33.4 0.0 copy-done.12
  33.4 0.1 copy.23
  33.5 0.0 copy-done.10
  33.6 0.0 copy-done.11
  33.6 0.1 pad_maximum_fusion.w0
  33.6 2.4 %collective-permute-start.1 = (bf16[3,128,768]{2,1,0:T(8,128)(2,1)S(1)}, bf16[3,128,768]{2,1,0:T(8,128)(2,1)S(1)}, u32[]{:S(2)}, u32[]{:S(2)}) collective-permute-start(bf16[3,128,768]{2,1,0:T(8,128)(2,1)S(1)} %pad_maximum_fusion.w0), channel_id=1, source_target_pairs={{0,64},{64,0},{1,65},{65,1},{2,66},{66,2},{3,67},{67,3},{4,68},{68... | collective-permute-start | bytes 1769480 | tf_op jit(solution)/shard_map/weights_to_quad/ppermute | solution.py:309
  36.1 0.0 copy-done.5
  36.1 0.0 copy-done.6
  36.1 0.0 copy-done.7
  36.1 4.7 %collective-permute-start.2 = (f32[576,128]{1,0:T(8,128)S(1)}, f32[576,128]{1,0:T(8,128)S(1)}, u32[]{:S(2)}, u32[]{:S(2)}) collective-permute-start(f32[576,128]{1,0:T(8,128)S(1)} %relocate.2.state_ref), channel_id=1, source_target_pairs={{0,16},{16,0},{1,17},{17,1},{2,18},{18,2},{3,19},{19,3},{4,20},{20... | collective-permute-start | bytes 884744 | tf_op jit(solution)/shard_map/relocate/ppermute | solution.py:305
  40.8 3.6 %collective-permute-start = (bf16[3,128,768]{2,1,0:T(8,128)(2,1)S(1)}, bf16[3,128,768]{2,1,0:T(8,128)(2,1)S(1)}, u32[]{:S(2)}, u32[]{:S(2)}) collective-permute-start(bf16[3,128,768]{2,1,0:T(8,128)(2,1)S(1)} %pad_maximum_fusion.w0), channel_id=1, source_target_pairs={{0,32},{32,0},{1,33},{33,1},{2,34},{34,2},{3,35},{35,3},{4,36},{36... | collective-permute-start | bytes 1769480 | tf_op jit(solution)/shard_map/weights_to_quad/ppermute | solution.py:310
  44.4 4.7 %collective-permute-done.2.partner_ref = f32[576,128]{1,0:T(8,128)S(1)} collective-permute-done((f32[576,128]{1,0:T(8,128)S(1)}, f32[576,128]{1,0:T(8,128)S(1)}, u32[]{:S(2)}, u32[]{:S(2)}) %collective-permute-start.2) | collective-permute-done | bytes 294944 | tf_op jit(solution)/shard_map/relocate/ppermute | solution.py:305
  49.1 0.0 copy-start.3
  49.1 0.0 collective-permute-done.1.w2
  49.1 4.1 %collective-permute-start.3 = (bf16[3,128,768]{2,1,0:T(8,128)(2,1)S(1)}, bf16[3,128,768]{2,1,0:T(8,128)(2,1)S(1)}, u32[]{:S(2)}, u32[]{:S(2)}) collective-permute-start(bf16[3,128,768]{2,1,0:T(8,128)(2,1)S(1)} %collective-permute-done.1.w2), channel_id=1, source_target_pairs={{0,32},{32,0},{1,33},{33,1},{2,34},{34,2},{3,35},{35,3},{4,36},{36... | collective-permute-start | bytes 1769480 | tf_op jit(solution)/shard_map/weights_to_quad/ppermute | solution.py:312
  53.2 0.0 collective-permute-done.w1
  53.2 1.6 collective-permute-done.3.w3
  54.8 4.7 %all-to-all-done.1 = bf16[32,24,256]{2,1,0:T(8,128)(2,1)S(1)} async-done(((bf16[32,24,256]{2,1,0:T(8,128)(2,1)}), bf16[32,24,256]{2,1,0:T(8,128)(2,1)S(1)}, u32[]{:S(2)}, u32[]{:S(2)}) %all-to-all-start.1) | async-done | bytes 393248 | tf_op jit(solution)/shard_map/dispatch/all_to_all | solution.py:329
  59.4 2.4 %partial_sums.1 = (bf16[192,2304]{1,0:T(8,128)(2,1)}, bf16[192,512]{1,0:T(8,128)(2,1)}, bf16[192,512]{1,0:T(8,128)(2,1)}) custom-call(bf16[768,256]{1,0:T(8,128)(2,1)S(1)} %bitcast.32, bf16[3,128,768]{2,1,0:T(8,128)(2,1)S(1)} %pad_maximum_fusion.w0, bf16[3,128,768]{2,1,0:T(8,128)(2,1)S(1)} %collective-permute-done.w1, ...), custom_call_target="tpu_custom_call" | custom-call | flops 452984832 | bytes 4000000 | tf_op jit(solution)/shard_map/partial_sums/pallas_call | solution.py:160
  61.9 0.0 copy-done.3
  61.9 24.9 %all_to_all.64 = bf16[8,24,2304]{2,1,0:T(8,128)(2,1)S(1)} all-to-all(bf16[8,24,2304]{2,1,0:T(8,128)(2,1)} %bitcast.40), channel_id=1, replica_groups=mesh['x_lo'=2,'y1'=4,'y0'=2,'core'=2,'x_hi'=2,'z'=16] {'x_lo','y1'}, dimensions={0} | all-to-all | bytes 1769472 | tf_op jit(solution)/shard_map/partial_sums/all_to_all | solution.py:333
  86.7 1.1 activation.1
  87.8 18.0 %all_to_all.65 = bf16[8,24,2304]{2,1,0:T(8,128)(2,1)S(1)} all-to-all(bf16[8,24,2304]{2,1,0:T(8,128)(2,1)} %bitcast.38), channel_id=1, replica_groups=mesh['x_lo'=2,'y1'=4,'y0'=2,'core'=2,'x_hi'=2,'z'=16] {'x_lo','y1'}, dimensions={0} | all-to-all | bytes 1769472 | tf_op jit(solution)/shard_map/activation/all_to_all | solution.py:339
  105.8 2.4 %slot_outputs.1 = bf16[768,256]{1,0:T(8,128)(2,1)} custom-call(bf16[192,2304]{1,0:T(8,128)(2,1)S(1)} %bitcast.29, bf16[3,128,768]{2,1,0:T(8,128)(2,1)S(1)} %pad_maximum_fusion.w0, bf16[3,128,768]{2,1,0:T(8,128)(2,1)S(1)} %collective-permute-done.w1, bf16[3,128,768]{2,1,0:T(8,128)(2,1)S(1)} %collective-permute-done.1.w2, ...), custom_call_target="tpu_custom_call" | custom-call | flops 452984832 | bytes 4000000 | tf_op jit(solution)/shard_map/slot_outputs/pallas_call | solution.py:41
  108.2 24.8 %all-to-all-start.4 = ((bf16[32,24,256]{2,1,0:T(8,128)(2,1)}), bf16[32,24,256]{2,1,0:T(8,128)(2,1)S(1)}, u32[]{:S(2)}, u32[]{:S(2)}) async-start(bf16[32,24,256]{2,1,0:T(8,128)(2,1)} %bitcast.39), calls=%async_computation.4 | async-start | bytes 786432 | tf_op jit(solution)/shard_map/slot_outputs/all_to_all | solution.py:350
  133.0 0.0 copy-start.8
  133.0 0.9 copy-done.8
  133.9 0.0 copy-start.9
  133.9 0.9 copy-done.9
  134.8 0.0 copy-start.4
  134.8 1.8 %weight_grads.3 = (f32[2,3,128,768]{3,2,1,0:T(8,128)S(1)}, bf16[2,3,128,768]{3,2,1,0:T(8,128)(2,1)}) custom-call(bf16[192,2304]{1,0:T(8,128)(2,1)S(1)} %bitcast.30, bf16[192,512]{1,0:T(8,128)(2,1)S(1)} %copy-done.8, bf16[192,512]{1,0:T(8,128)(2,1)S(1)} %copy-done.9), custom_call_target="tpu_custom_call" | custom-call | flops 9059696640 | bytes 100000000 | tf_op jit(solution)/shard_map/weight_grads/pallas_call | solution.py:41
  136.7 0.0 copy-start
  136.7 1.4 copy-done
  138.1 3.7 %collective-permute-start.4 = (bf16[2,3,128,768]{3,2,1,0:T(8,128)(2,1)}, bf16[2,3,128,768]{3,2,1,0:T(8,128)(2,1)S(1)}, u32[]{:S(2)}, u32[]{:S(2)}) collective-permute-start(bf16[2,3,128,768]{3,2,1,0:T(8,128)(2,1)} %get-tuple-element.41), channel_id=1, source_target_pairs={{0,32},{32,0},{1,33},{33,1},{2,34},{34,2},{3,35},{35,3},{4,36},{36... | collective-permute-start | bytes 3538952 | tf_op jit(solution)/shard_map/weight_grads/ppermute | solution.py:369
  142.4 0.0 copy-done.4
  142.4 0.7 relocate.3
  143.2 1.3 collective-permute-done.4.near_ref
  144.4 0.0 copy-start.1
  144.4 1.7 copy-done.1
  146.1 1.2 weight_grads.4
  147.3 0.0 copy-start.2
  147.3 2.1 %collective-permute-start.5 = (bf16[3,128,768]{2,1,0:T(8,128)(2,1)S(1)}, bf16[3,128,768]{2,1,0:T(8,128)(2,1)S(1)}, u32[]{:S(2)}, u32[]{:S(2)}) collective-permute-start(bf16[3,128,768]{2,1,0:T(8,128)(2,1)S(1)} %get-tuple-element.49), channel_id=1, source_target_pairs={{0,64},{64,0},{1,65},{65,1},{2,66},{66,2},{3,67},{67,3},{4,68},{68... | collective-permute-start | bytes 1769480 | tf_op jit(solution)/shard_map/weight_grads/ppermute | solution.py:376
  149.4 8.8 %all-to-all-done.4 = bf16[32,24,256]{2,1,0:T(8,128)(2,1)S(1)} async-done(((bf16[32,24,256]{2,1,0:T(8,128)(2,1)}), bf16[32,24,256]{2,1,0:T(8,128)(2,1)S(1)}, u32[]{:S(2)}, u32[]{:S(2)}) %all-to-all-start.4) | async-done | bytes 393248 | tf_op jit(solution)/shard_map/slot_outputs/all_to_all | solution.py:350
  158.2 2.2 %combine.1 = bf16[256,256]{1,0:T(8,128)(2,1)} custom-call(s32[1]{0:T(128)} %bitcast.q_ref, bf16[768,256]{1,0:T(8,128)(2,1)S(1)} %bitcast.33, f32[64,768]{1,0:T(8,128)} %get-tuple-element.36.prob_ref), custom_call_target="tpu_custom_call" | custom-call | flops 201326592 | bytes 800000 | tf_op jit(solution)/shard_map/combine/pallas_call | solution.py:41
  160.4 11.7 %all_to_all.66 = bf16[4,64,256]{2,1,0:T(8,128)(2,1)S(1)} all-to-all(bf16[4,64,256]{2,1,0:T(8,128)(2,1)} %bitcast.43), channel_id=1, replica_groups=mesh['x_lo'=2,'y1'=4,'y0'=2,'core'=2,'x_hi'=2,'z'=16] {'y0','core'}, dimensions={0} | all-to-all | bytes 262144 | tf_op jit(solution)/shard_map/combine/all_to_all | solution.py:393
  172.1 0.6 fusion
  172.8 0.0 collective-permute-done.5.other_ref
  172.8 0.0 copy-done.2
  172.8 1.0 weight_grads.5
  (2 shorter events, 0.0 us)
Async XLA Ops:
  0.6 32.8 %copy-start.12 = (bf16[1,768,128]{2,1,0:T(8,128)(2,1)S(1)}, bf16[1,768,128]{2,1,0:T(8,128)(2,1)}, u32[]{:S(2)}) copy-start(bf16[1,768,128]{2,1,0:T(8,128)(2,1)} %param.17) | copy-start | bytes 589828
  0.6 32.9 %copy-start.10 = (bf16[1,128,768]{2,1,0:T(8,128)(2,1)S(1)}, bf16[1,128,768]{2,1,0:T(8,128)(2,1)}, u32[]{:S(2)}) copy-start(bf16[1,128,768]{2,1,0:T(8,128)(2,1)} %param.16) | copy-start | bytes 589828
  0.7 32.9 %copy-start.11 = (bf16[1,128,768]{2,1,0:T(8,128)(2,1)S(1)}, bf16[1,128,768]{2,1,0:T(8,128)(2,1)}, u32[]{:S(2)}) copy-start(bf16[1,128,768]{2,1,0:T(8,128)(2,1)} %param.15) | copy-start | bytes 589828
  2.1 21.0 %all-to-all-start = ((bf16[4,64,256]{2,1,0:T(8,128)(2,1)}), bf16[4,64,256]{2,1,0:T(8,128)(2,1)S(1)}, u32[]{:S(2)}, u32[]{:S(2)}) async-start(bf16[4,64,256]{2,1,0:T(8,128)(2,1)} %bitcast.42), calls=%async_computation | async-start | bytes 262144 | tf_op jit(solution)/shard_map/tokens_to_quad/all_to_all | solution.py:289
  24.6 11.5 %copy-start.5 = (f32[1,12,2048]{2,0,1:T(1,128)S(1)}, f32[1,12,2048]{2,0,1:T(1,128)}, u32[]{:S(2)}) copy-start(f32[1,12,2048]{2,0,1:T(1,128)} %param.19) | copy-start | bytes 294916
  24.6 11.5 %copy-start.6 = (f32[1,12,2048]{2,0,1:T(1,128)S(1)}, f32[1,12,2048]{2,0,1:T(1,128)}, u32[]{:S(2)}) copy-start(f32[1,12,2048]{2,0,1:T(1,128)} %param.20) | copy-start | bytes 294916
  24.6 11.5 %copy-start.7 = (f32[1,12,2048]{2,0,1:T(1,128)S(1)}, f32[1,12,2048]{2,0,1:T(1,128)}, u32[]{:S(2)}) copy-start(f32[1,12,2048]{2,0,1:T(1,128)} %param.21) | copy-start | bytes 294916
  24.6 34.9 %all-to-all-start.1 = ((bf16[32,24,256]{2,1,0:T(8,128)(2,1)}), bf16[32,24,256]{2,1,0:T(8,128)(2,1)S(1)}, u32[]{:S(2)}, u32[]{:S(2)}) async-start(bf16[32,24,256]{2,1,0:T(8,128)(2,1)} %bitcast.5), calls=%async_computation.1 | async-start | bytes 786432 | tf_op jit(solution)/shard_map/dispatch/all_to_all | solution.py:329
  33.6 15.5 %collective-permute-start.1 = (bf16[3,128,768]{2,1,0:T(8,128)(2,1)S(1)}, bf16[3,128,768]{2,1,0:T(8,128)(2,1)S(1)}, u32[]{:S(2)}, u32[]{:S(2)}) collective-permute-start(bf16[3,128,768]{2,1,0:T(8,128)(2,1)S(1)} %pad_maximum_fusion.w0), channel_id=1, source_target_pairs={{0,64},{64,0},{1,65},{65,1},{2,66},{66,2},{3,67},{67,3},{4,68},{68... | collective-permute-start | bytes 1769480 | tf_op jit(solution)/shard_map/weights_to_quad/ppermute | solution.py:309
  36.1 13.0 %collective-permute-start.2 = (f32[576,128]{1,0:T(8,128)S(1)}, f32[576,128]{1,0:T(8,128)S(1)}, u32[]{:S(2)}, u32[]{:S(2)}) collective-permute-start(f32[576,128]{1,0:T(8,128)S(1)} %relocate.2.state_ref), channel_id=1, source_target_pairs={{0,16},{16,0},{1,17},{17,1},{2,18},{18,2},{3,19},{19,3},{4,20},{20... | collective-permute-start | bytes 884744 | tf_op jit(solution)/shard_map/relocate/ppermute | solution.py:305
  40.8 12.4 %collective-permute-start = (bf16[3,128,768]{2,1,0:T(8,128)(2,1)S(1)}, bf16[3,128,768]{2,1,0:T(8,128)(2,1)S(1)}, u32[]{:S(2)}, u32[]{:S(2)}) collective-permute-start(bf16[3,128,768]{2,1,0:T(8,128)(2,1)S(1)} %pad_maximum_fusion.w0), channel_id=1, source_target_pairs={{0,32},{32,0},{1,33},{33,1},{2,34},{34,2},{3,35},{35,3},{4,36},{36... | collective-permute-start | bytes 1769480 | tf_op jit(solution)/shard_map/weights_to_quad/ppermute | solution.py:310
  49.1 12.8 %copy-start.3 = (f32[576,128]{1,0:T(8,128)}, f32[576,128]{1,0:T(8,128)S(1)}, u32[]{:S(2)}) copy-start(f32[576,128]{1,0:T(8,128)S(1)} %collective-permute-done.2.partner_ref) | copy-start | bytes 884740
  49.1 5.7 %collective-permute-start.3 = (bf16[3,128,768]{2,1,0:T(8,128)(2,1)S(1)}, bf16[3,128,768]{2,1,0:T(8,128)(2,1)S(1)}, u32[]{:S(2)}, u32[]{:S(2)}) collective-permute-start(bf16[3,128,768]{2,1,0:T(8,128)(2,1)S(1)} %collective-permute-done.1.w2), channel_id=1, source_target_pairs={{0,32},{32,0},{1,33},{33,1},{2,34},{34,2},{3,35},{35,3},{4,36},{36... | collective-permute-start | bytes 1769480 | tf_op jit(solution)/shard_map/weights_to_quad/ppermute | solution.py:312
  108.2 50.0 %all-to-all-start.4 = ((bf16[32,24,256]{2,1,0:T(8,128)(2,1)}), bf16[32,24,256]{2,1,0:T(8,128)(2,1)S(1)}, u32[]{:S(2)}, u32[]{:S(2)}) async-start(bf16[32,24,256]{2,1,0:T(8,128)(2,1)} %bitcast.39), calls=%async_computation.4 | async-start | bytes 786432 | tf_op jit(solution)/shard_map/slot_outputs/all_to_all | solution.py:350
  133.0 0.9 copy-start.8
  133.9 0.9 copy-start.9
  134.8 7.6 %copy-start.4 = (f32[576,128]{1,0:T(8,128)S(1)}, f32[576,128]{1,0:T(8,128)}, u32[]{:S(2)}) copy-start(f32[576,128]{1,0:T(8,128)} %copy-done.3) | copy-start | bytes 884740
  136.7 1.4 copy-start
  138.1 6.3 %collective-permute-start.4 = (bf16[2,3,128,768]{3,2,1,0:T(8,128)(2,1)}, bf16[2,3,128,768]{3,2,1,0:T(8,128)(2,1)S(1)}, u32[]{:S(2)}, u32[]{:S(2)}) collective-permute-start(bf16[2,3,128,768]{3,2,1,0:T(8,128)(2,1)} %get-tuple-element.41), channel_id=1, source_target_pairs={{0,32},{32,0},{1,33},{33,1},{2,34},{34,2},{3,35},{35,3},{4,36},{36... | collective-permute-start | bytes 3538952 | tf_op jit(solution)/shard_map/weight_grads/ppermute | solution.py:369
  144.4 1.7 copy-start.1
  147.3 25.5 %copy-start.2 = (f32[3,128,768]{2,1,0:T(8,128)S(1)}, f32[3,128,768]{2,1,0:T(8,128)}, u32[]{:S(2)}) copy-start(f32[3,128,768]{2,1,0:T(8,128)} %get-tuple-element.42.kept_ref) | copy-start | bytes 3538948
  147.3 25.5 %collective-permute-start.5 = (bf16[3,128,768]{2,1,0:T(8,128)(2,1)S(1)}, bf16[3,128,768]{2,1,0:T(8,128)(2,1)S(1)}, u32[]{:S(2)}, u32[]{:S(2)}) collective-permute-start(bf16[3,128,768]{2,1,0:T(8,128)(2,1)S(1)} %get-tuple-element.49), channel_id=1, source_target_pairs={{0,64},{64,0},{1,65},{65,1},{2,66},{66,2},{3,67},{67,3},{4,68},{68... | collective-permute-start | bytes 1769480 | tf_op jit(solution)/shard_map/weight_grads/ppermute | solution.py:376

commit v9 on v8

--- a/solution.py
+++ b/solution.py
@@ -121,19 +121,18 @@
     )
 
 
-def place():
+def place(d):
     i = lax.broadcasted_iota(jnp.int32, (ROWS, BLK), 0)
     group = (i * 10923) >> 16
-    first = group * (QUADS * PART) + (i - group * PART)
-    return jnp.concatenate([equal_to(first + d * PART, WIDE) for d in range(QUADS)], axis=0)
+    return equal_to(group * (QUADS * PART) + d * PART + (i - group * PART), WIDE)
 
 
 def partial_kernel(pay_ref, w0, w1, w2, w3, sums_hbm, x_hbm, dy_hbm, sums_ref, rows_ref, sems):
-    moved = dot(place(), pay_ref[...], ((1,), (0,))).astype(BF16)
+    got = pay_ref[...]
     for d in range(QUADS):
-        block = moved[d * ROWS : (d + 1) * ROWS]
-        rows_ref[0, :, d * BLK : (d + 1) * BLK] = block[:, :BLK]
-        rows_ref[1, :, d * BLK : (d + 1) * BLK] = block[:, BLK:]
+        moved = dot(place(d), got, ((1,), (0,))).astype(BF16)
+        rows_ref[0, :, d * BLK : (d + 1) * BLK] = moved[:, :BLK]
+        rows_ref[1, :, d * BLK : (d + 1) * BLK] = moved[:, BLK:]
     copies = [
         pltpu.make_async_copy(rows_ref.at[0], x_hbm, sems.at[3]),
         pltpu.make_async_copy(rows_ref.at[1], dy_hbm, sems.at[4]),
@@ -240,14 +239,20 @@
 
 
 def combine_kernel(q_ref, pay_ref, prob_ref, out_ref):
-    prob = stacked(prob_ref[...], q_ref[0])
-    mask = jnp.where(prob > 0.0, 1.0, 0.0).astype(BF16)
-    parts = dot(jnp.concatenate(three(prob), axis=0), pay_ref[:, :BLK], ((1,), (0,)))
-    size = QUADS * TOK
-    mixed = (parts[:size] + parts[size : 2 * size]) + parts[2 * size :]
-    grad = dot(mask, pay_ref[:, BLK:], ((1,), (0,)))
-    out_ref[:, :BLK] = mixed.astype(BF16)
-    out_ref[:, BLK:] = grad.astype(BF16)
+    q = q_ref[0]
+    shape = (TOK, WIDE)
+    _, member, _ = row_fields(shape, 1)
+    y = pay_ref[:, :BLK]
+    dx = pay_ref[:, BLK:]
+    prob = prob_ref[...]
+    mask = jnp.where(prob > 0.0, 1.0, 0.0)
+    for d in range(QUADS):
+        at = member == d
+        mixed = jnp.zeros((TOK, BLK), F32)
+        for part in three(jnp.where(at, prob, 0.0)):
+            mixed = mixed + dot(part, y, ((1,), (0,)))
+        grad = dot(jnp.where(at, mask, 0.0).astype(BF16), dx, ((1,), (0,)))
+        out_ref[q ^ d] = jnp.concatenate([mixed, grad], axis=1).astype(BF16)
 
 
 def stack_kernel(a_ref, b_ref, c_ref, out_ref):
@@ -385,13 +390,13 @@
     with jax.named_scope("combine"):
         mixes = call(
             combine_kernel,
-            far_shape(QUADS * TOK, 2 * BLK),
+            shape_of(QUADS, TOK, 2 * BLK),
             (quad, returned, far(prob_again)),
             flops=2 * 16 * TOK * WIDE * BLK,
             moved=800000,
         )
         mixes = lax.all_to_all(mixes, QUAD, split_axis=0, concat_axis=0, tiled=True)
-        mixes = jnp.sum(mixes.reshape(QUADS, TOK, 2 * BLK).astype(F32), axis=0).astype(BF16)
+        mixes = jnp.sum(mixes.astype(F32), axis=0).astype(BF16)
         mixed, token_grad = mixes[:, :BLK], mixes[:, BLK:]
 
     return (

time: 175 us -> 173 us (0.989)
  transfers between devices with their start and end apart: 9 -> 9, of which waited for: 6 -> 6; matrix products, arithmetic and copies ran while one was open for 0% -> 0% of each run, Pallas kernels for 5% -> 4%
where the time goes in v9:
time: 173 us; the launch traced here: 172 us
  starting transfers between devices  71.5 us (41%)
  blocking collectives  53.8 us (31%)
  waiting for transfers between devices  22.7 us (13%)
  Pallas kernels  16.5 us (10%)
  local copies, waits for them, and re-layouts  5.74 us (3%)
    all_to_all x1, blocking collectives, shards(): parts = lax.all_to_all(sums, SUMS, split_axis=0, concat_axis=0, tiled=True)  24.9 us
    all_to_all x1, starting transfers between devices, shards(): lax.all_to_all(back, EXPERT, split_axis=0, concat_axis=0, tiled=True)  24.7 us
    all_to_all x1, blocking collectives, shards(): lax.all_to_all(hidden, SUMS, split_axis=0, concat_axis=0, tiled=True)  18.1 us
    all_to_all x1, starting transfers between devices, shards(): lax.all_to_all(call(blocks_kernel, far_shape(QUADS * TOK, 2 * BLK), (far(...  17.4 us
    pallas_call x11, Pallas kernels, call(): pl.pallas_call(kernel, out_shape=out_shape, in_specs=[smem if o.dtype ==...  14.4 us
    all_to_all x1, blocking collectives, shards(): mixes = lax.all_to_all(mixes, QUAD, split_axis=0, concat_axis=0, tiled=True)  10.8 us
    all_to_all x1, starting transfers between devices, shards(): got = lax.all_to_all(pay, EXPERT, split_axis=0, concat_axis=0, tiled=True)  8.81 us
    all_to_all x1, waiting for transfers between devices, shards(): lax.all_to_all(back, EXPERT, split_axis=0, concat_axis=0, tiled=True)  8.75 us
  transfers between devices with their start and end apart: 9, of which 6 were waited for; matrix products, arithmetic and copies ran while one was open for 0% of the time, Pallas kernels for 4%

profile of v9, /device:TPU:1, one launch (start us, length us, event | category | flops | bytes accessed | tf_op | source)
XLA Modules:
  0.0 171.8 jit_solution(13480348217022672863)
XLA Ops:
  0.6 0.0 copy-start.12
  0.6 0.0 copy-start.10
  0.7 0.0 copy-start.11
  0.7 1.5 tokens_to_quad.1
  2.1 17.4 %all-to-all-start = ((bf16[4,64,256]{2,1,0:T(8,128)(2,1)}), bf16[4,64,256]{2,1,0:T(8,128)(2,1)S(1)}, u32[]{:S(2)}, u32[]{:S(2)}) async-start(bf16[4,64,256]{2,1,0:T(8,128)(2,1)} %bitcast.41), calls=%async_computation | async-start | bytes 262144 | tf_op jit(solution)/shard_map/tokens_to_quad/all_to_all | solution.py:294
  19.6 1.9 %dispatch.2 = (f32[64,768]{1,0:T(8,128)S(1)}, f32[64,768]{1,0:T(8,128)}) custom-call(s32[1]{0:T(128)} %bitcast.q_ref, s32[8,64]{1,0:T(8,128)} %bitcast.48, f32[8,64]{1,0:T(8,128)} %bitcast.49), custom_call_target="tpu_custom_call" | custom-call | flops 6291456 | bytes 300000 | tf_op jit(solution)/shard_map/dispatch/pallas_call | solution.py:41
  21.4 1.7 %all-to-all-done = bf16[4,64,256]{2,1,0:T(8,128)(2,1)S(1)} async-done(((bf16[4,64,256]{2,1,0:T(8,128)(2,1)}), bf16[4,64,256]{2,1,0:T(8,128)(2,1)S(1)}, u32[]{:S(2)}, u32[]{:S(2)}) %all-to-all-start) | async-done | bytes 131104 | tf_op jit(solution)/shard_map/tokens_to_quad/all_to_all | solution.py:294
  23.2 1.4 dispatch.3
  24.6 0.0 copy-start.5
  24.6 0.0 copy-start.6
  24.6 0.0 copy-start.7
  24.6 8.8 %all-to-all-start.1 = ((bf16[32,24,256]{2,1,0:T(8,128)(2,1)}), bf16[32,24,256]{2,1,0:T(8,128)(2,1)S(1)}, u32[]{:S(2)}, u32[]{:S(2)}) async-start(bf16[32,24,256]{2,1,0:T(8,128)(2,1)} %bitcast.5), calls=%async_computation.1 | async-start | bytes 786432 | tf_op jit(solution)/shard_map/dispatch/all_to_all | solution.py:334
  33.4 0.0 copy-done.12
  33.4 0.1 copy.23
  33.5 0.0 copy-done.10
  33.6 0.0 copy-done.11
  33.6 0.1 pad_maximum_fusion.w0
  33.6 2.4 %collective-permute-start.1 = (bf16[3,128,768]{2,1,0:T(8,128)(2,1)S(1)}, bf16[3,128,768]{2,1,0:T(8,128)(2,1)S(1)}, u32[]{:S(2)}, u32[]{:S(2)}) collective-permute-start(bf16[3,128,768]{2,1,0:T(8,128)(2,1)S(1)} %pad_maximum_fusion.w0), channel_id=1, source_target_pairs={{0,64},{64,0},{1,65},{65,1},{2,66},{66,2},{3,67},{67,3},{4,68},{68... | collective-permute-start | bytes 1769480 | tf_op jit(solution)/shard_map/weights_to_quad/ppermute | solution.py:314
  36.1 0.0 copy-done.5
  36.1 0.0 copy-done.6
  36.1 0.0 copy-done.7
  36.1 4.7 %collective-permute-start.2 = (f32[576,128]{1,0:T(8,128)S(1)}, f32[576,128]{1,0:T(8,128)S(1)}, u32[]{:S(2)}, u32[]{:S(2)}) collective-permute-start(f32[576,128]{1,0:T(8,128)S(1)} %relocate.2.state_ref), channel_id=1, source_target_pairs={{0,16},{16,0},{1,17},{17,1},{2,18},{18,2},{3,19},{19,3},{4,20},{20... | collective-permute-start | bytes 884744 | tf_op jit(solution)/shard_map/relocate/ppermute | solution.py:310
  40.8 3.6 %collective-permute-start = (bf16[3,128,768]{2,1,0:T(8,128)(2,1)S(1)}, bf16[3,128,768]{2,1,0:T(8,128)(2,1)S(1)}, u32[]{:S(2)}, u32[]{:S(2)}) collective-permute-start(bf16[3,128,768]{2,1,0:T(8,128)(2,1)S(1)} %pad_maximum_fusion.w0), channel_id=1, source_target_pairs={{0,32},{32,0},{1,33},{33,1},{2,34},{34,2},{3,35},{35,3},{4,36},{36... | collective-permute-start | bytes 1769480 | tf_op jit(solution)/shard_map/weights_to_quad/ppermute | solution.py:315
  44.4 4.7 %collective-permute-done.2.partner_ref = f32[576,128]{1,0:T(8,128)S(1)} collective-permute-done((f32[576,128]{1,0:T(8,128)S(1)}, f32[576,128]{1,0:T(8,128)S(1)}, u32[]{:S(2)}, u32[]{:S(2)}) %collective-permute-start.2) | collective-permute-done | bytes 294944 | tf_op jit(solution)/shard_map/relocate/ppermute | solution.py:310
  49.1 0.0 copy-start.3
  49.1 0.0 collective-permute-done.1.w2
  49.1 4.1 %collective-permute-start.3 = (bf16[3,128,768]{2,1,0:T(8,128)(2,1)S(1)}, bf16[3,128,768]{2,1,0:T(8,128)(2,1)S(1)}, u32[]{:S(2)}, u32[]{:S(2)}) collective-permute-start(bf16[3,128,768]{2,1,0:T(8,128)(2,1)S(1)} %collective-permute-done.1.w2), channel_id=1, source_target_pairs={{0,32},{32,0},{1,33},{33,1},{2,34},{34,2},{3,35},{35,3},{4,36},{36... | collective-permute-start | bytes 1769480 | tf_op jit(solution)/shard_map/weights_to_quad/ppermute | solution.py:317
  53.2 0.0 collective-permute-done.w1
  53.2 1.6 collective-permute-done.3.w3
  54.8 4.7 %all-to-all-done.1 = bf16[32,24,256]{2,1,0:T(8,128)(2,1)S(1)} async-done(((bf16[32,24,256]{2,1,0:T(8,128)(2,1)}), bf16[32,24,256]{2,1,0:T(8,128)(2,1)S(1)}, u32[]{:S(2)}, u32[]{:S(2)}) %all-to-all-start.1) | async-done | bytes 393248 | tf_op jit(solution)/shard_map/dispatch/all_to_all | solution.py:334
  59.4 2.0 %partial_sums.1 = (bf16[192,2304]{1,0:T(8,128)(2,1)}, bf16[192,512]{1,0:T(8,128)(2,1)}, bf16[192,512]{1,0:T(8,128)(2,1)}) custom-call(bf16[768,256]{1,0:T(8,128)(2,1)S(1)} %bitcast.31, bf16[3,128,768]{2,1,0:T(8,128)(2,1)S(1)} %pad_maximum_fusion.w0, bf16[3,128,768]{2,1,0:T(8,128)(2,1)S(1)} %collective-permute-done.w1, ...), custom_call_target="tpu_custom_call" | custom-call | flops 452984832 | bytes 4000000 | tf_op jit(solution)/shard_map/partial_sums/pallas_call | solution.py:159
  61.5 0.0 copy-done.3
  61.5 24.9 %all_to_all.60 = bf16[8,24,2304]{2,1,0:T(8,128)(2,1)S(1)} all-to-all(bf16[8,24,2304]{2,1,0:T(8,128)(2,1)} %bitcast.39), channel_id=1, replica_groups=mesh['x_lo'=2,'y1'=4,'y0'=2,'core'=2,'x_hi'=2,'z'=16] {'x_lo','y1'}, dimensions={0} | all-to-all | bytes 1769472 | tf_op jit(solution)/shard_map/partial_sums/all_to_all | solution.py:338
  86.4 1.1 activation.1
  87.5 18.1 %all_to_all.61 = bf16[8,24,2304]{2,1,0:T(8,128)(2,1)S(1)} all-to-all(bf16[8,24,2304]{2,1,0:T(8,128)(2,1)} %bitcast.37), channel_id=1, replica_groups=mesh['x_lo'=2,'y1'=4,'y0'=2,'core'=2,'x_hi'=2,'z'=16] {'x_lo','y1'}, dimensions={0} | all-to-all | bytes 1769472 | tf_op jit(solution)/shard_map/activation/all_to_all | solution.py:344
  105.6 2.4 %slot_outputs.1 = bf16[768,256]{1,0:T(8,128)(2,1)} custom-call(bf16[192,2304]{1,0:T(8,128)(2,1)S(1)} %bitcast.28, bf16[3,128,768]{2,1,0:T(8,128)(2,1)S(1)} %pad_maximum_fusion.w0, bf16[3,128,768]{2,1,0:T(8,128)(2,1)S(1)} %collective-permute-done.w1, bf16[3,128,768]{2,1,0:T(8,128)(2,1)S(1)} %collective-permute-done.1.w2, ...), custom_call_target="tpu_custom_call" | custom-call | flops 452984832 | bytes 4000000 | tf_op jit(solution)/shard_map/slot_outputs/pallas_call | solution.py:41
  107.9 24.7 %all-to-all-start.4 = ((bf16[32,24,256]{2,1,0:T(8,128)(2,1)}), bf16[32,24,256]{2,1,0:T(8,128)(2,1)S(1)}, u32[]{:S(2)}, u32[]{:S(2)}) async-start(bf16[32,24,256]{2,1,0:T(8,128)(2,1)} %bitcast.38), calls=%async_computation.4 | async-start | bytes 786432 | tf_op jit(solution)/shard_map/slot_outputs/all_to_all | solution.py:355
  132.6 0.0 copy-start.8
  132.6 0.9 copy-done.8
  133.5 0.0 copy-start.9
  133.6 0.9 copy-done.9
  134.5 0.0 copy-start.4
  134.5 1.8 %weight_grads.3 = (f32[2,3,128,768]{3,2,1,0:T(8,128)S(1)}, bf16[2,3,128,768]{3,2,1,0:T(8,128)(2,1)}) custom-call(bf16[192,2304]{1,0:T(8,128)(2,1)S(1)} %bitcast.29, bf16[192,512]{1,0:T(8,128)(2,1)S(1)} %copy-done.8, bf16[192,512]{1,0:T(8,128)(2,1)S(1)} %copy-done.9), custom_call_target="tpu_custom_call" | custom-call | flops 9059696640 | bytes 100000000 | tf_op jit(solution)/shard_map/weight_grads/pallas_call | solution.py:41
  136.3 0.0 copy-start
  136.3 1.4 copy-done
  137.7 3.7 %collective-permute-start.4 = (bf16[2,3,128,768]{3,2,1,0:T(8,128)(2,1)}, bf16[2,3,128,768]{3,2,1,0:T(8,128)(2,1)S(1)}, u32[]{:S(2)}, u32[]{:S(2)}) collective-permute-start(bf16[2,3,128,768]{3,2,1,0:T(8,128)(2,1)} %get-tuple-element.41), channel_id=1, source_target_pairs={{0,32},{32,0},{1,33},{33,1},{2,34},{34,2},{3,35},{35,3},{4,36},{36... | collective-permute-start | bytes 3538952 | tf_op jit(solution)/shard_map/weight_grads/ppermute | solution.py:374
  142.1 0.0 copy-done.4
  142.1 0.7 relocate.3
  142.8 1.3 collective-permute-done.4.near_ref
  144.1 0.0 copy-start.1
  144.1 1.7 copy-done.1
  145.7 1.2 weight_grads.4
  146.9 0.0 copy-start.2
  146.9 2.2 %collective-permute-start.5 = (bf16[3,128,768]{2,1,0:T(8,128)(2,1)S(1)}, bf16[3,128,768]{2,1,0:T(8,128)(2,1)S(1)}, u32[]{:S(2)}, u32[]{:S(2)}) collective-permute-start(bf16[3,128,768]{2,1,0:T(8,128)(2,1)S(1)} %get-tuple-element.49), channel_id=1, source_target_pairs={{0,64},{64,0},{1,65},{65,1},{2,66},{66,2},{3,67},{67,3},{4,68},{68... | collective-permute-start | bytes 1769480 | tf_op jit(solution)/shard_map/weight_grads/ppermute | solution.py:381
  149.1 8.7 %all-to-all-done.4 = bf16[32,24,256]{2,1,0:T(8,128)(2,1)S(1)} async-done(((bf16[32,24,256]{2,1,0:T(8,128)(2,1)}), bf16[32,24,256]{2,1,0:T(8,128)(2,1)S(1)}, u32[]{:S(2)}, u32[]{:S(2)}) %all-to-all-start.4) | async-done | bytes 393248 | tf_op jit(solution)/shard_map/slot_outputs/all_to_all | solution.py:355
  157.9 1.5 combine.1
  159.4 10.8 %all_to_all.62 = bf16[4,64,256]{2,1,0:T(8,128)(2,1)S(1)} all-to-all(bf16[4,64,256]{2,1,0:T(8,128)(2,1)S(1)} %combine.1), channel_id=1, replica_groups=mesh['x_lo'=2,'y1'=4,'y0'=2,'core'=2,'x_hi'=2,'z'=16] {'y0','core'}, dimensions={0} | all-to-all | bytes 262144 | tf_op jit(solution)/shard_map/combine/all_to_all | solution.py:398
  170.2 0.6 fusion
  170.8 0.0 collective-permute-done.5.other_ref
  170.8 0.0 copy-done.2
  170.8 1.0 weight_grads.5
  (2 shorter events, 0.0 us)
Async XLA Ops:
  0.6 32.8 %copy-start.12 = (bf16[1,768,128]{2,1,0:T(8,128)(2,1)S(1)}, bf16[1,768,128]{2,1,0:T(8,128)(2,1)}, u32[]{:S(2)}) copy-start(bf16[1,768,128]{2,1,0:T(8,128)(2,1)} %param.17) | copy-start | bytes 589828
  0.6 32.9 %copy-start.10 = (bf16[1,128,768]{2,1,0:T(8,128)(2,1)S(1)}, bf16[1,128,768]{2,1,0:T(8,128)(2,1)}, u32[]{:S(2)}) copy-start(bf16[1,128,768]{2,1,0:T(8,128)(2,1)} %param.16) | copy-start | bytes 589828
  0.7 32.9 %copy-start.11 = (bf16[1,128,768]{2,1,0:T(8,128)(2,1)S(1)}, bf16[1,128,768]{2,1,0:T(8,128)(2,1)}, u32[]{:S(2)}) copy-start(bf16[1,128,768]{2,1,0:T(8,128)(2,1)} %param.15) | copy-start | bytes 589828
  2.1 21.0 %all-to-all-start = ((bf16[4,64,256]{2,1,0:T(8,128)(2,1)}), bf16[4,64,256]{2,1,0:T(8,128)(2,1)S(1)}, u32[]{:S(2)}, u32[]{:S(2)}) async-start(bf16[4,64,256]{2,1,0:T(8,128)(2,1)} %bitcast.41), calls=%async_computation | async-start | bytes 262144 | tf_op jit(solution)/shard_map/tokens_to_quad/all_to_all | solution.py:294
  24.6 11.5 %copy-start.5 = (f32[1,12,2048]{2,0,1:T(1,128)S(1)}, f32[1,12,2048]{2,0,1:T(1,128)}, u32[]{:S(2)}) copy-start(f32[1,12,2048]{2,0,1:T(1,128)} %param.19) | copy-start | bytes 294916
  24.6 11.5 %copy-start.6 = (f32[1,12,2048]{2,0,1:T(1,128)S(1)}, f32[1,12,2048]{2,0,1:T(1,128)}, u32[]{:S(2)}) copy-start(f32[1,12,2048]{2,0,1:T(1,128)} %param.20) | copy-start | bytes 294916
  24.6 11.5 %copy-start.7 = (f32[1,12,2048]{2,0,1:T(1,128)S(1)}, f32[1,12,2048]{2,0,1:T(1,128)}, u32[]{:S(2)}) copy-start(f32[1,12,2048]{2,0,1:T(1,128)} %param.21) | copy-start | bytes 294916
  24.6 34.9 %all-to-all-start.1 = ((bf16[32,24,256]{2,1,0:T(8,128)(2,1)}), bf16[32,24,256]{2,1,0:T(8,128)(2,1)S(1)}, u32[]{:S(2)}, u32[]{:S(2)}) async-start(bf16[32,24,256]{2,1,0:T(8,128)(2,1)} %bitcast.5), calls=%async_computation.1 | async-start | bytes 786432 | tf_op jit(solution)/shard_map/dispatch/all_to_all | solution.py:334
  33.6 15.5 %collective-permute-start.1 = (bf16[3,128,768]{2,1,0:T(8,128)(2,1)S(1)}, bf16[3,128,768]{2,1,0:T(8,128)(2,1)S(1)}, u32[]{:S(2)}, u32[]{:S(2)}) collective-permute-start(bf16[3,128,768]{2,1,0:T(8,128)(2,1)S(1)} %pad_maximum_fusion.w0), channel_id=1, source_target_pairs={{0,64},{64,0},{1,65},{65,1},{2,66},{66,2},{3,67},{67,3},{4,68},{68... | collective-permute-start | bytes 1769480 | tf_op jit(solution)/shard_map/weights_to_quad/ppermute | solution.py:314
  36.1 13.0 %collective-permute-start.2 = (f32[576,128]{1,0:T(8,128)S(1)}, f32[576,128]{1,0:T(8,128)S(1)}, u32[]{:S(2)}, u32[]{:S(2)}) collective-permute-start(f32[576,128]{1,0:T(8,128)S(1)} %relocate.2.state_ref), channel_id=1, source_target_pairs={{0,16},{16,0},{1,17},{17,1},{2,18},{18,2},{3,19},{19,3},{4,20},{20... | collective-permute-start | bytes 884744 | tf_op jit(solution)/shard_map/relocate/ppermute | solution.py:310
  40.8 12.4 %collective-permute-start = (bf16[3,128,768]{2,1,0:T(8,128)(2,1)S(1)}, bf16[3,128,768]{2,1,0:T(8,128)(2,1)S(1)}, u32[]{:S(2)}, u32[]{:S(2)}) collective-permute-start(bf16[3,128,768]{2,1,0:T(8,128)(2,1)S(1)} %pad_maximum_fusion.w0), channel_id=1, source_target_pairs={{0,32},{32,0},{1,33},{33,1},{2,34},{34,2},{3,35},{35,3},{4,36},{36... | collective-permute-start | bytes 1769480 | tf_op jit(solution)/shard_map/weights_to_quad/ppermute | solution.py:315
  49.1 12.4 %copy-start.3 = (f32[576,128]{1,0:T(8,128)}, f32[576,128]{1,0:T(8,128)S(1)}, u32[]{:S(2)}) copy-start(f32[576,128]{1,0:T(8,128)S(1)} %collective-permute-done.2.partner_ref) | copy-start | bytes 884740
  49.1 5.7 %collective-permute-start.3 = (bf16[3,128,768]{2,1,0:T(8,128)(2,1)S(1)}, bf16[3,128,768]{2,1,0:T(8,128)(2,1)S(1)}, u32[]{:S(2)}, u32[]{:S(2)}) collective-permute-start(bf16[3,128,768]{2,1,0:T(8,128)(2,1)S(1)} %collective-permute-done.1.w2), channel_id=1, source_target_pairs={{0,32},{32,0},{1,33},{33,1},{2,34},{34,2},{3,35},{35,3},{4,36},{36... | collective-permute-start | bytes 1769480 | tf_op jit(solution)/shard_map/weights_to_quad/ppermute | solution.py:317
  107.9 49.9 %all-to-all-start.4 = ((bf16[32,24,256]{2,1,0:T(8,128)(2,1)}), bf16[32,24,256]{2,1,0:T(8,128)(2,1)S(1)}, u32[]{:S(2)}, u32[]{:S(2)}) async-start(bf16[32,24,256]{2,1,0:T(8,128)(2,1)} %bitcast.38), calls=%async_computation.4 | async-start | bytes 786432 | tf_op jit(solution)/shard_map/slot_outputs/all_to_all | solution.py:355
  132.6 0.9 copy-start.8
  133.5 0.9 copy-start.9
  134.5 7.6 %copy-start.4 = (f32[576,128]{1,0:T(8,128)S(1)}, f32[576,128]{1,0:T(8,128)}, u32[]{:S(2)}) copy-start(f32[576,128]{1,0:T(8,128)} %copy-done.3) | copy-start | bytes 884740
  136.3 1.4 copy-start
  137.7 6.3 %collective-permute-start.4 = (bf16[2,3,128,768]{3,2,1,0:T(8,128)(2,1)}, bf16[2,3,128,768]{3,2,1,0:T(8,128)(2,1)S(1)}, u32[]{:S(2)}, u32[]{:S(2)}) collective-permute-start(bf16[2,3,128,768]{3,2,1,0:T(8,128)(2,1)} %get-tuple-element.41), channel_id=1, source_target_pairs={{0,32},{32,0},{1,33},{33,1},{2,34},{34,2},{3,35},{35,3},{4,36},{36... | collective-permute-start | bytes 3538952 | tf_op jit(solution)/shard_map/weight_grads/ppermute | solution.py:374
  144.1 1.7 copy-start.1
  146.9 23.9 %copy-start.2 = (f32[3,128,768]{2,1,0:T(8,128)S(1)}, f32[3,128,768]{2,1,0:T(8,128)}, u32[]{:S(2)}) copy-start(f32[3,128,768]{2,1,0:T(8,128)} %get-tuple-element.42.kept_ref) | copy-start | bytes 3538948
  146.9 23.9 %collective-permute-start.5 = (bf16[3,128,768]{2,1,0:T(8,128)(2,1)S(1)}, bf16[3,128,768]{2,1,0:T(8,128)(2,1)S(1)}, u32[]{:S(2)}, u32[]{:S(2)}) collective-permute-start(bf16[3,128,768]{2,1,0:T(8,128)(2,1)S(1)} %get-tuple-element.49), channel_id=1, source_target_pairs={{0,64},{64,0},{1,65},{65,1},{2,66},{66,2},{3,67},{67,3},{4,68},{68... | collective-permute-start | bytes 1769480 | tf_op jit(solution)/shard_map/weight_grads/ppermute | solution.py:381

commit v10 on v9

--- a/solution.py
+++ b/solution.py
@@ -11,7 +11,7 @@
 EXPERT = ("x_hi", "z")
 DP = ("x_lo", "y1", "y0", "core")
 QUAD = ("y0", "core")
-SUMS = ("x_lo", "y1")
+SUMS = ("y1", "x_lo")
 F32 = jnp.float32
 BF16 = jnp.bfloat16
 SWAP = [(0, 1), (1, 0)]

time: 173 us -> 172 us (level)
  no operation moved by 1% of the time
where the time goes in v10:
time: 172 us; the launch traced here: 171 us
  starting transfers between devices  71.9 us (42%)
  blocking collectives  53.7 us (31%)
  waiting for transfers between devices  21.2 us (12%)
  Pallas kernels  16.4 us (10%)
  local copies, waits for them, and re-layouts  5.74 us (3%)
    all_to_all x1, starting transfers between devices, shards(): lax.all_to_all(back, EXPERT, split_axis=0, concat_axis=0, tiled=True)  24.3 us
    all_to_all x1, blocking collectives, shards(): parts = lax.all_to_all(sums, SUMS, split_axis=0, concat_axis=0, tiled=True)  23.5 us
    all_to_all x1, blocking collectives, shards(): lax.all_to_all(hidden, SUMS, split_axis=0, concat_axis=0, tiled=True)  19 us
    all_to_all x1, starting transfers between devices, shards(): lax.all_to_all(call(blocks_kernel, far_shape(QUADS * TOK, 2 * BLK), (far(...  17.4 us
    pallas_call x11, Pallas kernels, call(): pl.pallas_call(kernel, out_shape=out_shape, in_specs=[smem if o.dtype ==...  14.4 us
    all_to_all x1, blocking collectives, shards(): mixes = lax.all_to_all(mixes, QUAD, split_axis=0, concat_axis=0, tiled=True)  11.2 us
    all_to_all x1, starting transfers between devices, shards(): got = lax.all_to_all(pay, EXPERT, split_axis=0, concat_axis=0, tiled=True)  8.81 us
    all_to_all x1, waiting for transfers between devices, shards(): lax.all_to_all(back, EXPERT, split_axis=0, concat_axis=0, tiled=True)  7.32 us
  transfers between devices with their start and end apart: 9, of which 6 were waited for; matrix products, arithmetic and copies ran while one was open for 0% of the time, Pallas kernels for 4%

profile of v10, /device:TPU:1, one launch (start us, length us, event | category | flops | bytes accessed | tf_op | source)
XLA Modules:
  0.0 170.6 jit_solution(8503258367432198021)
XLA Ops:
  0.6 0.0 copy-start.12
  0.6 0.0 copy-start.10
  0.7 0.0 copy-start.11
  0.7 1.5 tokens_to_quad.1
  2.1 17.4 %all-to-all-start = ((bf16[4,64,256]{2,1,0:T(8,128)(2,1)}), bf16[4,64,256]{2,1,0:T(8,128)(2,1)S(1)}, u32[]{:S(2)}, u32[]{:S(2)}) async-start(bf16[4,64,256]{2,1,0:T(8,128)(2,1)} %bitcast.41), calls=%async_computation | async-start | bytes 262144 | tf_op jit(solution)/shard_map/tokens_to_quad/all_to_all | solution.py:294
  19.6 1.9 %dispatch.2 = (f32[64,768]{1,0:T(8,128)S(1)}, f32[64,768]{1,0:T(8,128)}) custom-call(s32[1]{0:T(128)} %bitcast.q_ref, s32[8,64]{1,0:T(8,128)} %bitcast.48, f32[8,64]{1,0:T(8,128)} %bitcast.49), custom_call_target="tpu_custom_call" | custom-call | flops 6291456 | bytes 300000 | tf_op jit(solution)/shard_map/dispatch/pallas_call | solution.py:41
  21.4 1.7 %all-to-all-done = bf16[4,64,256]{2,1,0:T(8,128)(2,1)S(1)} async-done(((bf16[4,64,256]{2,1,0:T(8,128)(2,1)}), bf16[4,64,256]{2,1,0:T(8,128)(2,1)S(1)}, u32[]{:S(2)}, u32[]{:S(2)}) %all-to-all-start) | async-done | bytes 131104 | tf_op jit(solution)/shard_map/tokens_to_quad/all_to_all | solution.py:294
  23.2 1.4 dispatch.3
  24.6 0.0 copy-start.5
  24.6 0.0 copy-start.6
  24.6 0.0 copy-start.7
  24.6 8.8 %all-to-all-start.1 = ((bf16[32,24,256]{2,1,0:T(8,128)(2,1)}), bf16[32,24,256]{2,1,0:T(8,128)(2,1)S(1)}, u32[]{:S(2)}, u32[]{:S(2)}) async-start(bf16[32,24,256]{2,1,0:T(8,128)(2,1)} %bitcast.5), calls=%async_computation.1 | async-start | bytes 786432 | tf_op jit(solution)/shard_map/dispatch/all_to_all | solution.py:334
  33.4 0.0 copy-done.12
  33.4 0.1 copy.23
  33.5 0.0 copy-done.10
  33.6 0.0 copy-done.11
  33.6 0.1 pad_maximum_fusion.w0
  33.6 2.4 %collective-permute-start.1 = (bf16[3,128,768]{2,1,0:T(8,128)(2,1)S(1)}, bf16[3,128,768]{2,1,0:T(8,128)(2,1)S(1)}, u32[]{:S(2)}, u32[]{:S(2)}) collective-permute-start(bf16[3,128,768]{2,1,0:T(8,128)(2,1)S(1)} %pad_maximum_fusion.w0), channel_id=1, source_target_pairs={{0,64},{64,0},{1,65},{65,1},{2,66},{66,2},{3,67},{67,3},{4,68},{68... | collective-permute-start | bytes 1769480 | tf_op jit(solution)/shard_map/weights_to_quad/ppermute | solution.py:314
  36.1 0.0 copy-done.5
  36.1 0.0 copy-done.6
  36.1 0.0 copy-done.7
  36.1 4.7 %collective-permute-start.2 = (f32[576,128]{1,0:T(8,128)S(1)}, f32[576,128]{1,0:T(8,128)S(1)}, u32[]{:S(2)}, u32[]{:S(2)}) collective-permute-start(f32[576,128]{1,0:T(8,128)S(1)} %relocate.2.state_ref), channel_id=1, source_target_pairs={{0,16},{16,0},{1,17},{17,1},{2,18},{18,2},{3,19},{19,3},{4,20},{20... | collective-permute-start | bytes 884744 | tf_op jit(solution)/shard_map/relocate/ppermute | solution.py:310
  40.8 3.6 %collective-permute-start = (bf16[3,128,768]{2,1,0:T(8,128)(2,1)S(1)}, bf16[3,128,768]{2,1,0:T(8,128)(2,1)S(1)}, u32[]{:S(2)}, u32[]{:S(2)}) collective-permute-start(bf16[3,128,768]{2,1,0:T(8,128)(2,1)S(1)} %pad_maximum_fusion.w0), channel_id=1, source_target_pairs={{0,32},{32,0},{1,33},{33,1},{2,34},{34,2},{3,35},{35,3},{4,36},{36... | collective-permute-start | bytes 1769480 | tf_op jit(solution)/shard_map/weights_to_quad/ppermute | solution.py:315
  44.4 4.7 %collective-permute-done.2.partner_ref = f32[576,128]{1,0:T(8,128)S(1)} collective-permute-done((f32[576,128]{1,0:T(8,128)S(1)}, f32[576,128]{1,0:T(8,128)S(1)}, u32[]{:S(2)}, u32[]{:S(2)}) %collective-permute-start.2) | collective-permute-done | bytes 294944 | tf_op jit(solution)/shard_map/relocate/ppermute | solution.py:310
  49.1 0.0 copy-start.3
  49.1 0.0 collective-permute-done.1.w2
  49.1 4.1 %collective-permute-start.3 = (bf16[3,128,768]{2,1,0:T(8,128)(2,1)S(1)}, bf16[3,128,768]{2,1,0:T(8,128)(2,1)S(1)}, u32[]{:S(2)}, u32[]{:S(2)}) collective-permute-start(bf16[3,128,768]{2,1,0:T(8,128)(2,1)S(1)} %collective-permute-done.1.w2), channel_id=1, source_target_pairs={{0,32},{32,0},{1,33},{33,1},{2,34},{34,2},{3,35},{35,3},{4,36},{36... | collective-permute-start | bytes 1769480 | tf_op jit(solution)/shard_map/weights_to_quad/ppermute | solution.py:317
  53.2 0.0 collective-permute-done.w1
  53.2 1.6 collective-permute-done.3.w3
  54.8 4.7 %all-to-all-done.1 = bf16[32,24,256]{2,1,0:T(8,128)(2,1)S(1)} async-done(((bf16[32,24,256]{2,1,0:T(8,128)(2,1)}), bf16[32,24,256]{2,1,0:T(8,128)(2,1)S(1)}, u32[]{:S(2)}, u32[]{:S(2)}) %all-to-all-start.1) | async-done | bytes 393248 | tf_op jit(solution)/shard_map/dispatch/all_to_all | solution.py:334
  59.4 2.0 %partial_sums.1 = (bf16[192,2304]{1,0:T(8,128)(2,1)}, bf16[192,512]{1,0:T(8,128)(2,1)}, bf16[192,512]{1,0:T(8,128)(2,1)}) custom-call(bf16[768,256]{1,0:T(8,128)(2,1)S(1)} %bitcast.31, bf16[3,128,768]{2,1,0:T(8,128)(2,1)S(1)} %pad_maximum_fusion.w0, bf16[3,128,768]{2,1,0:T(8,128)(2,1)S(1)} %collective-permute-done.w1, ...), custom_call_target="tpu_custom_call" | custom-call | flops 452984832 | bytes 4000000 | tf_op jit(solution)/shard_map/partial_sums/pallas_call | solution.py:159
  61.5 0.0 copy-done.3
  61.5 23.5 %all_to_all.60 = bf16[8,24,2304]{2,1,0:T(8,128)(2,1)S(1)} all-to-all(bf16[8,24,2304]{2,1,0:T(8,128)(2,1)} %bitcast.39), channel_id=1, replica_groups=mesh['x_lo'=2,'y1'=4,'y0'=2,'core'=2,'x_hi'=2,'z'=16] {'y1','x_lo'}, dimensions={0} | all-to-all | bytes 1769472 | tf_op jit(solution)/shard_map/partial_sums/all_to_all | solution.py:338
  85.0 1.1 activation.1
  86.1 19.0 %all_to_all.61 = bf16[8,24,2304]{2,1,0:T(8,128)(2,1)S(1)} all-to-all(bf16[8,24,2304]{2,1,0:T(8,128)(2,1)} %bitcast.37), channel_id=1, replica_groups=mesh['x_lo'=2,'y1'=4,'y0'=2,'core'=2,'x_hi'=2,'z'=16] {'y1','x_lo'}, dimensions={0} | all-to-all | bytes 1769472 | tf_op jit(solution)/shard_map/activation/all_to_all | solution.py:344
  105.1 2.3 %slot_outputs.1 = bf16[768,256]{1,0:T(8,128)(2,1)} custom-call(bf16[192,2304]{1,0:T(8,128)(2,1)S(1)} %bitcast.28, bf16[3,128,768]{2,1,0:T(8,128)(2,1)S(1)} %pad_maximum_fusion.w0, bf16[3,128,768]{2,1,0:T(8,128)(2,1)S(1)} %collective-permute-done.w1, bf16[3,128,768]{2,1,0:T(8,128)(2,1)S(1)} %collective-permute-done.1.w2, ...), custom_call_target="tpu_custom_call" | custom-call | flops 452984832 | bytes 4000000 | tf_op jit(solution)/shard_map/slot_outputs/pallas_call | solution.py:41
  107.4 24.3 %all-to-all-start.4 = ((bf16[32,24,256]{2,1,0:T(8,128)(2,1)}), bf16[32,24,256]{2,1,0:T(8,128)(2,1)S(1)}, u32[]{:S(2)}, u32[]{:S(2)}) async-start(bf16[32,24,256]{2,1,0:T(8,128)(2,1)} %bitcast.38), calls=%async_computation.4 | async-start | bytes 786432 | tf_op jit(solution)/shard_map/slot_outputs/all_to_all | solution.py:355
  131.7 0.0 copy-start.8
  131.7 0.9 copy-done.8
  132.6 0.0 copy-start.9
  132.6 0.9 copy-done.9
  133.6 0.0 copy-start.4
  133.6 1.8 %weight_grads.3 = (f32[2,3,128,768]{3,2,1,0:T(8,128)S(1)}, bf16[2,3,128,768]{3,2,1,0:T(8,128)(2,1)}) custom-call(bf16[192,2304]{1,0:T(8,128)(2,1)S(1)} %bitcast.29, bf16[192,512]{1,0:T(8,128)(2,1)S(1)} %copy-done.8, bf16[192,512]{1,0:T(8,128)(2,1)S(1)} %copy-done.9), custom_call_target="tpu_custom_call" | custom-call | flops 9059696640 | bytes 100000000 | tf_op jit(solution)/shard_map/weight_grads/pallas_call | solution.py:41
  135.4 0.0 copy-start
  135.4 1.4 copy-done
  136.8 4.4 %collective-permute-start.4 = (bf16[2,3,128,768]{3,2,1,0:T(8,128)(2,1)}, bf16[2,3,128,768]{3,2,1,0:T(8,128)(2,1)S(1)}, u32[]{:S(2)}, u32[]{:S(2)}) collective-permute-start(bf16[2,3,128,768]{3,2,1,0:T(8,128)(2,1)} %get-tuple-element.41), channel_id=1, source_target_pairs={{0,32},{32,0},{1,33},{33,1},{2,34},{34,2},{3,35},{35,3},{4,36},{36... | collective-permute-start | bytes 3538952 | tf_op jit(solution)/shard_map/weight_grads/ppermute | solution.py:374
  141.9 0.0 copy-done.4
  141.9 0.7 relocate.3
  142.7 1.3 collective-permute-done.4.near_ref
  143.9 0.0 copy-start.1
  143.9 1.7 copy-done.1
  145.6 1.2 weight_grads.4
  146.8 0.0 copy-start.2
  146.8 2.1 %collective-permute-start.5 = (bf16[3,128,768]{2,1,0:T(8,128)(2,1)S(1)}, bf16[3,128,768]{2,1,0:T(8,128)(2,1)S(1)}, u32[]{:S(2)}, u32[]{:S(2)}) collective-permute-start(bf16[3,128,768]{2,1,0:T(8,128)(2,1)S(1)} %get-tuple-element.49), channel_id=1, source_target_pairs={{0,64},{64,0},{1,65},{65,1},{2,66},{66,2},{3,67},{67,3},{4,68},{68... | collective-permute-start | bytes 1769480 | tf_op jit(solution)/shard_map/weight_grads/ppermute | solution.py:381
  148.9 7.3 %all-to-all-done.4 = bf16[32,24,256]{2,1,0:T(8,128)(2,1)S(1)} async-done(((bf16[32,24,256]{2,1,0:T(8,128)(2,1)}), bf16[32,24,256]{2,1,0:T(8,128)(2,1)S(1)}, u32[]{:S(2)}, u32[]{:S(2)}) %all-to-all-start.4) | async-done | bytes 393248 | tf_op jit(solution)/shard_map/slot_outputs/all_to_all | solution.py:355
  156.3 1.5 combine.1
  157.8 11.2 %all_to_all.62 = bf16[4,64,256]{2,1,0:T(8,128)(2,1)S(1)} all-to-all(bf16[4,64,256]{2,1,0:T(8,128)(2,1)S(1)} %combine.1), channel_id=1, replica_groups=mesh['x_lo'=2,'y1'=4,'y0'=2,'core'=2,'x_hi'=2,'z'=16] {'y0','core'}, dimensions={0} | all-to-all | bytes 262144 | tf_op jit(solution)/shard_map/combine/all_to_all | solution.py:398
  169.0 0.6 fusion
  169.6 0.0 collective-permute-done.5.other_ref
  169.7 0.0 copy-done.2
  169.7 1.0 weight_grads.5
  (2 shorter events, 0.0 us)
Async XLA Ops:
  0.6 32.8 %copy-start.12 = (bf16[1,768,128]{2,1,0:T(8,128)(2,1)S(1)}, bf16[1,768,128]{2,1,0:T(8,128)(2,1)}, u32[]{:S(2)}) copy-start(bf16[1,768,128]{2,1,0:T(8,128)(2,1)} %param.17) | copy-start | bytes 589828
  0.6 32.9 %copy-start.10 = (bf16[1,128,768]{2,1,0:T(8,128)(2,1)S(1)}, bf16[1,128,768]{2,1,0:T(8,128)(2,1)}, u32[]{:S(2)}) copy-start(bf16[1,128,768]{2,1,0:T(8,128)(2,1)} %param.16) | copy-start | bytes 589828
  0.7 32.9 %copy-start.11 = (bf16[1,128,768]{2,1,0:T(8,128)(2,1)S(1)}, bf16[1,128,768]{2,1,0:T(8,128)(2,1)}, u32[]{:S(2)}) copy-start(bf16[1,128,768]{2,1,0:T(8,128)(2,1)} %param.15) | copy-start | bytes 589828
  2.1 21.0 %all-to-all-start = ((bf16[4,64,256]{2,1,0:T(8,128)(2,1)}), bf16[4,64,256]{2,1,0:T(8,128)(2,1)S(1)}, u32[]{:S(2)}, u32[]{:S(2)}) async-start(bf16[4,64,256]{2,1,0:T(8,128)(2,1)} %bitcast.41), calls=%async_computation | async-start | bytes 262144 | tf_op jit(solution)/shard_map/tokens_to_quad/all_to_all | solution.py:294
  24.6 11.5 %copy-start.5 = (f32[1,12,2048]{2,0,1:T(1,128)S(1)}, f32[1,12,2048]{2,0,1:T(1,128)}, u32[]{:S(2)}) copy-start(f32[1,12,2048]{2,0,1:T(1,128)} %param.19) | copy-start | bytes 294916
  24.6 11.5 %copy-start.6 = (f32[1,12,2048]{2,0,1:T(1,128)S(1)}, f32[1,12,2048]{2,0,1:T(1,128)}, u32[]{:S(2)}) copy-start(f32[1,12,2048]{2,0,1:T(1,128)} %param.20) | copy-start | bytes 294916
  24.6 11.5 %copy-start.7 = (f32[1,12,2048]{2,0,1:T(1,128)S(1)}, f32[1,12,2048]{2,0,1:T(1,128)}, u32[]{:S(2)}) copy-start(f32[1,12,2048]{2,0,1:T(1,128)} %param.21) | copy-start | bytes 294916
  24.6 34.9 %all-to-all-start.1 = ((bf16[32,24,256]{2,1,0:T(8,128)(2,1)}), bf16[32,24,256]{2,1,0:T(8,128)(2,1)S(1)}, u32[]{:S(2)}, u32[]{:S(2)}) async-start(bf16[32,24,256]{2,1,0:T(8,128)(2,1)} %bitcast.5), calls=%async_computation.1 | async-start | bytes 786432 | tf_op jit(solution)/shard_map/dispatch/all_to_all | solution.py:334
  33.6 15.5 %collective-permute-start.1 = (bf16[3,128,768]{2,1,0:T(8,128)(2,1)S(1)}, bf16[3,128,768]{2,1,0:T(8,128)(2,1)S(1)}, u32[]{:S(2)}, u32[]{:S(2)}) collective-permute-start(bf16[3,128,768]{2,1,0:T(8,128)(2,1)S(1)} %pad_maximum_fusion.w0), channel_id=1, source_target_pairs={{0,64},{64,0},{1,65},{65,1},{2,66},{66,2},{3,67},{67,3},{4,68},{68... | collective-permute-start | bytes 1769480 | tf_op jit(solution)/shard_map/weights_to_quad/ppermute | solution.py:314
  36.1 13.0 %collective-permute-start.2 = (f32[576,128]{1,0:T(8,128)S(1)}, f32[576,128]{1,0:T(8,128)S(1)}, u32[]{:S(2)}, u32[]{:S(2)}) collective-permute-start(f32[576,128]{1,0:T(8,128)S(1)} %relocate.2.state_ref), channel_id=1, source_target_pairs={{0,16},{16,0},{1,17},{17,1},{2,18},{18,2},{3,19},{19,3},{4,20},{20... | collective-permute-start | bytes 884744 | tf_op jit(solution)/shard_map/relocate/ppermute | solution.py:310
  40.8 12.4 %collective-permute-start = (bf16[3,128,768]{2,1,0:T(8,128)(2,1)S(1)}, bf16[3,128,768]{2,1,0:T(8,128)(2,1)S(1)}, u32[]{:S(2)}, u32[]{:S(2)}) collective-permute-start(bf16[3,128,768]{2,1,0:T(8,128)(2,1)S(1)} %pad_maximum_fusion.w0), channel_id=1, source_target_pairs={{0,32},{32,0},{1,33},{33,1},{2,34},{34,2},{3,35},{35,3},{4,36},{36... | collective-permute-start | bytes 1769480 | tf_op jit(solution)/shard_map/weights_to_quad/ppermute | solution.py:315
  49.1 12.4 %copy-start.3 = (f32[576,128]{1,0:T(8,128)}, f32[576,128]{1,0:T(8,128)S(1)}, u32[]{:S(2)}) copy-start(f32[576,128]{1,0:T(8,128)S(1)} %collective-permute-done.2.partner_ref) | copy-start | bytes 884740
  49.1 5.7 %collective-permute-start.3 = (bf16[3,128,768]{2,1,0:T(8,128)(2,1)S(1)}, bf16[3,128,768]{2,1,0:T(8,128)(2,1)S(1)}, u32[]{:S(2)}, u32[]{:S(2)}) collective-permute-start(bf16[3,128,768]{2,1,0:T(8,128)(2,1)S(1)} %collective-permute-done.1.w2), channel_id=1, source_target_pairs={{0,32},{32,0},{1,33},{33,1},{2,34},{34,2},{3,35},{35,3},{4,36},{36... | collective-permute-start | bytes 1769480 | tf_op jit(solution)/shard_map/weights_to_quad/ppermute | solution.py:317
  107.4 48.8 %all-to-all-start.4 = ((bf16[32,24,256]{2,1,0:T(8,128)(2,1)}), bf16[32,24,256]{2,1,0:T(8,128)(2,1)S(1)}, u32[]{:S(2)}, u32[]{:S(2)}) async-start(bf16[32,24,256]{2,1,0:T(8,128)(2,1)} %bitcast.38), calls=%async_computation.4 | async-start | bytes 786432 | tf_op jit(solution)/shard_map/slot_outputs/all_to_all | solution.py:355
  131.7 0.9 copy-start.8
  132.6 0.9 copy-start.9
  133.6 8.4 %copy-start.4 = (f32[576,128]{1,0:T(8,128)S(1)}, f32[576,128]{1,0:T(8,128)}, u32[]{:S(2)}) copy-start(f32[576,128]{1,0:T(8,128)} %copy-done.3) | copy-start | bytes 884740
  135.4 1.4 copy-start
  136.8 7.1 %collective-permute-start.4 = (bf16[2,3,128,768]{3,2,1,0:T(8,128)(2,1)}, bf16[2,3,128,768]{3,2,1,0:T(8,128)(2,1)S(1)}, u32[]{:S(2)}, u32[]{:S(2)}) collective-permute-start(bf16[2,3,128,768]{3,2,1,0:T(8,128)(2,1)} %get-tuple-element.41), channel_id=1, source_target_pairs={{0,32},{32,0},{1,33},{33,1},{2,34},{34,2},{3,35},{35,3},{4,36},{36... | collective-permute-start | bytes 3538952 | tf_op jit(solution)/shard_map/weight_grads/ppermute | solution.py:374
  143.9 1.7 copy-start.1
  146.8 22.9 %copy-start.2 = (f32[3,128,768]{2,1,0:T(8,128)S(1)}, f32[3,128,768]{2,1,0:T(8,128)}, u32[]{:S(2)}) copy-start(f32[3,128,768]{2,1,0:T(8,128)} %get-tuple-element.42.kept_ref) | copy-start | bytes 3538948
  146.8 22.8 %collective-permute-start.5 = (bf16[3,128,768]{2,1,0:T(8,128)(2,1)S(1)}, bf16[3,128,768]{2,1,0:T(8,128)(2,1)S(1)}, u32[]{:S(2)}, u32[]{:S(2)}) collective-permute-start(bf16[3,128,768]{2,1,0:T(8,128)(2,1)S(1)} %get-tuple-element.49), channel_id=1, source_target_pairs={{0,64},{64,0},{1,65},{65,1},{2,66},{66,2},{3,67},{67,3},{4,68},{68... | collective-permute-start | bytes 1769480 | tf_op jit(solution)/shard_map/weight_grads/ppermute | solution.py:381
